TPU v7x, 32 devices: a whole 2x2x4 slice. The times are simulated.
32 devices in a mesh: tensor: 2 (over x), context: 4 (over y, core), fsdp: 4 (over z).
Axes of the slice: x: 2, y: 2, z: 4, core: 2. Of those that a mesh axis runs over, the one named last changes fastest.
Arguments:
- tokens: bfloat16 [4, 1024, 2048], P('fsdp', 'context'), may hold values from -6 to 6
- segments: int32 [4, 1024], P('fsdp'), may hold values from 0 to 7, as said below
- positions: int32 [4, 1024], P('fsdp', 'context'), may hold values from 0 to 511, as said below
- attn_gain: bfloat16 [2048], P('fsdp'), may hold values from 0.099609375 to 1.8984375
- w_query: bfloat16 [2048, 2048], P('fsdp', 'tensor'), may hold values from -0.125 to 0.125
- w_key: bfloat16 [2048, 1024], P('fsdp', 'tensor'), may hold values from -0.125 to 0.125
- w_value: bfloat16 [2048, 1024], P('fsdp', 'tensor'), may hold values from -0.125 to 0.125
- w_out: bfloat16 [2048, 2048], P(('tensor', 'fsdp')), may hold values from -0.5 to 0.5
- ffn_gain: bfloat16 [2048], P('fsdp'), may hold values from 0.099609375 to 1.8984375
- w_gate: bfloat16 [2048, 8192], P('fsdp', 'tensor'), may hold values from -0.125 to 0.125
- w_up: bfloat16 [2048, 8192], P('fsdp', 'tensor'), may hold values from -0.125 to 0.125
- w_down: bfloat16 [8192, 2048], P(('tensor', 'fsdp')), may hold values from -0.0625 to 0.0625
- cotangent: bfloat16 [4, 1024, 2048], P('fsdp', 'context'), may hold values from -6 to 6
Outputs:
- output: bfloat16 [4, 1024, 2048], P('fsdp', 'context')
- grad_tokens: bfloat16 [4, 1024, 2048], P('fsdp', 'context')
- grad_attn_gain: float32 [2048], P(('context', 'fsdp'))
- grad_w_query: float32 [2048, 2048], P(('context', 'fsdp'), 'tensor')
- grad_w_key: float32 [2048, 1024], P(('context', 'fsdp'), 'tensor')
- grad_w_value: float32 [2048, 1024], P(('context', 'fsdp'), 'tensor')
- grad_w_out: float32 [2048, 2048], P(('tensor', 'context', 'fsdp'))
- grad_ffn_gain: float32 [2048], P(('context', 'fsdp'))
- grad_w_gate: float32 [2048, 8192], P(('context', 'fsdp'), 'tensor')
- grad_w_up: float32 [2048, 8192], P(('context', 'fsdp'), 'tensor')
- grad_w_down: float32 [8192, 2048], P(('tensor', 'context', 'fsdp'))
Inputs may be any that keep to these rules, and one draw needn't show every extreme that they name: `segments`: A token's document number within its sequence: never falls along the sequence; each sequence holds 8 documents, one of them 1024 // 2 tokens long. `positions`: A token's place within its document: 0 at a document's first token, rising by one along it.
All inputs are finite; a program needn't handle non-finite values.
Results may differ from a plain program's by a relative error of at most 0.014.
Values may be sent and summed in bfloat16 or wider, within the bound.
No kernel may reach another device: no remote copies, remote signals or barrier semaphores. Data moves between devices by JAX's collectives and lax.ppermute only.
A program may use at most 320 MiB of HBM per device.

v0:
```python
import math

import jax
import jax.numpy as jnp
from jax import lax
from jax.sharding import PartitionSpec as P

HEAD = 128


norm_epsilon = 1e-05
rope_base = 1000000.0


def rotary(positions):
    freq_index = jnp.arange(HEAD // 2, dtype=jnp.float32)
    inverse = rope_base ** (-2.0 * freq_index / HEAD)
    angles = positions.astype(jnp.float32)[:, None] * inverse[None, :]
    angles = jnp.concatenate([angles, angles], axis=1)
    return (jnp.cos(angles), jnp.sin(angles))


def rotate(values, cos_table, sine_table):
    half_size = values.shape[-1] // 2
    lower_half = values[..., :half_size]
    upper_half = values[..., half_size:]
    turned = jnp.concatenate([-upper_half, lower_half], axis=-1)
    return values * cos_table[:, None, :] + turned * sine_table[:, None, :]


def unrotate(grad_rot, cos_table, sine_table):
    half_size = grad_rot.shape[-1] // 2
    scaled = grad_rot * sine_table[:, None, :]
    swapped = jnp.concatenate([scaled[..., half_size:], -scaled[..., :half_size]], axis=-1)
    return grad_rot * cos_table[:, None, :] + swapped


def norm_forward(values):
    inverse_rms = lax.rsqrt(jnp.mean(values * values, axis=-1, keepdims=True) + norm_epsilon)
    return (inverse_rms, values * inverse_rms)


def norm_backward(grad_normed, gain, inverse_rms, normalized):
    scaled = grad_normed * gain
    return inverse_rms * (
        scaled - normalized * jnp.mean(scaled * normalized, axis=-1, keepdims=True)
    )


def contract_rows(left, right):
    return lax.dot_general(
        left, right, (((0,), (0,)), ((), ())), preferred_element_type=jnp.float32
    )


def contract_cols(left, right):
    return lax.dot_general(
        left, right, (((1,), (1,)), ((), ())), preferred_element_type=jnp.float32
    )


def block_scores(query_blk, key_all, query_seg, key_seg, query_order, key_order, score_scale):
    scores = (
        jnp.einsum("qhgd,khd->hgqk", query_blk, key_all, preferred_element_type=jnp.float32)
        * score_scale
    )
    allowed = (query_seg[:, None] == key_seg[None, :]) & (
        query_order[:, None] >= key_order[None, :]
    )
    return jnp.where(allowed[None, None], scores, -1e30)


def attend_forward(
    queries, key_all, value_all, query_seg, key_seg, query_order, key_order, block_rows, score_scale
):
    block_count = queries.shape[0] // block_rows

    def one_block(pieces):
        query_blk, seg_blk, order_blk = pieces
        scores = block_scores(
            query_blk, key_all, seg_blk, key_seg, order_blk, key_order, score_scale
        )
        highest = jnp.max(scores, axis=-1, keepdims=True)
        weights = jnp.exp(scores - highest)
        row_total = jnp.sum(weights, axis=-1, keepdims=True)
        probabilities = weights / row_total
        attended = jnp.einsum(
            "hgqk,khd->qhgd",
            probabilities.astype(jnp.bfloat16),
            value_all,
            preferred_element_type=jnp.float32,
        )
        return (attended, highest + jnp.log(row_total))

    stacked = (
        queries.reshape((block_count, block_rows) + queries.shape[1:]),
        query_seg.reshape(block_count, block_rows),
        query_order.reshape(block_count, block_rows),
    )
    attended, logsum = lax.map(one_block, stacked)
    return (attended.reshape(queries.shape), logsum)


def attend_backward(
    queries,
    key_all,
    value_all,
    grad_attended,
    logsum,
    query_seg,
    key_seg,
    query_order,
    key_order,
    block_rows,
    score_scale,
):
    block_count = queries.shape[0] // block_rows
    empty_grad = jnp.zeros(key_all.shape, jnp.float32)

    def one_block(carry, pieces):
        grad_key, grad_value = carry
        query_blk, grad_blk, logsum_blk, seg_blk, order_blk = pieces
        scores = block_scores(
            query_blk, key_all, seg_blk, key_seg, order_blk, key_order, score_scale
        )
        probabilities = jnp.exp(scores - logsum_blk)
        grad_probs = jnp.einsum(
            "qhgd,khd->hgqk", grad_blk, value_all, preferred_element_type=jnp.float32
        )
        row_delta = jnp.sum(probabilities * grad_probs, axis=-1, keepdims=True)
        grad_scores = (probabilities * (grad_probs - row_delta)).astype(jnp.bfloat16)
        grad_query = score_scale * jnp.einsum(
            "hgqk,khd->qhgd", grad_scores, key_all, preferred_element_type=jnp.float32
        )
        grad_key = grad_key + score_scale * jnp.einsum(
            "hgqk,qhgd->khd", grad_scores, query_blk, preferred_element_type=jnp.float32
        )
        grad_value = grad_value + jnp.einsum(
            "hgqk,qhgd->khd",
            probabilities.astype(jnp.bfloat16),
            grad_blk,
            preferred_element_type=jnp.float32,
        )
        return ((grad_key, grad_value), grad_query)

    stacked = (
        queries.reshape((block_count, block_rows) + queries.shape[1:]),
        grad_attended.reshape((block_count, block_rows) + grad_attended.shape[1:]),
        logsum,
        query_seg.reshape(block_count, block_rows),
        query_order.reshape(block_count, block_rows),
    )
    (grad_key, grad_value), grad_query = lax.scan(one_block, (empty_grad, empty_grad), stacked)
    return (grad_query.reshape(queries.shape), grad_key, grad_value)


def per_device(
    tokens,
    segments,
    positions,
    attn_gain,
    w_query,
    w_key,
    w_value,
    w_out,
    ffn_gain,
    w_gate,
    w_up,
    w_down,
    cotangent,
):
    token_count = tokens.shape[1]
    residual = tokens[0].astype(jnp.float32)
    seq_start = lax.axis_index("context") * token_count
    key_seg = segments[0]
    key_order = jnp.arange(key_seg.shape[0], dtype=jnp.int32)
    query_seg = lax.dynamic_slice_in_dim(key_seg, seq_start, token_count)
    query_order = seq_start + jnp.arange(token_count, dtype=jnp.int32)
    cos_table, sine_table = rotary(positions[0])
    block_rows = math.gcd(token_count, 512)
    score_scale = 1.0 / math.sqrt(HEAD)
    gain_one, query_w, key_w, value_w, out_w = (
        lax.all_gather(attn_gain, "fsdp", axis=0, tiled=True),
        lax.all_gather(w_query, "fsdp", axis=0, tiled=True),
        lax.all_gather(w_key, "fsdp", axis=0, tiled=True),
        lax.all_gather(w_value, "fsdp", axis=0, tiled=True),
        lax.all_gather(w_out, "fsdp", axis=0, tiled=True),
    )
    gain_two, gate_w, up_w, down_w = (
        lax.all_gather(ffn_gain, "fsdp", axis=0, tiled=True),
        lax.all_gather(w_gate, "fsdp", axis=0, tiled=True),
        lax.all_gather(w_up, "fsdp", axis=0, tiled=True),
        lax.all_gather(w_down, "fsdp", axis=0, tiled=True),
    )
    query_heads = query_w.shape[1] // HEAD
    kv_heads = key_w.shape[1] // HEAD
    group_size = query_heads // kv_heads
    inverse_one, normal_one = norm_forward(residual)
    normed_one = (normal_one * gain_one.astype(jnp.float32)).astype(jnp.bfloat16)
    query_raw = jnp.dot(normed_one, query_w, preferred_element_type=jnp.float32)
    key_raw = jnp.dot(normed_one, key_w, preferred_element_type=jnp.float32)
    value_raw = jnp.dot(normed_one, value_w, preferred_element_type=jnp.float32)
    queries = rotate(
        query_raw.reshape(token_count, query_heads, HEAD), cos_table, sine_table
    ).astype(jnp.bfloat16)
    queries = queries.reshape(token_count, kv_heads, group_size, HEAD)
    key_local = rotate(key_raw.reshape(token_count, kv_heads, HEAD), cos_table, sine_table).astype(
        jnp.bfloat16
    )
    value_local = value_raw.astype(jnp.bfloat16).reshape(token_count, kv_heads, HEAD)
    key_all, value_all = (
        lax.all_gather(key_local, "context", axis=0, tiled=True),
        lax.all_gather(value_local, "context", axis=0, tiled=True),
    )
    attended, logsum = attend_forward(
        queries,
        key_all,
        value_all,
        query_seg,
        key_seg,
        query_order,
        key_order,
        block_rows,
        score_scale,
    )
    attended_low = attended.reshape(token_count, query_heads * HEAD).astype(jnp.bfloat16)
    attn_part = jnp.dot(attended_low, out_w, preferred_element_type=jnp.float32)
    hidden = residual + lax.psum(attn_part, "tensor")
    inverse_two, normal_two = norm_forward(hidden)
    normed_two = (normal_two * gain_two.astype(jnp.float32)).astype(jnp.bfloat16)
    gate_proj = jnp.dot(normed_two, gate_w, preferred_element_type=jnp.float32)
    up_proj = jnp.dot(normed_two, up_w, preferred_element_type=jnp.float32)
    sigmoid_gate = jax.nn.sigmoid(gate_proj)
    silu_gate = gate_proj * sigmoid_gate
    activation = (silu_gate * up_proj).astype(jnp.bfloat16)
    ffn_part = jnp.dot(activation, down_w, preferred_element_type=jnp.float32)
    block_out = hidden + lax.psum(ffn_part.astype(jnp.bfloat16), "tensor").astype(jnp.float32)
    output = block_out.astype(jnp.bfloat16)[None]
    grad_rows = cotangent[0]
    term_down = contract_rows(activation, grad_rows)
    grad_act = contract_cols(grad_rows, down_w)
    grad_gate = (
        grad_act * up_proj * sigmoid_gate * (1.0 + gate_proj * (1.0 - sigmoid_gate))
    ).astype(jnp.bfloat16)
    grad_up = (grad_act * silu_gate).astype(jnp.bfloat16)
    term_gate = contract_rows(normed_two, grad_gate)
    term_up = contract_rows(normed_two, grad_up)
    grad_norm_two = contract_cols(grad_gate, gate_w) + contract_cols(grad_up, up_w)
    grad_norm_two = lax.psum(grad_norm_two, "tensor")
    term_gain_two = jnp.sum(grad_norm_two * normal_two, axis=0)
    grad_hidden = grad_rows.astype(jnp.float32) + norm_backward(
        grad_norm_two, gain_two.astype(jnp.float32), inverse_two, normal_two
    )
    hidden_low = grad_hidden.astype(jnp.bfloat16)
    term_out = contract_rows(attended_low, hidden_low)
    grad_attended = (
        contract_cols(hidden_low, out_w)
        .astype(jnp.bfloat16)
        .reshape(token_count, kv_heads, group_size, HEAD)
    )
    key_back, value_back = (key_all, value_all)
    grad_query, grad_key_all, grad_value_all = attend_backward(
        queries,
        key_back,
        value_back,
        grad_attended,
        logsum,
        query_seg,
        key_seg,
        query_order,
        key_order,
        block_rows,
        score_scale,
    )
    grad_key_rot, grad_value_rot = (
        lax.psum_scatter(grad_key_all, "context", scatter_dimension=0, tiled=True),
        lax.psum_scatter(grad_value_all, "context", scatter_dimension=0, tiled=True),
    )
    grad_query_low = unrotate(
        grad_query.reshape(token_count, query_heads, HEAD), cos_table, sine_table
    )
    grad_query_low = grad_query_low.reshape(token_count, query_heads * HEAD).astype(jnp.bfloat16)
    grad_key_low = (
        unrotate(grad_key_rot, cos_table, sine_table)
        .reshape(token_count, kv_heads * HEAD)
        .astype(jnp.bfloat16)
    )
    grad_value_low = grad_value_rot.reshape(token_count, kv_heads * HEAD).astype(jnp.bfloat16)
    term_query = contract_rows(normed_one, grad_query_low)
    term_key = contract_rows(normed_one, grad_key_low)
    term_value = contract_rows(normed_one, grad_value_low)
    grad_norm_one = (
        contract_cols(grad_query_low, query_w)
        + contract_cols(grad_key_low, key_w)
        + contract_cols(grad_value_low, value_w)
    )
    grad_norm_one = lax.psum(grad_norm_one, "tensor")
    term_gain_one = jnp.sum(grad_norm_one * normal_one, axis=0)
    grad_input = grad_hidden + norm_backward(
        grad_norm_one, gain_one.astype(jnp.float32), inverse_one, normal_one
    )
    summed = (
        lax.psum_scatter(term_gain_one, ("context", "fsdp"), scatter_dimension=0, tiled=True),
        lax.psum_scatter(term_query, ("context", "fsdp"), scatter_dimension=0, tiled=True),
        lax.psum_scatter(term_key, ("context", "fsdp"), scatter_dimension=0, tiled=True),
        lax.psum_scatter(term_value, ("context", "fsdp"), scatter_dimension=0, tiled=True),
        lax.psum_scatter(term_out, ("context", "fsdp"), scatter_dimension=0, tiled=True),
        lax.psum_scatter(term_gain_two, ("context", "fsdp"), scatter_dimension=0, tiled=True),
        lax.psum_scatter(term_gate, ("context", "fsdp"), scatter_dimension=0, tiled=True),
        lax.psum_scatter(term_up, ("context", "fsdp"), scatter_dimension=0, tiled=True),
        lax.psum_scatter(term_down, ("context", "fsdp"), scatter_dimension=0, tiled=True),
    )
    return (
        output,
        grad_input.astype(jnp.bfloat16)[None],
        summed[0],
        summed[1],
        summed[2],
        summed[3],
        summed[4],
        summed[5],
        summed[6],
        summed[7],
        summed[8],
    )


def solution(mesh):
    return jax.shard_map(
        per_device,
        mesh=mesh,
        in_specs=(
            P("fsdp", "context", None),
            P("fsdp", None),
            P("fsdp", "context"),
            P("fsdp"),
            P("fsdp", "tensor"),
            P("fsdp", "tensor"),
            P("fsdp", "tensor"),
            P(("tensor", "fsdp"), None),
            P("fsdp"),
            P("fsdp", "tensor"),
            P("fsdp", "tensor"),
            P(("tensor", "fsdp"), None),
            P("fsdp", "context", None),
        ),
        out_specs=(
            P("fsdp", "context", None),
            P("fsdp", "context", None),
            P(("context", "fsdp")),
            P(("context", "fsdp"), "tensor"),
            P(("context", "fsdp"), "tensor"),
            P(("context", "fsdp"), "tensor"),
            P(("tensor", "context", "fsdp"), None),
            P(("context", "fsdp")),
            P(("context", "fsdp"), "tensor"),
            P(("context", "fsdp"), "tensor"),
            P(("tensor", "context", "fsdp"), None),
        ),
        check_vma=False,
    )
```

profile of v0, /device:TPU:0, one launch (start us, length us, event | category | flops | bytes accessed | tf_op | source)
XLA Modules:
  0.0 2918.4 jit_solution(17732838352116925399)
XLA Ops:
  9.5 13.6 all-gather
  23.9 34.3 %all-gather.16.cloned.1.call-done = bf16[2048,512]{1,0:T(8,128)(2,1)} async-done(((bf16[512,512]{1,0:T(8,128)(2,1)}), bf16[2048,512]{1,0:T(8,128)(2,1)}) %all-gather.16.cloned.1.call-update) | async-done | bytes 2097168 | tf_op jit(solution)/shard_map/all_gather | solution.py:185
  63.0 41.9 %all-gather.12.cloned.1.call-done = bf16[2048,512]{1,0:T(8,128)(2,1)} async-done(((bf16[512,512]{1,0:T(8,128)(2,1)}), bf16[2048,512]{1,0:T(8,128)(2,1)}) %all-gather.12.cloned.1.call-update) | async-done | bytes 2097168 | tf_op jit(solution)/shard_map/all_gather | solution.py:186
  109.0 76.9 %all-gather.20.cloned.1.call-done = bf16[2048,1024]{1,0:T(8,128)(2,1)} async-done(((bf16[512,1024]{1,0:T(8,128)(2,1)}), bf16[2048,1024]{1,0:T(8,128)(2,1)}) %all-gather.20.cloned.1.call-update) | async-done | bytes 4194320 | tf_op jit(solution)/shard_map/all_gather | solution.py:184
  227.4 77.0 %all-gather.22.cloned.1.call-done = bf16[1024,2048]{1,0:T(8,128)(2,1)} async-done(((bf16[256,2048]{1,0:T(8,128)(2,1)}), bf16[1024,2048]{1,0:T(8,128)(2,1)}) %all-gather.22.cloned.1.call-update) | async-done | bytes 4194320 | tf_op jit(solution)/shard_map/all_gather | solution.py:187
  323.4 47.3 %all-reduce.8.cloned.1.call-done = f32[256,2048]{1,0:T(8,128)} async-done(((f32[256,2048]{1,0:T(8,128)}), f32[256,2048]{1,0:T(8,128)}) %all-reduce.8.cloned.1.call-update) | async-done | bytes 2097168 | tf_op jit(solution)/shard_map/psum | solution.py:228
  374.0 285.3 %all-gather.26.cloned.1.call-done = bf16[2048,4096]{1,0:T(8,128)(2,1)} async-done(((bf16[512,4096]{1,0:T(8,128)(2,1)}), bf16[2048,4096]{1,0:T(8,128)(2,1)}) %all-gather.26.cloned.1.call-update) | async-done | bytes 16777232 | tf_op jit(solution)/shard_map/all_gather | solution.py:192
  671.9 274.0 %all-gather.24.cloned.1.call-done = bf16[2048,4096]{1,0:T(8,128)(2,1)} async-done(((bf16[512,4096]{1,0:T(8,128)(2,1)}), bf16[2048,4096]{1,0:T(8,128)(2,1)}) %all-gather.24.cloned.1.call-update) | async-done | bytes 16777232 | tf_op jit(solution)/shard_map/all_gather | solution.py:191
  958.5 273.9 %all-gather.28.cloned.1.call-done = bf16[4096,2048]{1,0:T(8,128)(2,1)} async-done(((bf16[1024,2048]{1,0:T(8,128)(2,1)}), bf16[4096,2048]{1,0:T(8,128)(2,1)}) %all-gather.28.cloned.1.call-update) | async-done | bytes 16777232 | tf_op jit(solution)/shard_map/all_gather | solution.py:193
  1232.4 13.7 multiply_convert_fusion
  1284.1 48.4 %all-reduce.12.cloned.1.call-done = f32[256,2048]{1,0:T(8,128)} async-done(((f32[256,2048]{1,0:T(8,128)}), f32[256,2048]{1,0:T(8,128)}) %all-reduce.12.cloned.1.call-update) | async-done | bytes 2097168 | tf_op jit(solution)/shard_map/psum | solution.py:249
  1335.3 40.0 %all-reduce.10.cloned.1.call-done = bf16[256,2048]{1,0:T(8,128)(2,1)} async-done(((bf16[256,2048]{1,0:T(8,128)(2,1)}), bf16[256,2048]{1,0:T(8,128)(2,1)}) %all-reduce.10.cloned.1.call-update) | async-done | bytes 1048592 | tf_op jit(solution)/shard_map/psum | solution.py:237
  1410.7 15.6 reduce-scatter.10.cloned.1.call-done
  1428.2 31.9 %reduce-scatter.12.cloned.1.call-done = f32[256,4,128]{0,2,1:T(8,128)} async-done(((f32[1024,4,128]{0,2,1:T(8,128)}), f32[256,4,128]{0,2,1:T(8,128)}) %reduce-scatter.12.cloned.1.call-update) | async-done | bytes 524304 | tf_op jit(solution)/shard_map/reduce_scatter | solution.py:277
  1486.6 18.1 fusion.46
  1504.7 17.9 fusion.86
  1523.0 17.9 fusion.85
  1545.2 61.3 %all-reduce.2 = (f32[2048]{0:T(1024)S(1)}, f32[2048]{0:T(1024)S(1)}) all-reduce(f32[2048]{0:T(1024)S(1)} %get-tuple-element.69, f32[2048]{0:T(1024)S(1)} %copy-done.16), channel_id=4, replica_groups=mesh['tensor'=2,'context'=4,'fsdp'=4] {'context','fsdp'}, use_global_device_ids=true, to_apply=%region_14.15.clone | all-reduce | flops 4096 | bytes 32768
  1610.8 72.4 %reduce-scatter.16.cloned.1.call-done = f32[128,512]{1,0:T(8,128)} async-done(((f32[2048,512]{1,0:T(8,128)}), f32[128,512]{1,0:T(8,128)}) %reduce-scatter.16.cloned.1.call-update) | async-done | bytes 262160 | tf_op jit(solution)/shard_map/reduce_scatter | solution.py:305
  1683.3 108.2 %reduce-scatter.20.cloned.1.call-done = f32[64,2048]{1,0:T(8,128)} async-done(((f32[1024,2048]{1,0:T(8,128)}), f32[64,2048]{1,0:T(8,128)}) %reduce-scatter.20.cloned.1.call-update) | async-done | bytes 524304 | tf_op jit(solution)/shard_map/reduce_scatter | solution.py:307
  1791.5 109.0 %reduce-scatter.14.cloned.1.call-done = f32[128,1024]{1,0:T(8,128)} async-done(((f32[2048,1024]{1,0:T(8,128)}), f32[128,1024]{1,0:T(8,128)}) %reduce-scatter.14.cloned.1.call-update) | async-done | bytes 524304 | tf_op jit(solution)/shard_map/reduce_scatter | solution.py:304
  1900.5 337.2 %reduce-scatter.26.cloned.1.call-done = f32[256,2048]{1,0:T(8,128)} async-done(((f32[4096,2048]{1,0:T(8,128)}), f32[256,2048]{1,0:T(8,128)}) %reduce-scatter.26.cloned.1.call-update) | async-done | bytes 2097168 | tf_op jit(solution)/shard_map/reduce_scatter | solution.py:311
  2237.7 336.6 %reduce-scatter.24.cloned.1.call-done = f32[128,4096]{1,0:T(8,128)} async-done(((f32[2048,4096]{1,0:T(8,128)}), f32[128,4096]{1,0:T(8,128)}) %reduce-scatter.24.cloned.1.call-update) | async-done | bytes 2097168 | tf_op jit(solution)/shard_map/reduce_scatter | solution.py:310
  2574.3 336.7 %reduce-scatter.22.cloned.1.call-done = f32[128,4096]{1,0:T(8,128)} async-done(((f32[2048,4096]{1,0:T(8,128)}), f32[128,4096]{1,0:T(8,128)}) %reduce-scatter.22.cloned.1.call-update) | async-done | bytes 2097168 | tf_op jit(solution)/shard_map/reduce_scatter | solution.py:309
  (167 shorter events, 213.2 us)
Async XLA Ops:
  7.2 51.1 %all-gather.16.cloned.1.call-start = ((), (), s32[]{:S(2)}) async-start(), calls=%async_computation.11 | async-start | bytes 2621440 | tf_op jit(solution)/shard_map/all_gather | solution.py:185
  7.9 96.9 %all-gather.12.cloned.1.call-start = ((), (), s32[]{:S(2)}) async-start(), calls=%async_computation.9 | async-start | bytes 2621440 | tf_op jit(solution)/shard_map/all_gather | solution.py:186
  8.7 177.2 %all-gather.20.cloned.1.call-start = ((), (), s32[]{:S(2)}) async-start(), calls=%async_computation.13 | async-start | bytes 5242880 | tf_op jit(solution)/shard_map/all_gather | solution.py:184
  9.4 193.9 %all-gather.18.cloned.1.call-start = ((), (), s32[]{:S(2)}) async-start(), calls=%async_computation.12 | async-start | bytes 1310720 | tf_op jit(solution)/shard_map/all_gather | solution.py:212
  62.9 159.2 %all-gather.14.cloned.1.call-start = ((), (), s32[]{:S(2)}) async-start(), calls=%async_computation.10 | async-start | bytes 1310720 | tf_op jit(solution)/shard_map/all_gather | solution.py:213
  108.0 196.3 %all-gather.22.cloned.1.call-start = ((), (), s32[]{:S(2)}) async-start(), calls=%async_computation.14 | async-start | bytes 5242880 | tf_op jit(solution)/shard_map/all_gather | solution.py:187
  108.6 262.2 %all-reduce.8.cloned.1.call-start = ((), (), s32[]{:S(2)}) async-start(), calls=%async_computation.15 | async-start | bytes 4194304 | tf_op jit(solution)/shard_map/psum | solution.py:228
  227.4 81.8 %copy-start.15 = (bf16[4,128,2,256]{3,1,2,0:T(8,128)(2,1)}, bf16[4,128,2,256]{3,1,2,0:T(8,128)(2,1)S(1)}, u32[]{:S(2)}) copy-start(bf16[4,128,2,256]{3,1,2,0:T(8,128)(2,1)S(1)} %fusion.31) | copy-start | bytes 1572868
  309.2 350.1 %all-gather.26.cloned.1.call-start = ((), (), s32[]{:S(2)}) async-start(), calls=%async_computation.17 | async-start | bytes 20971520 | tf_op jit(solution)/shard_map/all_gather | solution.py:192
  309.9 636.0 %all-gather.24.cloned.1.call-start = ((), (), s32[]{:S(2)}) async-start(), calls=%async_computation.16 | async-start | bytes 20971520 | tf_op jit(solution)/shard_map/all_gather | solution.py:191
  310.7 921.7 %all-gather.28.cloned.1.call-start = ((), (), s32[]{:S(2)}) async-start(), calls=%async_computation.18 | async-start | bytes 20971520 | tf_op jit(solution)/shard_map/all_gather | solution.py:193
  311.3 1021.2 %all-reduce.12.cloned.1.call-start = ((), (), s32[]{:S(2)}) async-start(), calls=%async_computation.20 | async-start | bytes 4194304 | tf_op jit(solution)/shard_map/psum | solution.py:249
  1271.2 104.1 %all-reduce.10.cloned.1.call-start = ((), (), s32[]{:S(2)}) async-start(), calls=%async_computation.19 | async-start | bytes 2097152 | tf_op jit(solution)/shard_map/psum | solution.py:237
  1284.1 142.3 %reduce-scatter.10.cloned.1.call-start = ((), (), s32[]{:S(2)}) async-start(), calls=%async_computation.21 | async-start | bytes 2621440 | tf_op jit(solution)/shard_map/reduce_scatter | solution.py:276
  1394.7 65.5 %reduce-scatter.12.cloned.1.call-start = ((), (), s32[]{:S(2)}) async-start(), calls=%async_computation.22 | async-start | bytes 2621440 | tf_op jit(solution)/shard_map/reduce_scatter | solution.py:277
  1401.0 141.7 %all-reduce.14.cloned.1.call-start = ((), (), s32[]{:S(2)}) async-start(), calls=%async_computation.23 | async-start | bytes 4194304 | tf_op jit(solution)/shard_map/psum | solution.py:297
  1410.7 52.0 %copy-start.5 = (bf16[2048,512]{1,0:T(8,128)(2,1)S(1)}, bf16[2048,512]{1,0:T(8,128)(2,1)}, u32[]{:S(2)}) copy-start(bf16[2048,512]{1,0:T(8,128)(2,1)} %all-gather.16.cloned.1.call-done) | copy-start | bytes 6291460
  1466.5 144.3 %reduce-scatter.18.cloned.1.call-start = ((), (), s32[]{:S(2)}) async-start(), calls=%async_computation.26 | async-start | bytes 4456448 | tf_op jit(solution)/shard_map/reduce_scatter | solution.py:306
  1469.5 213.8 %reduce-scatter.16.cloned.1.call-start = ((), (), s32[]{:S(2)}) async-start(), calls=%async_computation.25 | async-start | bytes 4456448 | tf_op jit(solution)/shard_map/reduce_scatter | solution.py:305
  1473.3 318.2 %reduce-scatter.20.cloned.1.call-start = ((), (), s32[]{:S(2)}) async-start(), calls=%async_computation.27 | async-start | bytes 8912896 | tf_op jit(solution)/shard_map/reduce_scatter | solution.py:307
  1480.5 420.0 %reduce-scatter.14.cloned.1.call-start = ((), (), s32[]{:S(2)}) async-start(), calls=%async_computation.24 | async-start | bytes 8912896 | tf_op jit(solution)/shard_map/reduce_scatter | solution.py:304
  1486.3 751.4 %reduce-scatter.26.cloned.1.call-start = ((), (), s32[]{:S(2)}) async-start(), calls=%async_computation.30 | async-start | bytes 35651584 | tf_op jit(solution)/shard_map/reduce_scatter | solution.py:311
  1504.7 1069.6 %reduce-scatter.24.cloned.1.call-start = ((), (), s32[]{:S(2)}) async-start(), calls=%async_computation.29 | async-start | bytes 35651584 | tf_op jit(solution)/shard_map/reduce_scatter | solution.py:310
  1522.6 1388.4 %reduce-scatter.22.cloned.1.call-start = ((), (), s32[]{:S(2)}) async-start(), calls=%async_computation.28 | async-start | bytes 35651584 | tf_op jit(solution)/shard_map/reduce_scatter | solution.py:309
  (23 other events, 121.9 us)
Sparse Core Ops, SparseCore 0:
  9.6 48.6 all-gather.15
  59.8 44.9 all-gather.11
  106.4 79.4 all-gather.19
  187.9 15.3 all-gather.17
  205.3 16.8 all-gather.13
  223.6 80.7 all-gather.21
  309.3 61.4 all-reduce.7
  372.4 286.7 all-gather.25
  660.9 284.9 all-gather.23
  947.4 284.9 all-gather.27
  1271.4 61.0 all-reduce.11
  1335.2 40.0 all-reduce.9
  1394.8 31.4 reduce-scatter.9
  1428.7 31.4 reduce-scatter.11
  1466.6 62.8 all-reduce.13
  1533.9 72.9 reduce-scatter.17
  1611.6 71.6 reduce-scatter.15
  1687.8 103.6 reduce-scatter.19
  1796.1 104.3 reduce-scatter.13
  1905.1 332.5 reduce-scatter.25
  2242.5 331.7 reduce-scatter.23
  2579.1 331.8 reduce-scatter.21
where the time goes:
time: 2930 us; the launch traced here: 2920 us
  waiting for transfers between devices  2570 us (88%)
  matrix products  192 us (7%)
  blocking collectives  87 us (3%)
    reduce_scatter x1, waiting for transfers between devices, per_device(): lax.psum_scatter(term_down, ('context', 'fsdp'), scatter_dimension=0, til...  337 us
    reduce_scatter x1, waiting for transfers between devices, per_device(): lax.psum_scatter(term_gate, ('context', 'fsdp'), scatter_dimension=0, til...  337 us
    reduce_scatter x1, waiting for transfers between devices, per_device(): lax.psum_scatter(term_up, ('context', 'fsdp'), scatter_dimension=0, tiled...  337 us
    all_gather x1, waiting for transfers between devices, per_device(): lax.all_gather(w_up, 'fsdp', axis=0, tiled=True)  285 us
    all_gather x1, waiting for transfers between devices, per_device(): lax.all_gather(w_gate, 'fsdp', axis=0, tiled=True)  274 us
    all_gather x1, waiting for transfers between devices, per_device(): lax.all_gather(w_down, 'fsdp', axis=0, tiled=True)  274 us
    reduce_scatter x1, waiting for transfers between devices, per_device(): lax.psum_scatter(term_query, ('context', 'fsdp'), scatter_dimension=0, ti...  109 us
    reduce_scatter x1, waiting for transfers between devices, per_device(): lax.psum_scatter(term_out, ('context', 'fsdp'), scatter_dimension=0, tile...  108 us
  transfers between devices with their start and end apart: 22, of which 20 were waited for; matrix products, arithmetic and copies ran while one was open for 6% of the time, Pallas kernels for 0%

commit v1 on v0

--- a/solution.py
+++ b/solution.py
@@ -154,7 +154,7 @@
     return (grad_query.reshape(queries.shape), grad_key, grad_value)
 
 
-def per_device(
+def per_device_general(
     tokens,
     segments,
     positions,
@@ -325,9 +325,379 @@
     )
 
 
+def order_pair(mine, theirs, index):
+    first = index == 0
+    return jnp.stack([jnp.where(first, mine, theirs), jnp.where(first, theirs, mine)])
+
+
+def pick(stack, index, axis=0):
+    return lax.dynamic_index_in_dim(stack, index, axis, keepdims=False)
+
+
+def over_core(block):
+    return lax.ppermute(block, "context", [(i, i ^ 1) for i in range(4)])
+
+
+def over_y(block):
+    return lax.ppermute(block, "context", [(i, i ^ 2) for i in range(4)])
+
+
+def over_diagonal(block):
+    return lax.ppermute(block, "context", [(i, i ^ 3) for i in range(4)])
+
+
+def over_x(block):
+    return lax.ppermute(block, "tensor", [(0, 1), (1, 0)])
+
+
+def shift_z(block, step):
+    return lax.ppermute(block, "fsdp", [(i, (i + step) % 4) for i in range(4)])
+
+
+def exchange_z(block, distance):
+    return lax.ppermute(block, "fsdp", [(i, i ^ distance) for i in range(4)])
+
+
+def ring_gather(block):
+    blocks = [block]
+    for _ in range(3):
+        blocks.append(shift_z(blocks[-1], 1))
+    return blocks
+
+
+def ring_reduce(terms):
+    total = terms[1]
+    for step in (2, 3, 0):
+        total = shift_z(total, 1).astype(jnp.float32) + terms[step].astype(jnp.float32)
+        if step:
+            total = total.astype(jnp.bfloat16)
+    return total
+
+
+def low(values):
+    return values.astype(jnp.bfloat16)
+
+
+def wide(values):
+    return values.astype(jnp.float32)
+
+
+def plane_reduce(partial):
+    half = partial.shape[-1] // 2
+    mine = low(wide(partial[0]) + wide(over_core(partial[1])))
+    left, right = mine[..., :half], mine[..., half:]
+    left = low(wide(left[:, 0]) + wide(over_x(left[:, 1])))
+    right = low(wide(right[0]) + wide(over_y(right[1])))
+    left = wide(left[0]) + wide(over_y(left[1]))
+    right = wide(right[0]) + wide(over_x(right[1]))
+    return jnp.concatenate([left, right], axis=-1)
+
+
+def plane_gather(block):
+    half = block.shape[-1] // 2
+    left, right = block[:, :half], block[:, half:]
+    left = jnp.stack([left, over_x(left)])
+    right = jnp.stack([right, over_y(right)])
+    left = jnp.stack([left, over_y(left)])
+    right = jnp.stack([right, over_x(right)], axis=1)
+    mine = jnp.concatenate([left, right], axis=-1)
+    return jnp.stack([mine, over_core(mine)])
+
+
+def group_spread(block):
+    pair = jnp.stack([block, over_x(block)])
+    return jnp.stack([pair, over_core(pair)])
+
+
+def group_reduce(partial):
+    mine = low(wide(partial[0]) + wide(over_core(partial[1])))
+    return low(wide(mine[0]) + wide(over_x(mine[1])))
+
+
+def gain_reduce(term, context_at, fsdp_at):
+    y_at, core_at = context_at // 2, context_at % 2
+    term = term + over_x(term)
+    term = term.reshape(2, 2, 2, 2, -1)
+    term = pick(term, core_at, 1) + over_core(pick(term, 1 - core_at, 1))
+    term = pick(term, y_at) + over_y(pick(term, 1 - y_at))
+    high, lowest = fsdp_at // 2, fsdp_at % 2
+    term = pick(term, high) + exchange_z(pick(term, 1 - high), 2)
+    return pick(term, lowest) + exchange_z(pick(term, 1 - lowest), 1)
+
+
+def context_spread(blocks, context_at):
+    got = jnp.stack(
+        [
+            pick(blocks, context_at),
+            over_core(pick(blocks, context_at ^ 1)),
+            over_y(pick(blocks, context_at ^ 2)),
+            over_diagonal(pick(blocks, context_at ^ 3)),
+        ]
+    )
+    return [pick(got, i ^ context_at) for i in range(4)]
+
+
+def fsdp_spread(blocks, fsdp_at):
+    got = [pick(blocks, fsdp_at)]
+    for step in (1, 2, 3):
+        got.append(shift_z(pick(blocks, (fsdp_at + step) % 4), step))
+    got = jnp.stack(got)
+    return [pick(got, (fsdp_at - i) % 4) for i in range(4)]
+
+
+def attention_forward(queries, keys, values, allowed, score_scale):
+    scores = jnp.einsum("qhd,kd->hqk", queries, keys, preferred_element_type=jnp.float32)
+    scores = jnp.where(allowed[None], scores * score_scale, -1e30)
+    highest = jnp.max(scores, axis=-1, keepdims=True)
+    weights = jnp.exp(scores - highest)
+    row_total = jnp.sum(weights, axis=-1, keepdims=True)
+    probabilities = low(weights / row_total)
+    attended = jnp.einsum(
+        "hqk,kd->qhd", probabilities, values, preferred_element_type=jnp.float32
+    )
+    return low(attended), highest + jnp.log(row_total)
+
+
+def attention_backward(queries, keys, values, grad_attended, logsum, allowed, score_scale):
+    scores = jnp.einsum("qhd,kd->hqk", queries, keys, preferred_element_type=jnp.float32)
+    scores = jnp.where(allowed[None], scores * score_scale, -1e30)
+    probabilities = jnp.exp(scores - logsum)
+    grad_probs = jnp.einsum(
+        "qhd,kd->hqk", grad_attended, values, preferred_element_type=jnp.float32
+    )
+    row_delta = jnp.sum(probabilities * grad_probs, axis=-1, keepdims=True)
+    grad_scores = low(probabilities * (grad_probs - row_delta))
+    grad_query = score_scale * jnp.einsum(
+        "hqk,kd->qhd", grad_scores, keys, preferred_element_type=jnp.float32
+    )
+    grad_key = score_scale * jnp.einsum(
+        "hqk,qhd->kd", grad_scores, queries, preferred_element_type=jnp.float32
+    )
+    grad_value = jnp.einsum(
+        "hqk,qhd->kd", low(probabilities), grad_attended, preferred_element_type=jnp.float32
+    )
+    return grad_query, grad_key, grad_value
+
+
+def per_device_moved(
+    tokens,
+    segments,
+    positions,
+    attn_gain,
+    w_query,
+    w_key,
+    w_value,
+    w_out,
+    ffn_gain,
+    w_gate,
+    w_up,
+    w_down,
+    cotangent,
+):
+    tensor_at, context_at, fsdp_at = (lax.axis_index(a) for a in ("tensor", "context", "fsdp"))
+    y_at, core_at = context_at // 2, context_at % 2
+    width = tokens.shape[2]
+    block_rows = tokens.shape[1]
+    rows = block_rows // 2
+    length = segments.shape[1]
+    score_scale = 1.0 / math.sqrt(HEAD)
+    shard = attn_gain.shape[0]
+    head_cols = w_query.shape[1] // 4
+    kv_cols = w_key.shape[1] // 4
+    group_size = head_cols // kv_cols
+
+    def split_x(block):
+        pair = block.reshape((2, rows) + block.shape[1:])
+        return jnp.where(tensor_at == 0, pair, pair[::-1])
+
+    def spread_context(block):
+        pair = jnp.stack([block, over_y(block)])
+        return jnp.stack([pair, over_core(pair)])
+
+    own_tokens = split_x(tokens[0])
+    all_tokens = spread_context(own_tokens)
+    all_places = spread_context(split_x(positions[0])).reshape(length)
+
+    def head_slice(weight, cols):
+        return lax.dynamic_slice_in_dim(weight, context_at * cols, cols, axis=1)
+
+    gains = jnp.zeros((16, head_cols + 2 * kv_cols), jnp.bfloat16)
+    gains = gains.at[0, :shard].set(attn_gain).at[1, :shard].set(ffn_gain)
+    packed = jnp.concatenate(
+        [
+            jnp.concatenate(
+                [
+                    head_slice(w_query, head_cols),
+                    head_slice(w_key, kv_cols),
+                    head_slice(w_value, kv_cols),
+                ],
+                axis=1,
+            ),
+            gains,
+        ],
+        axis=0,
+    )
+    packed_all = jnp.stack(ring_gather(packed))
+    packed_all = jnp.stack([pick(packed_all, (fsdp_at - i) % 4) for i in range(4)])
+    attn_w = packed_all[:, :shard].reshape(width, head_cols + 2 * kv_cols)
+    gain_one = wide(packed_all[:, shard, :shard].reshape(width))
+    gain_two = wide(packed_all[:, shard + 1, :shard].reshape(width))
+
+    out_cols = w_out.shape[1] // 4
+    out_part = lax.dynamic_slice_in_dim(w_out, context_at * out_cols, out_cols, axis=1)
+    out_all = jnp.stack(ring_gather(out_part))
+    out_all = jnp.stack([pick(out_all, (fsdp_at - i) % 4) for i in range(4)])
+    out_w = jnp.concatenate(context_spread(out_all, context_at), axis=1)
+
+    unit_half = w_gate.shape[1] // 16
+    units = 2 * unit_half
+
+    def unit_weights(weight):
+        mine = weight.reshape(shard, 4, 2, 2, unit_half)
+        mine = pick(pick(mine, core_at, 2), y_at, 2)
+        return jnp.moveaxis(mine, 1, 0)
+
+    both = jnp.stack([unit_weights(w_gate), unit_weights(w_up)], axis=1)
+    both = jnp.stack(fsdp_spread(both, fsdp_at), axis=1).reshape(2, width, unit_half)
+    both = order_pair(both, over_y(both), y_at)
+    gate_w = jnp.concatenate([both[0, 0], both[1, 0]], axis=1)
+    up_w = jnp.concatenate([both[0, 1], both[1, 1]], axis=1)
+    down_w = lax.dynamic_slice_in_dim(w_down, core_at * units, units, axis=0)
+
+    own_cotangent = split_x(cotangent[0])
+    cotangent_ring = ring_gather(own_cotangent[0])
+    cotangents = [jnp.stack([own_cotangent, over_core(own_cotangent)])] + [
+        group_spread(block) for block in cotangent_ring[1:]
+    ]
+    cotangents = [block.reshape(4 * rows, width) for block in cotangents]
+
+    def flip(block, axis, index):
+        return jnp.where(index == 0, block, jnp.flip(block, axis))
+
+    def relative(block):
+        block = block.reshape(2, 2, 2, rows)
+        block = flip(flip(flip(block, 0, y_at), 1, core_at), 2, tensor_at)
+        return jnp.swapaxes(block, 0, 1).reshape(length)
+
+    order = relative(jnp.arange(length, dtype=jnp.int32))
+    seg = relative(segments[0])
+    allowed = (seg[:, None] == seg[None, :]) & (order[:, None] >= order[None, :])
+    cos_table, sine_table = rotary(all_places)
+    residual = wide(all_tokens.reshape(length, width))
+    inverse_one, normal_one = norm_forward(residual)
+    normed_one = low(normal_one * gain_one)
+    projected = jnp.dot(normed_one, attn_w, preferred_element_type=jnp.float32)
+    heads = projected[:, : head_cols + kv_cols].reshape(length, group_size + 1, HEAD)
+    turned = low(rotate(heads, cos_table, sine_table))
+    queries, keys = turned[:, :group_size], turned[:, group_size]
+    values = low(projected[:, head_cols + kv_cols :])
+    attended, logsum = attention_forward(queries, keys, values, allowed, score_scale)
+    attended = attended.reshape(length, head_cols)
+    attn_part = low(jnp.dot(attended, out_w, preferred_element_type=jnp.float32))
+    hidden = residual[:rows] + plane_reduce(attn_part.reshape(2, 2, 2, rows, width))
+    inverse_two, normal_two = norm_forward(hidden)
+    normed_two = low(normal_two * gain_two)
+
+    kept = []
+    out_terms, norm_terms = [None] * 4, [None] * 4
+    ring = ring_gather(normed_two)
+    for step in (0, 1, 2, 3):
+        normed = group_spread(ring[step]).reshape(4 * rows, width)
+        gate_proj = jnp.dot(normed, gate_w, preferred_element_type=jnp.float32)
+        up_proj = jnp.dot(normed, up_w, preferred_element_type=jnp.float32)
+        sigmoid_gate = jax.nn.sigmoid(gate_proj)
+        silu_gate = gate_proj * sigmoid_gate
+        activation = low(silu_gate * up_proj)
+        grad_rows = cotangents[step]
+        grad_act = contract_cols(grad_rows, down_w)
+        grad_gate = low(grad_act * up_proj * sigmoid_gate * (1.0 + gate_proj * (1.0 - sigmoid_gate)))
+        grad_up = low(grad_act * silu_gate)
+        grad_norm = low(contract_cols(grad_gate, gate_w) + contract_cols(grad_up, up_w))
+        norm_terms[step] = group_reduce(grad_norm.reshape(2, 2, rows, width))
+        ffn_part = low(jnp.dot(activation, down_w, preferred_element_type=jnp.float32))
+        out_terms[step] = group_reduce(ffn_part.reshape(2, 2, rows, width))
+        kept.append((normed, activation, grad_gate, grad_up))
+    grad_norm_two = ring_reduce(norm_terms)
+    block_out = low(hidden + ring_reduce(out_terms))
+    output = order_pair(block_out, over_x(block_out), tensor_at).reshape(1, block_rows, width)
+
+    normed_all, activation_all, grad_gate_all, grad_up_all = (
+        jnp.concatenate([parts[i] for parts in kept]) for i in range(4)
+    )
+    cotangent_all = jnp.concatenate(cotangents)
+
+    def spread_columns(term):
+        term = term.reshape(2, 2, 4, width // 16, units)
+        term = low(wide(pick(term, y_at)) + wide(over_y(pick(term, 1 - y_at))))
+        term = order_pair(pick(term, core_at), over_core(pick(term, 1 - core_at)), core_at)
+        term = jnp.moveaxis(term, 0, 2).reshape(4, width // 16, 2 * units)
+        return wide(jnp.concatenate(fsdp_spread(term, fsdp_at), axis=1))
+
+    term_gate = low(contract_rows(normed_all, grad_gate_all))
+    term_up = low(contract_rows(normed_all, grad_up_all))
+    term_down = low(contract_rows(activation_all, cotangent_all))
+    grad_w_gate = spread_columns(term_gate)
+    grad_w_up = spread_columns(term_up)
+    term_down = term_down.reshape(2, unit_half, width)
+    term_down = low(wide(pick(term_down, y_at)) + wide(over_y(pick(term_down, 1 - y_at))))
+    grad_w_down = wide(
+        lax.ppermute(
+            term_down,
+            ("context", "fsdp"),
+            [(c * 4 + f, f * 4 + (c % 2) * 2 + c // 2) for c in range(4) for f in range(4)],
+        )
+    )
+
+    grad_ffn_gain = gain_reduce(jnp.sum(grad_norm_two * normal_two, axis=0), context_at, fsdp_at)
+    grad_hidden = wide(own_cotangent[0]) + norm_backward(
+        grad_norm_two, gain_two, inverse_two, normal_two
+    )
+    hidden_low = plane_gather(low(grad_hidden)).reshape(length, width)
+    term_out = low(contract_rows(attended, hidden_low)).reshape(4, head_cols // 4, width)
+    grad_w_out = ring_reduce([pick(term_out, (fsdp_at - r) % 4) for r in range(4)])
+    grad_attended = low(contract_cols(hidden_low, out_w)).reshape(length, group_size, HEAD)
+    grad_query, grad_key, grad_value = attention_backward(
+        queries, keys, values, grad_attended, logsum, allowed, score_scale
+    )
+    grad_turned = jnp.concatenate([grad_query, grad_key[:, None]], axis=1)
+    grad_heads = low(unrotate(grad_turned, cos_table, sine_table)).reshape(length, head_cols + kv_cols)
+    grad_heads = jnp.concatenate([grad_heads, low(grad_value)], axis=1)
+    grad_norm_one = contract_cols(grad_heads, attn_w)
+    grad_attn_gain = gain_reduce(jnp.sum(grad_norm_one * normal_one, axis=0), context_at, fsdp_at)
+    grad_norm_one = plane_reduce(low(grad_norm_one).reshape(2, 2, 2, rows, width))
+    term_heads = low(contract_rows(normed_one, grad_heads))
+    term_heads = term_heads.reshape(4, 4, width // 16, head_cols + 2 * kv_cols)
+    term_heads = low(ring_reduce([pick(term_heads, (fsdp_at - r) % 4, 1) for r in range(4)]))
+    blocks = [wide(block) for block in context_spread(term_heads, context_at)]
+    grad_w_query = jnp.concatenate([block[:, :head_cols] for block in blocks], axis=1)
+    grad_w_key = jnp.concatenate(
+        [block[:, head_cols : head_cols + kv_cols] for block in blocks], axis=1
+    )
+    grad_w_value = jnp.concatenate([block[:, head_cols + kv_cols :] for block in blocks], axis=1)
+    grad_input = low(
+        grad_hidden
+        + norm_backward(grad_norm_one, gain_one, inverse_one[:rows], normal_one[:rows])
+    )
+    grad_tokens = order_pair(grad_input, over_x(grad_input), tensor_at)
+    return (
+        output,
+        grad_tokens.reshape(1, block_rows, width),
+        grad_attn_gain,
+        grad_w_query,
+        grad_w_key,
+        grad_w_value,
+        grad_w_out,
+        grad_ffn_gain,
+        grad_w_gate,
+        grad_w_up,
+        grad_w_down,
+    )
+
+
 def solution(mesh):
+    sizes = tuple(mesh.shape[a] for a in ("tensor", "context", "fsdp"))
     return jax.shard_map(
-        per_device,
+        per_device_moved if sizes == (2, 4, 4) else per_device_general,
         mesh=mesh,
         in_specs=(
             P("fsdp", "context", None),

time: 2930 us -> 722 us (0.25)
  waiting for transfers between devices: 2570 us -> 312 us
  starting transfers between devices: 1.82 us -> 137 us
  matrix products: 192 us -> 88 us
  blocking collectives: 87 us -> 0 us
  other arithmetic: 26.4 us -> 96 us
  local copies, waits for them, and re-layouts: 25.3 us -> 80.9 us
    reduce_scatter x9 -> x0, waiting for transfers between devices: 1350 us -> none  [the longest x1 337 us: per_device(): lax.psum_scatter(term_down, ('context', 'fsdp'), scatter_dimension=0, til...]
    all_gather x9 -> x0, waiting for transfers between devices: 1080 us -> none  [the longest x1 285 us: per_device(): lax.all_gather(w_up, 'fsdp', axis=0, tiled=True)]
    ppermute x0 -> x108, waiting for transfers between devices: none -> 312 us  [the longest x33 145 us: shift_z(): return lax.ppermute(block, 'fsdp', [(i, (i + step) % 4) for i in range(4)])]
    ppermute x0 -> x108, starting transfers between devices: none -> 137 us  [the longest x33 55.3 us: shift_z(): return lax.ppermute(block, 'fsdp', [(i, (i + step) % 4) for i in range(4)])]
    psum x4 -> x0, waiting for transfers between devices: 136 us -> none  [the longest x1 48.4 us: per_device(): grad_norm_two = lax.psum(grad_norm_two, 'tensor')]
    unnamed x1 -> x0, blocking collectives: 61.3 us -> none
    dot_general x7 -> x5, matrix products: 70.9 us -> 26.2 us  [contract_rows(): lax.dot_general(left, right, (((0,), (0,)), ((), ())), preferred_element_...]
    dot_general x13 -> x20, matrix products: 75.4 us -> 35.1 us  [the longest x4 8.95 us: per_device_moved(): jnp.dot(activation, down_w, preferred_element_type=jnp.float32)]
  transfers between devices with their start and end apart: 22 -> 108, of which waited for: 20 -> 47; matrix products, arithmetic and copies ran while one was open for 6% -> 31% of each run, Pallas kernels for 0% -> 0%
where the time goes in v1:
time: 722 us; the launch traced here: 717 us
  waiting for transfers between devices  312 us (43%)
  starting transfers between devices  137 us (19%)
  other arithmetic  96 us (13%)
  matrix products  88 us (12%)
  local copies, waits for them, and re-layouts  80.9 us (11%)
    ppermute x33, waiting for transfers between devices, shift_z(): return lax.ppermute(block, 'fsdp', [(i, (i + step) % 4) for i in range(4)])  145 us
    ppermute x25, waiting for transfers between devices, over_x(): return lax.ppermute(block, 'tensor', [(0, 1), (1, 0)])  89.9 us
    ppermute x16, waiting for transfers between devices, over_y(): return lax.ppermute(block, 'context', [(i, i ^ 2) for i in range(4)])  66.9 us
    ppermute x33, starting transfers between devices, shift_z(): return lax.ppermute(block, 'fsdp', [(i, (i + step) % 4) for i in range(4)])  55.3 us
    ppermute x25, starting transfers between devices, over_x(): return lax.ppermute(block, 'tensor', [(0, 1), (1, 0)])  32.6 us
    ppermute x16, starting transfers between devices, over_y(): return lax.ppermute(block, 'context', [(i, i ^ 2) for i in range(4)])  27.4 us
    unnamed x206, local copies, waits for them, and re-layouts  26.9 us
    dot_general x14, matrix products, contract_cols(): lax.dot_general(left, right, (((1,), (1,)), ((), ())), preferred_element_...  26.7 us
  transfers between devices with their start and end apart: 108, of which 47 were waited for; matrix products, arithmetic and copies ran while one was open for 31% of the time, Pallas kernels for 0%

profile of v1, /device:TPU:0, one launch (start us, length us, event | category | flops | bytes accessed | tf_op | source)
XLA Modules:
  0.0 717.1 jit_solution(7509177754977345957)
XLA Ops:
  47.1 16.6 %collective-permute-done.9 = bf16[256,512]{1,0:T(8,128)(2,1)S(1)} collective-permute-done((bf16[256,512]{1,0:T(8,128)(2,1)}, bf16[256,512]{1,0:T(8,128)(2,1)S(1)}, u32[]{:S(2)}, u32[]{:S(2)}) %collective-permute-start.9) | collective-permute-done | bytes 262176 | tf_op jit(solution)/shard_map/ppermute | solution.py:354
  74.0 16.2 %collective-permute-done.22 = bf16[2,512,256]{2,1,0:T(8,128)(2,1)S(1)} collective-permute-done((bf16[2,512,256]{2,1,0:T(8,128)(2,1)}, bf16[2,512,256]{2,1,0:T(8,128)(2,1)S(1)}, u32[]{:S(2)}, u32[]{:S(2)}) %collective-permute-start.22) | collective-permute-done | bytes 524320 | tf_op jit(solution)/shard_map/ppermute | solution.py:354
  91.1 10.6 %collective-permute-done.23 = bf16[2,512,256]{2,1,0:T(8,128)(2,1)S(1)} collective-permute-done((bf16[2,512,256]{2,1,0:T(8,128)(2,1)}, bf16[2,512,256]{2,1,0:T(8,128)(2,1)S(1)}, u32[]{:S(2)}, u32[]{:S(2)}) %collective-permute-start.23) | collective-permute-done | bytes 524320 | tf_op jit(solution)/shard_map/ppermute | solution.py:354
  103.7 21.8 %collective-permute-start.4 = (bf16[528,512]{1,0:T(8,128)(2,1)S(1)}, bf16[528,512]{1,0:T(8,128)(2,1)S(1)}, u32[]{:S(2)}, u32[]{:S(2)}) collective-permute-start(bf16[528,512]{1,0:T(8,128)(2,1)S(1)} %collective-permute-done.3), channel_id=1, source_target_pairs={{0,1},{1,2},{2,3},{3,0},{4,5},{5,6},{6,7},{7,4},{8,9},{9,10},{10,1... | collective-permute-start | bytes 1622024 | tf_op jit(solution)/shard_map/ppermute | solution.py:354
  137.1 11.9 %collective-permute-done.51 = bf16[128,2048]{1,0:T(8,128)(2,1)} collective-permute-done((bf16[128,2048]{1,0:T(8,128)(2,1)}, bf16[128,2048]{1,0:T(8,128)(2,1)}, u32[]{:S(2)}, u32[]{:S(2)}) %collective-permute-start.51) | collective-permute-done | bytes 524320 | tf_op jit(solution)/shard_map/ppermute | solution.py:354
  188.0 9.2 %collective-permute-done.58 = bf16[128,2048]{1,0:T(8,128)(2,1)S(1)} collective-permute-done((bf16[128,2048]{1,0:T(8,128)(2,1)}, bf16[128,2048]{1,0:T(8,128)(2,1)S(1)}, u32[]{:S(2)}, u32[]{:S(2)}) %collective-permute-start.58) | collective-permute-done | bytes 524320 | tf_op jit(solution)/shard_map/ppermute | solution.py:350
  206.1 12.2 %collective-permute-start.14 = (bf16[2,128,1024]{2,1,0:T(8,128)(2,1)S(1)}, bf16[2,128,1024]{2,1,0:T(8,128)(2,1)S(1)}, u32[]{:S(2)}, u32[]{:S(2)}) collective-permute-start(bf16[2,128,1024]{2,1,0:T(8,128)(2,1)S(1)} %slice_bitcast_fusion.27), channel_id=1, source_target_pairs={{0,16},{16,0},{1,17},{17,1},{2,18},{18,2},{3,19},{19,3},{4,20},{20... | collective-permute-start | bytes 1572872 | tf_op jit(solution)/shard_map/ppermute | solution.py:350
  218.9 12.5 %collective-permute-done.14 = bf16[2,128,1024]{2,1,0:T(8,128)(2,1)S(1)} collective-permute-done((bf16[2,128,1024]{2,1,0:T(8,128)(2,1)S(1)}, bf16[2,128,1024]{2,1,0:T(8,128)(2,1)S(1)}, u32[]{:S(2)}, u32[]{:S(2)}) %collective-permute-start.14) | collective-permute-done | bytes 524320 | tf_op jit(solution)/shard_map/ppermute | solution.py:350
  243.4 10.2 %collective-permute-done.40 = bf16[128,2048]{1,0:T(8,128)(2,1)S(1)} collective-permute-done((bf16[128,2048]{1,0:T(8,128)(2,1)S(1)}, bf16[128,2048]{1,0:T(8,128)(2,1)S(1)}, u32[]{:S(2)}, u32[]{:S(2)}) %collective-permute-start.40) | collective-permute-done | bytes 524320 | tf_op jit(solution)/shard_map/ppermute | solution.py:350
  258.8 10.7 %collective-permute-done.19 = bf16[128,2048]{1,0:T(8,128)(2,1)S(1)} collective-permute-done((bf16[128,2048]{1,0:T(8,128)(2,1)S(1)}, bf16[128,2048]{1,0:T(8,128)(2,1)S(1)}, u32[]{:S(2)}, u32[]{:S(2)}) %collective-permute-start.19) | collective-permute-done | bytes 524320 | tf_op jit(solution)/shard_map/ppermute | solution.py:350
  338.9 7.6 %convolution_convert_fusion.2 = bf16[2048,512]{1,0:T(8,128)(2,1)} fusion(bf16[512,512]{1,0:T(8,128)(2,1)} %get-tuple-element.68, bf16[512,512]{1,0:T(8,128)(2,1)S(1)} %copy-done.70, bf16[512,512]{1,0:T(8,128)(2,1)S(1)} %copy-done.68, bf16[512,512]{1,0:T(8,128)(2,1)S(1)} %copy-done.66, bf16[512,2048]{1,0:T(8,128)(2,1)} %bitcast.664, ...), kind=kOutput, calls=%fused_computation.45 | convolution fusion | flops 4337958912 | bytes 12582912 | tf_op jit(solution)/shard_map/dot_general | solution.py:51
  371.6 27.1 %collective-permute-done.96 = bf16[2,4,128,512]{3,2,1,0:T(8,128)(2,1)S(1)} collective-permute-done((bf16[2,4,128,512]{3,2,1,0:T(8,128)(2,1)S(1)}, bf16[2,4,128,512]{3,2,1,0:T(8,128)(2,1)S(1)}, u32[]{:S(2)}, u32[]{:S(2)}) %collective-permute-start.96) | collective-permute-done | bytes 1048608 | tf_op jit(solution)/shard_map/ppermute | solution.py:342
  399.7 20.0 %collective-permute-done.101 = bf16[2,4,128,512]{3,2,1,0:T(8,128)(2,1)S(1)} collective-permute-done((bf16[2,4,128,512]{3,2,1,0:T(8,128)(2,1)S(1)}, bf16[2,4,128,512]{3,2,1,0:T(8,128)(2,1)S(1)}, u32[]{:S(2)}, u32[]{:S(2)}) %collective-permute-start.101) | collective-permute-done | bytes 1048608 | tf_op jit(solution)/shard_map/ppermute | solution.py:342
  427.7 8.6 %collective-permute-done.27 = bf16[128,2048]{1,0:T(8,128)(2,1)S(1)} collective-permute-done((bf16[128,2048]{1,0:T(8,128)(2,1)S(1)}, bf16[128,2048]{1,0:T(8,128)(2,1)S(1)}, u32[]{:S(2)}, u32[]{:S(2)}) %collective-permute-start.27) | collective-permute-done | bytes 524320 | tf_op jit(solution)/shard_map/ppermute | solution.py:354
  438.0 7.1 collective-permute-done.50
  482.8 20.9 %collective-permute-done.99 = bf16[128,1024]{0,1:T(8,128)(2,1)} collective-permute-done((bf16[128,1024]{0,1:T(8,128)(2,1)}, bf16[128,1024]{0,1:T(8,128)(2,1)}, u32[]{:S(2)}, u32[]{:S(2)}) %collective-permute-start.99) | collective-permute-done | bytes 262176 | tf_op jit(solution)/shard_map/ppermute | solution.py:354
  534.7 9.4 %collective-permute-start.107 = (bf16[256,2048]{1,0:T(8,128)(2,1)}, bf16[256,2048]{1,0:T(8,128)(2,1)}, u32[]{:S(2)}, u32[]{:S(2)}) collective-permute-start(bf16[256,2048]{1,0:T(8,128)(2,1)} %fusion.46), channel_id=1, source_target_pairs={{0,0},{1,4},{2,8},{3,12},{4,2},{5,6},{6,10},{7,14},{8,1},{9,5},{10... | collective-permute-start | bytes 3145736 | tf_op jit(solution)/shard_map/ppermute | solution.py:644
  545.3 7.1 collective-permute-start.93
  552.4 11.5 %collective-permute-done.67 = bf16[2,128,1024]{2,1,0:T(8,128)(2,1)S(1)} collective-permute-done((bf16[2,128,1024]{2,1,0:T(8,128)(2,1)S(1)}, bf16[2,128,1024]{2,1,0:T(8,128)(2,1)S(1)}, u32[]{:S(2)}, u32[]{:S(2)}) %collective-permute-start.67) | collective-permute-done | bytes 524320 | tf_op jit(solution)/shard_map/ppermute | solution.py:342
  626.2 7.6 %collective-permute-done.80 = f32[2,128]{1,0:T(2,128)S(1)} collective-permute-done((f32[2,128]{1,0:T(2,128)S(1)}, f32[2,128]{1,0:T(2,128)S(1)}, u32[]{:S(2)}, u32[]{:S(2)}) %collective-permute-start.80) | collective-permute-done | bytes 1056 | tf_op jit(solution)/shard_map/ppermute | solution.py:358
  640.5 13.9 %collective-permute-done.83 = bf16[4,128,512]{2,1,0:T(8,128)(2,1)S(1)} collective-permute-done((bf16[4,128,512]{2,1,0:T(8,128)(2,1)S(1)}, bf16[4,128,512]{2,1,0:T(8,128)(2,1)S(1)}, u32[]{:S(2)}, u32[]{:S(2)}) %collective-permute-start.83) | collective-permute-done | bytes 524320 | tf_op jit(solution)/shard_map/ppermute | solution.py:354
  660.4 10.9 %collective-permute-done.84 = bf16[4,128,512]{2,1,0:T(8,128)(2,1)S(1)} collective-permute-done((bf16[4,128,512]{2,1,0:T(8,128)(2,1)S(1)}, bf16[4,128,512]{2,1,0:T(8,128)(2,1)S(1)}, u32[]{:S(2)}, u32[]{:S(2)}) %collective-permute-start.84) | collective-permute-done | bytes 524320 | tf_op jit(solution)/shard_map/ppermute | solution.py:354
  682.3 11.3 %collective-permute-done.72 = bf16[2,128,1024]{2,1,0:T(8,128)(2,1)S(1)} collective-permute-done((bf16[2,128,1024]{2,1,0:T(8,128)(2,1)S(1)}, bf16[2,128,1024]{2,1,0:T(8,128)(2,1)S(1)}, u32[]{:S(2)}, u32[]{:S(2)}) %collective-permute-start.72) | collective-permute-done | bytes 524320 | tf_op jit(solution)/shard_map/ppermute | solution.py:350
  707.2 8.6 %collective-permute-done.76 = bf16[128,2048]{1,0:T(8,128)(2,1)S(1)} collective-permute-done((bf16[128,2048]{1,0:T(8,128)(2,1)S(1)}, bf16[128,2048]{1,0:T(8,128)(2,1)S(1)}, u32[]{:S(2)}, u32[]{:S(2)}) %collective-permute-start.76) | collective-permute-done | bytes 524320 | tf_op jit(solution)/shard_map/ppermute | solution.py:350
  (662 shorter events, 410.2 us)
Async XLA Ops:
  2.2 38.5 %collective-permute-start.5 = (s32[2,128]{1,0:T(2,128)S(1)}, s32[2,128]{1,0:T(2,128)S(1)}, u32[]{:S(2)}, u32[]{:S(2)}) collective-permute-start(s32[2,128]{1,0:T(2,128)S(1)} %broadcast_select_fusion.2), channel_id=1, source_target_pairs={{0,8},{4,12},{8,0},{12,4},{1,9},{5,13},{9,1},{13,5},{2,10},{6,14},... | collective-permute-start | bytes 3080 | tf_op jit(solution)/shard_map/ppermute | solution.py:342
  11.9 57.0 %collective-permute-start.2 = (bf16[528,512]{1,0:T(8,128)(2,1)}, bf16[528,512]{1,0:T(8,128)(2,1)}, u32[]{:S(2)}, u32[]{:S(2)}) collective-permute-start(bf16[528,512]{1,0:T(8,128)(2,1)} %get-tuple-element.160), channel_id=1, source_target_pairs={{0,1},{1,2},{2,3},{3,0},{4,5},{5,6},{6,7},{7,4},{8,9},{9,10},{10,1... | collective-permute-start | bytes 1622024 | tf_op jit(solution)/shard_map/ppermute | solution.py:354
  16.6 52.1 %collective-permute-start.45 = (bf16[128,2048]{1,0:T(8,128)(2,1)}, bf16[128,2048]{1,0:T(8,128)(2,1)}, u32[]{:S(2)}, u32[]{:S(2)}) collective-permute-start(bf16[128,2048]{1,0:T(8,128)(2,1)} %slice_bitcast_fusion.16), channel_id=1, source_target_pairs={{0,1},{1,2},{2,3},{3,0},{4,5},{5,6},{6,7},{7,4},{8,9},{9,10},{10,1... | collective-permute-start | bytes 1572872 | tf_op jit(solution)/shard_map/ppermute | solution.py:354
  19.4 46.4 %collective-permute-start = (bf16[2,128,2048]{2,1,0:T(8,128)(2,1)}, bf16[2,128,2048]{2,1,0:T(8,128)(2,1)}, u32[]{:S(2)}, u32[]{:S(2)}) collective-permute-start(bf16[2,128,2048]{2,1,0:T(8,128)(2,1)} %reverse_select_fusion.1), channel_id=1, source_target_pairs={{0,8},{4,12},{8,0},{12,4},{1,9},{5,13},{9,1},{13,5},{2,10},{6,14},... | collective-permute-start | bytes 3145736 | tf_op jit(solution)/shard_map/ppermute | solution.py:342
  68.7 84.8 %collective-permute-start.1 = (bf16[2,2,128,2048]{3,2,1,0:T(8,128)(2,1)S(1)}, bf16[2,2,128,2048]{3,2,1,0:T(8,128)(2,1)S(1)}, u32[]{:S(2)}, u32[]{:S(2)}) collective-permute-start(bf16[2,2,128,2048]{3,2,1,0:T(8,128)(2,1)S(1)} %get-tuple-element.103), channel_id=1, source_target_pairs={{0,4},{4,0},{8,12},{12,8},{1,5},{5,1},{9,13},{13,9},{2,6},{6,2},{1... | collective-permute-start | bytes 6291464 | tf_op jit(solution)/shard_map/ppermute | solution.py:338
  90.2 42.8 %collective-permute-start.46 = (bf16[128,2048]{1,0:T(8,128)(2,1)}, bf16[128,2048]{1,0:T(8,128)(2,1)S(1)}, u32[]{:S(2)}, u32[]{:S(2)}) collective-permute-start(bf16[128,2048]{1,0:T(8,128)(2,1)} %collective-permute-done.45), channel_id=1, source_target_pairs={{0,16},{16,0},{1,17},{17,1},{2,18},{18,2},{3,19},{19,3},{4,20},{20... | collective-permute-start | bytes 1572872 | tf_op jit(solution)/shard_map/ppermute | solution.py:350
  103.7 45.3 %collective-permute-start.4 = (bf16[528,512]{1,0:T(8,128)(2,1)S(1)}, bf16[528,512]{1,0:T(8,128)(2,1)S(1)}, u32[]{:S(2)}, u32[]{:S(2)}) collective-permute-start(bf16[528,512]{1,0:T(8,128)(2,1)S(1)} %collective-permute-done.3), channel_id=1, source_target_pairs={{0,1},{1,2},{2,3},{3,0},{4,5},{5,6},{6,7},{7,4},{8,9},{9,10},{10,1... | collective-permute-start | bytes 1622024 | tf_op jit(solution)/shard_map/ppermute | solution.py:354
  127.2 54.2 %collective-permute-start.63 = (bf16[2,128,2048]{2,1,0:T(8,128)(2,1)}, bf16[2,128,2048]{2,1,0:T(8,128)(2,1)}, u32[]{:S(2)}, u32[]{:S(2)}) collective-permute-start(bf16[2,128,2048]{2,1,0:T(8,128)(2,1)} %reverse_select_fusion), channel_id=1, source_target_pairs={{0,4},{4,0},{8,12},{12,8},{1,5},{5,1},{9,13},{13,9},{2,6},{6,2},{1... | collective-permute-start | bytes 3145736 | tf_op jit(solution)/shard_map/ppermute | solution.py:338
  133.0 67.0 %collective-permute-start.24 = (bf16[2,2048,256]{2,1,0:T(8,128)(2,1)}, bf16[2,2048,256]{2,1,0:T(8,128)(2,1)}, u32[]{:S(2)}, u32[]{:S(2)}) collective-permute-start(bf16[2,2048,256]{2,1,0:T(8,128)(2,1)} %bitcast.81), channel_id=1, source_target_pairs={{0,8},{4,12},{8,0},{12,4},{1,9},{5,13},{9,1},{13,5},{2,10},{6,14},... | collective-permute-start | bytes 6291464 | tf_op jit(solution)/shard_map/ppermute | solution.py:342
  149.0 49.5 %collective-permute-start.47 = (bf16[2,128,2048]{2,1,0:T(8,128)(2,1)}, bf16[2,128,2048]{2,1,0:T(8,128)(2,1)}, u32[]{:S(2)}, u32[]{:S(2)}) collective-permute-start(bf16[2,128,2048]{2,1,0:T(8,128)(2,1)} %get-tuple-element.136), channel_id=1, source_target_pairs={{0,4},{4,0},{8,12},{12,8},{1,5},{5,1},{9,13},{13,9},{2,6},{6,2},{1... | collective-permute-start | bytes 3145736 | tf_op jit(solution)/shard_map/ppermute | solution.py:338
  187.7 66.0 %collective-permute-start.53 = (bf16[2,128,2048]{2,1,0:T(8,128)(2,1)S(1)}, bf16[2,128,2048]{2,1,0:T(8,128)(2,1)}, u32[]{:S(2)}, u32[]{:S(2)}) collective-permute-start(bf16[2,128,2048]{2,1,0:T(8,128)(2,1)S(1)} %get-tuple-element.134), channel_id=1, source_target_pairs={{0,4},{4,0},{8,12},{12,8},{1,5},{5,1},{9,13},{13,9},{2,6},{6,2},{1... | collective-permute-start | bytes 3145736 | tf_op jit(solution)/shard_map/ppermute | solution.py:338
  198.5 60.2 %collective-permute-start.59 = (bf16[2,128,2048]{2,1,0:T(8,128)(2,1)S(1)}, bf16[2,128,2048]{2,1,0:T(8,128)(2,1)S(1)}, u32[]{:S(2)}, u32[]{:S(2)}) collective-permute-start(bf16[2,128,2048]{2,1,0:T(8,128)(2,1)S(1)} %get-tuple-element.132), channel_id=1, source_target_pairs={{0,4},{4,0},{8,12},{12,8},{1,5},{5,1},{9,13},{13,9},{2,6},{6,2},{1... | collective-permute-start | bytes 3145736 | tf_op jit(solution)/shard_map/ppermute | solution.py:338
  311.0 53.6 %collective-permute-start.31 = (bf16[2,128,2048]{2,1,0:T(8,128)(2,1)}, bf16[2,128,2048]{2,1,0:T(8,128)(2,1)}, u32[]{:S(2)}, u32[]{:S(2)}) collective-permute-start(bf16[2,128,2048]{2,1,0:T(8,128)(2,1)} %bitcast.98), channel_id=1, source_target_pairs={{0,4},{4,0},{8,12},{12,8},{1,5},{5,1},{9,13},{13,9},{2,6},{6,2},{1... | collective-permute-start | bytes 3145736 | tf_op jit(solution)/shard_map/ppermute | solution.py:338
  314.8 52.7 %collective-permute-start.54 = (bf16[2,128,2048]{2,1,0:T(8,128)(2,1)}, bf16[2,128,2048]{2,1,0:T(8,128)(2,1)}, u32[]{:S(2)}, u32[]{:S(2)}) collective-permute-start(bf16[2,128,2048]{2,1,0:T(8,128)(2,1)} %bitcast.139), channel_id=1, source_target_pairs={{0,4},{4,0},{8,12},{12,8},{1,5},{5,1},{9,13},{13,9},{2,6},{6,2},{1... | collective-permute-start | bytes 3145736 | tf_op jit(solution)/shard_map/ppermute | solution.py:338
  316.5 46.8 %collective-permute-start.26 = (bf16[128,2048]{1,0:T(8,128)(2,1)}, bf16[128,2048]{1,0:T(8,128)(2,1)}, u32[]{:S(2)}, u32[]{:S(2)}) collective-permute-start(bf16[128,2048]{1,0:T(8,128)(2,1)} %slice_bitcast_fusion.23), channel_id=1, source_target_pairs={{0,16},{16,0},{1,17},{17,1},{2,18},{18,2},{3,19},{19,3},{4,20},{20... | collective-permute-start | bytes 1572872 | tf_op jit(solution)/shard_map/ppermute | solution.py:350
  318.4 51.8 %collective-permute-start.49 = (bf16[128,2048]{1,0:T(8,128)(2,1)}, bf16[128,2048]{1,0:T(8,128)(2,1)}, u32[]{:S(2)}, u32[]{:S(2)}) collective-permute-start(bf16[128,2048]{1,0:T(8,128)(2,1)} %slice_bitcast_fusion.14), channel_id=1, source_target_pairs={{0,16},{16,0},{1,17},{17,1},{2,18},{18,2},{3,19},{19,3},{4,20},{20... | collective-permute-start | bytes 1572872 | tf_op jit(solution)/shard_map/ppermute | solution.py:350
  350.0 70.0 %collective-permute-start.106 = (bf16[256,2048]{1,0:T(8,128)(2,1)}, bf16[256,2048]{1,0:T(8,128)(2,1)}, u32[]{:S(2)}, u32[]{:S(2)}) collective-permute-start(bf16[256,2048]{1,0:T(8,128)(2,1)} %dynamic-slice_bitcast_fusion), channel_id=1, source_target_pairs={{0,8},{4,12},{8,0},{12,4},{1,9},{5,13},{9,1},{13,5},{2,10},{6,14},... | collective-permute-start | bytes 3145736 | tf_op jit(solution)/shard_map/ppermute | solution.py:342
  363.5 60.8 %collective-permute-start.37 = (bf16[2,128,2048]{2,1,0:T(8,128)(2,1)S(1)}, bf16[2,128,2048]{2,1,0:T(8,128)(2,1)S(1)}, u32[]{:S(2)}, u32[]{:S(2)}) collective-permute-start(bf16[2,128,2048]{2,1,0:T(8,128)(2,1)S(1)} %bitcast.683), channel_id=1, source_target_pairs={{0,4},{4,0},{8,12},{12,8},{1,5},{5,1},{9,13},{13,9},{2,6},{6,2},{1... | collective-permute-start | bytes 3145736 | tf_op jit(solution)/shard_map/ppermute | solution.py:338
  367.6 52.1 %collective-permute-start.101 = (bf16[2,4,128,512]{3,2,1,0:T(8,128)(2,1)S(1)}, bf16[2,4,128,512]{3,2,1,0:T(8,128)(2,1)S(1)}, u32[]{:S(2)}, u32[]{:S(2)}) collective-permute-start(bf16[2,4,128,512]{3,2,1,0:T(8,128)(2,1)S(1)} %dynamic-slice_bitcast_fusion.1), channel_id=1, source_target_pairs={{0,8},{4,12},{8,0},{12,4},{1,9},{5,13},{9,1},{13,5},{2,10},{6,14},... | collective-permute-start | bytes 3145736 | tf_op jit(solution)/shard_map/ppermute | solution.py:342
  370.2 76.0 %collective-permute-start.60 = (bf16[2,128,2048]{2,1,0:T(8,128)(2,1)S(1)}, bf16[2,128,2048]{2,1,0:T(8,128)(2,1)S(1)}, u32[]{:S(2)}, u32[]{:S(2)}) collective-permute-start(bf16[2,128,2048]{2,1,0:T(8,128)(2,1)S(1)} %bitcast.682), channel_id=1, source_target_pairs={{0,4},{4,0},{8,12},{12,8},{1,5},{5,1},{9,13},{13,9},{2,6},{6,2},{1... | collective-permute-start | bytes 3145736 | tf_op jit(solution)/shard_map/ppermute | solution.py:338
  426.5 89.8 %collective-permute-start.65 = (bf16[128,2048]{1,0:T(8,128)(2,1)}, bf16[128,2048]{1,0:T(8,128)(2,1)}, u32[]{:S(2)}, u32[]{:S(2)}) collective-permute-start(bf16[128,2048]{1,0:T(8,128)(2,1)} %slice_bitcast_fusion.8), channel_id=1, source_target_pairs={{0,16},{16,0},{1,17},{17,1},{2,18},{18,2},{3,19},{19,3},{4,20},{20... | collective-permute-start | bytes 1572872 | tf_op jit(solution)/shard_map/ppermute | solution.py:350
  475.7 40.7 %collective-permute-start.62 = (bf16[128,2048]{1,0:T(8,128)(2,1)}, bf16[128,2048]{1,0:T(8,128)(2,1)}, u32[]{:S(2)}, u32[]{:S(2)}) collective-permute-start(bf16[128,2048]{1,0:T(8,128)(2,1)} %add_convert_fusion.5), channel_id=1, source_target_pairs={{0,1},{1,2},{2,3},{3,0},{4,5},{5,6},{6,7},{7,4},{8,9},{9,10},{10,1... | collective-permute-start | bytes 1572872 | tf_op jit(solution)/shard_map/ppermute | solution.py:354
  534.7 40.6 %collective-permute-start.107 = (bf16[256,2048]{1,0:T(8,128)(2,1)}, bf16[256,2048]{1,0:T(8,128)(2,1)}, u32[]{:S(2)}, u32[]{:S(2)}) collective-permute-start(bf16[256,2048]{1,0:T(8,128)(2,1)} %fusion.46), channel_id=1, source_target_pairs={{0,0},{1,4},{2,8},{3,12},{4,2},{5,6},{6,10},{7,14},{8,1},{9,5},{10... | collective-permute-start | bytes 3145736 | tf_op jit(solution)/shard_map/ppermute | solution.py:644
  626.1 51.9 %collective-permute-start.71 = (bf16[2,2,128,2048]{3,2,1,0:T(8,128)(2,1)S(1)}, bf16[2,2,128,2048]{3,2,1,0:T(8,128)(2,1)S(1)}, u32[]{:S(2)}, u32[]{:S(2)}) collective-permute-start(bf16[2,2,128,2048]{3,2,1,0:T(8,128)(2,1)S(1)} %bitcast.666), channel_id=1, source_target_pairs={{0,4},{4,0},{8,12},{12,8},{1,5},{5,1},{9,13},{13,9},{2,6},{6,2},{1... | collective-permute-start | bytes 6291464 | tf_op jit(solution)/shard_map/ppermute | solution.py:338
  (186 other events, 2574.4 us)

commit v2 on v0

--- a/solution.py
+++ b/solution.py
@@ -1,11 +1,16 @@
+import functools
 import math
 
 import jax
 import jax.numpy as jnp
 from jax import lax
+from jax.experimental import pallas as pl
+from jax.experimental.pallas import tpu as pltpu
 from jax.sharding import PartitionSpec as P
 
 HEAD = 128
+PARTS = 2
+NO_COST = pl.CostEstimate(flops=1, bytes_accessed=1, transcendentals=0)
 
 
 norm_epsilon = 1e-05
@@ -154,7 +159,7 @@
     return (grad_query.reshape(queries.shape), grad_key, grad_value)
 
 
-def per_device(
+def per_device_general(
     tokens,
     segments,
     positions,
@@ -325,9 +330,739 @@
     )
 
 
+def low(values):
+    return values.astype(jnp.bfloat16)
+
+
+def wide(values):
+    return values.astype(jnp.float32)
+
+
+def matmul(left, right):
+    return jnp.dot(left, right, preferred_element_type=jnp.float32)
+
+
+def fence(*arrays):
+    return lax.optimization_barrier(arrays)
+
+
+def place_pair(mine, theirs, index, axis):
+    first = index == 0
+    return jnp.concatenate(
+        [jnp.where(first, mine, theirs), jnp.where(first, theirs, mine)], axis=axis
+    )
+
+
+def cut(block, index, size, axis):
+    return lax.dynamic_slice_in_dim(block, index * size, size, axis=axis)
+
+
+def over_core(block):
+    return lax.ppermute(block, "context", [(i, i ^ 1) for i in range(4)])
+
+
+def over_y(block):
+    return lax.ppermute(block, "context", [(i, i ^ 2) for i in range(4)])
+
+
+def over_diagonal(block):
+    return lax.ppermute(block, "context", [(i, i ^ 3) for i in range(4)])
+
+
+def over_x(block):
+    return lax.ppermute(block, "tensor", [(0, 1), (1, 0)])
+
+
+def shift_z(block, step=1):
+    return lax.ppermute(block, "fsdp", [(i, (i + step) % 4) for i in range(4)])
+
+
+def exchange_z(block, distance):
+    return lax.ppermute(block, "fsdp", [(i, i ^ distance) for i in range(4)])
+
+
+def gather_z(block):
+    return lax.all_gather(block, "fsdp", axis=0, tiled=True)
+
+
+def scatter_z(block):
+    return lax.psum_scatter(block, "fsdp", scatter_dimension=0, tiled=True)
+
+
+def gain_start(term):
+    return term, over_x(term)
+
+
+def gain_next(term, got, index, exchange, axis=0):
+    term = term + got
+    kept = lax.dynamic_index_in_dim(term, index, axis, keepdims=False)
+    return kept, exchange(lax.dynamic_index_in_dim(term, 1 - index, axis, keepdims=False))
+
+
+def flat(pieces):
+    return [block for piece in pieces for block in piece]
+
+
+def context_send(blocks, context_at):
+    size = blocks.shape[0] // 4
+    return (
+        cut(blocks, context_at, size, 0),
+        over_core(cut(blocks, context_at ^ 1, size, 0)),
+        over_y(cut(blocks, context_at ^ 2, size, 0)),
+        over_diagonal(cut(blocks, context_at ^ 3, size, 0)),
+    )
+
+
+def context_order(got, context_at):
+    got = jnp.stack(got)
+    return [lax.dynamic_index_in_dim(got, i ^ context_at, 0, keepdims=False) for i in range(4)]
+
+
+def dot_dims(left, right, left_dim, right_dim):
+    return lax.dot_general(
+        left, right, (((left_dim,), (right_dim,)), ((), ())), preferred_element_type=jnp.float32
+    )
+
+
+def attend_kernel(
+    scale, block, raw_ref, cos_ref, sine_ref, tag_ref, tag_row_ref, turned_ref, out_ref, sum_ref
+):
+    length = raw_ref.shape[0]
+    heads = out_ref.shape[1] // HEAD
+
+    def turn(rows, cols):
+        part = raw_ref[rows, cols]
+        return low(part * cos_ref[rows, :] + pltpu.roll(part, HEAD // 2, 1) * sine_ref[rows, :])
+
+    everything = slice(0, length)
+    key_cols = slice(heads * HEAD, (heads + 1) * HEAD)
+    value_cols = slice((heads + 1) * HEAD, (heads + 2) * HEAD)
+    keys = turn(everything, key_cols)
+    values = low(raw_ref[:, value_cols])
+    turned_ref[:, key_cols] = keys
+    turned_ref[:, value_cols] = values
+    for start in range(0, length, block):
+        rows = slice(start, start + block)
+        allowed = (tag_ref[rows, 0:1] == tag_row_ref[0:1, :]) & (
+            tag_ref[rows, 1:2] >= tag_row_ref[1:2, :]
+        )
+        for head in range(heads):
+            cols = slice(head * HEAD, (head + 1) * HEAD)
+            queries = turn(rows, cols)
+            turned_ref[rows, cols] = queries
+            scores = jnp.where(allowed, dot_dims(queries, keys, 1, 1) * scale, -1e30)
+            highest = jnp.max(scores, axis=-1, keepdims=True)
+            weights = jnp.exp(scores - highest)
+            row_total = jnp.sum(weights, axis=-1, keepdims=True)
+            probabilities = low(weights * (1.0 / row_total))
+            out_ref[rows, cols] = low(dot_dims(probabilities, values, 1, 0))
+            sum_ref[rows, head : head + 1] = highest + jnp.log(row_total)
+
+
+def attend_back_kernel(
+    scale,
+    block,
+    turned_ref,
+    grad_ref,
+    sum_ref,
+    cos_ref,
+    sine_ref,
+    tag_ref,
+    tag_row_ref,
+    out_ref,
+    key_acc,
+    value_acc,
+):
+    length = turned_ref.shape[0]
+    heads = grad_ref.shape[1] // HEAD
+
+    def turn_back(part, rows):
+        return low(part * cos_ref[rows, :] - pltpu.roll(part, HEAD // 2, 1) * sine_ref[rows, :])
+
+    key_cols = slice(heads * HEAD, (heads + 1) * HEAD)
+    value_cols = slice((heads + 1) * HEAD, (heads + 2) * HEAD)
+    keys, values = turned_ref[:, key_cols], turned_ref[:, value_cols]
+    key_acc[...] = jnp.zeros_like(key_acc)
+    value_acc[...] = jnp.zeros_like(value_acc)
+    for start in range(0, length, block):
+        rows = slice(start, start + block)
+        allowed = (tag_ref[rows, 0:1] == tag_row_ref[0:1, :]) & (
+            tag_ref[rows, 1:2] >= tag_row_ref[1:2, :]
+        )
+        for head in range(heads):
+            cols = slice(head * HEAD, (head + 1) * HEAD)
+            queries, grad = turned_ref[rows, cols], grad_ref[rows, cols]
+            scores = jnp.where(allowed, dot_dims(queries, keys, 1, 1) * scale, -1e30)
+            probabilities = jnp.exp(scores - sum_ref[rows, head : head + 1])
+            grad_probs = dot_dims(grad, values, 1, 1)
+            row_delta = jnp.sum(probabilities * grad_probs, axis=-1, keepdims=True)
+            grad_scores = low(probabilities * (grad_probs - row_delta))
+            out_ref[rows, cols] = turn_back(scale * dot_dims(grad_scores, keys, 1, 0), rows)
+            key_acc[...] += dot_dims(grad_scores, queries, 0, 0)
+            value_acc[...] += dot_dims(low(probabilities), grad, 0, 0)
+    out_ref[:, key_cols] = turn_back(scale * key_acc[...], slice(0, length))
+    out_ref[:, value_cols] = low(value_acc[...])
+
+
+def feed_forward_kernel(*refs):
+    tokens_refs, cotangent_refs, (gate_ref, up_ref, down_ref) = refs[:2], refs[2:4], refs[4:7]
+    activation_ref, gate_grad_ref, up_grad_ref = refs[7:10]
+    norm_refs, part_refs = refs[10:12], refs[12:14]
+    size = tokens_refs[0].shape[0]
+    for i in range(2):
+        rows = slice(i * size, (i + 1) * size)
+        gate_proj = dot_dims(tokens_refs[i][...], gate_ref[...], 1, 0)
+        up_proj = dot_dims(tokens_refs[i][...], up_ref[...], 1, 0)
+        sigmoid_gate = jax.nn.sigmoid(gate_proj)
+        silu_gate = gate_proj * sigmoid_gate
+        activation = low(silu_gate * up_proj)
+        activation_ref[rows, :] = activation
+        part_refs[i][...] = low(dot_dims(activation, down_ref[...], 1, 0))
+        grad_act = dot_dims(cotangent_refs[i][...], down_ref[...], 1, 1)
+        grad_gate = low(
+            grad_act * up_proj * sigmoid_gate * (1.0 + gate_proj * (1.0 - sigmoid_gate))
+        )
+        grad_up = low(grad_act * silu_gate)
+        gate_grad_ref[rows, :] = grad_gate
+        up_grad_ref[rows, :] = grad_up
+        norm_refs[i][...] = low(
+            dot_dims(grad_gate, gate_ref[...], 1, 1) + dot_dims(grad_up, up_ref[...], 1, 1)
+        )
+
+
+def feed_forward_local(tokens, cotangents, gate_w, up_w, down_w):
+    size, width = tokens[0].shape
+    units = gate_w.shape[1]
+    small = jax.ShapeDtypeStruct((2 * size, units), jnp.bfloat16)
+    large = jax.ShapeDtypeStruct((size, width), jnp.bfloat16)
+    return pl.pallas_call(
+        feed_forward_kernel,
+        out_shape=[small] * 3 + [large] * 4,
+        compiler_params=pltpu.CompilerParams(vmem_limit_bytes=48 * 2**20),
+        cost_estimate=NO_COST,
+    )(*tokens, *cotangents, gate_w, up_w, down_w)
+
+
+def weight_kernel(count, *refs):
+    wide_refs, narrow_refs, (out_ref, acc_ref) = refs[:count], refs[count:-2], refs[-2:]
+    size = wide_refs[0].shape[0]
+    each = count // len(narrow_refs)
+    transposed = out_ref.shape[1] == wide_refs[0].shape[1]
+    for i in range(count):
+        first = (i % each) * size
+        narrow = narrow_refs[i // each][first : first + size, :]
+        pair = (narrow, wide_refs[i][...]) if transposed else (wide_refs[i][...], narrow)
+        term = dot_dims(*pair, 0, 0)
+        if i == 0:
+            acc_ref[...] = term
+        else:
+            acc_ref[...] += term
+    out_ref[...] = low(acc_ref[...])
+
+
+def weight_local(wides, narrows, transposed):
+    size, width = wides[0].shape
+    length, units = narrows[0].shape
+    cols = width // 2
+    tile = (units, cols) if transposed else (cols, units)
+    return pl.pallas_call(
+        functools.partial(weight_kernel, len(wides)),
+        grid=(2,),
+        in_specs=[pl.BlockSpec((size, cols), lambda i: (0, i))] * len(wides)
+        + [pl.BlockSpec((length, units), lambda i: (0, 0))] * len(narrows),
+        out_specs=pl.BlockSpec(tile, (lambda i: (0, i)) if transposed else (lambda i: (i, 0))),
+        out_shape=jax.ShapeDtypeStruct(
+            (units, width) if transposed else (width, units), jnp.bfloat16
+        ),
+        scratch_shapes=[pltpu.VMEM(tile, jnp.float32)],
+        compiler_params=pltpu.CompilerParams(vmem_limit_bytes=48 * 2**20),
+        cost_estimate=NO_COST,
+    )(*wides, *narrows)
+
+
+def attend_tables(places, seg, order):
+    cos_table, sine_table = rotary(places)
+    signs = jnp.where(jnp.arange(HEAD) < HEAD // 2, -1.0, 1.0)
+    return cos_table, sine_table * signs, jnp.stack([seg, order], axis=1), jnp.stack([seg, order])
+
+
+def attend_forward_local(raw, tables, heads, score_scale):
+    length = raw.shape[0]
+    return pl.pallas_call(
+        functools.partial(attend_kernel, score_scale, math.gcd(length, 512)),
+        out_shape=[
+            jax.ShapeDtypeStruct(raw.shape, jnp.bfloat16),
+            jax.ShapeDtypeStruct((length, heads * HEAD), jnp.bfloat16),
+            jax.ShapeDtypeStruct((length, heads), jnp.float32),
+        ],
+        compiler_params=pltpu.CompilerParams(vmem_limit_bytes=48 * 2**20),
+        cost_estimate=NO_COST,
+    )(raw, *tables)
+
+
+def attend_backward_local(turned, grad_attended, logsum, tables, heads, score_scale):
+    length = turned.shape[0]
+    return pl.pallas_call(
+        functools.partial(attend_back_kernel, score_scale, math.gcd(length, 512)),
+        out_shape=jax.ShapeDtypeStruct(turned.shape, jnp.bfloat16),
+        scratch_shapes=[pltpu.VMEM((length, HEAD), jnp.float32)] * 2,
+        compiler_params=pltpu.CompilerParams(vmem_limit_bytes=48 * 2**20),
+        cost_estimate=NO_COST,
+    )(turned, grad_attended, logsum, *tables)
+
+
+def per_device_moved(
+    tokens,
+    segments,
+    positions,
+    attn_gain,
+    w_query,
+    w_key,
+    w_value,
+    w_out,
+    ffn_gain,
+    w_gate,
+    w_up,
+    w_down,
+    cotangent,
+):
+    tensor_at, context_at, fsdp_at = (lax.axis_index(a) for a in ("tensor", "context", "fsdp"))
+    y_at, core_at = context_at // 2, context_at % 2
+    places = [(fsdp_at - r) % 4 for r in range(4)]
+    width = tokens.shape[2]
+    block_rows = tokens.shape[1]
+    rows = block_rows // 2
+    length = segments.shape[1]
+    score_scale = 1.0 / math.sqrt(HEAD)
+    shard = attn_gain.shape[0]
+    head_cols = w_query.shape[1] // 4
+    kv_cols = w_key.shape[1] // 4
+    heads = head_cols // HEAD
+    all_cols = head_cols + 2 * kv_cols
+    unit_half = w_gate.shape[1] // 16
+    units = 2 * unit_half
+
+    half_width = width // 2
+
+    def split_x(block):
+        first, second = block[:rows], block[rows:]
+        return jnp.concatenate(
+            [
+                jnp.where(tensor_at == 0, first, second),
+                jnp.where(tensor_at == 0, second, first),
+            ]
+        )
+
+    def spread_context(block):
+        pair = jnp.concatenate([block, over_y(block)])
+        return jnp.concatenate([pair, over_core(pair)])
+
+    own_cotangent = split_x(cotangent[0])
+    part = rows // PARTS
+    gains = jnp.concatenate([attn_gain, ffn_gain]).reshape(-1, all_cols)
+    gain_rows = gains.shape[0] // 2
+    pieces = [
+        jnp.concatenate(
+            [
+                cut(w_query, context_at, head_cols, 1),
+                cut(w_key, context_at, kv_cols, 1),
+                cut(w_value, context_at, kv_cols, 1),
+            ],
+            axis=1,
+        ),
+        cut(w_out, context_at, all_cols, 1),
+        jnp.pad(gains, ((0, 16 - gains.shape[0]), (0, 0))),
+    ]
+    packed = lax.all_gather(jnp.concatenate(pieces), "fsdp", axis=0, tiled=False)
+    own_tokens = split_x(tokens[0])
+    all_tokens = spread_context(own_tokens)
+    all_places = spread_context(split_x(positions[0]))
+
+    def unit_weights(place):
+        first = ((place * 2 + core_at) * 2 + y_at) * unit_half
+        return jnp.concatenate(
+            [
+                lax.dynamic_slice_in_dim(w_gate, first, unit_half, axis=1),
+                lax.dynamic_slice_in_dim(w_up, first, unit_half, axis=1),
+            ],
+            axis=1,
+        )
+
+    unit_own = unit_weights(fsdp_at)
+    unit_out = [unit_weights((fsdp_at + step) % 4) for step in (1, 2, 3)]
+    down_w = cut(w_down, core_at, units, 0)
+
+    def flip(block, axis, index):
+        return jnp.where(index == 0, block, jnp.flip(block, axis))
+
+    def relative(block):
+        block = block.reshape(2, 2, 2, rows)
+        block = flip(flip(flip(block, 0, y_at), 1, core_at), 2, tensor_at)
+        return jnp.swapaxes(block, 0, 1).reshape(length)
+
+    order = relative(jnp.arange(length, dtype=jnp.int32))
+    tables = attend_tables(all_places, relative(segments[0]), order)
+    residual = wide(all_tokens)
+    inverse_one = lax.rsqrt(jnp.mean(residual * residual, axis=-1, keepdims=True) + norm_epsilon)
+    all_tokens, unit_own = fence(all_tokens, unit_own)
+    packed, unit_own_given, all_tokens, inverse_one, own_cotangent, *rest = fence(
+        packed, over_y(unit_own), all_tokens, inverse_one, own_cotangent, *unit_out, *tables
+    )
+    unit_out, tables = rest[:3], rest[3:]
+
+    at = [0]
+    for piece in pieces:
+        at.append(at[-1] + piece.shape[0])
+    attn_w = packed[:, : at[1]].reshape(width, all_cols)
+    out_part = packed[:, at[1] : at[2]].reshape(4 * w_out.shape[0], all_cols)
+    gain_one = wide(packed[:, at[2] : at[2] + gain_rows].reshape(width))
+    gain_two = wide(packed[:, at[2] + gain_rows : at[2] + 2 * gain_rows].reshape(width))
+    cot_own = [gather_z(own_cotangent[:part]), None]
+    unit_got = [shift_z(unit_out[0], 1), unit_out[1], shift_z(unit_out[2], 3)]
+    out_got = context_send(out_part, context_at)
+    normed_one = low(wide(all_tokens) * inverse_one * gain_one)
+    turned, attended, logsum = attend_forward_local(
+        matmul(normed_one, attn_w), tables, heads, score_scale
+    )
+    attended, cot_own[0], cot_late, *rest = fence(
+        attended, cot_own[0], own_cotangent[part:rows], *unit_got, *out_got
+    )
+    unit_got, out_got = rest[:3], rest[3:]
+
+    unit_got[1] = shift_z(unit_got[1], 2)
+    cot_own[1] = gather_z(cot_late)
+    cot_x = [over_x(cot_own[0])]
+    out_w = jnp.concatenate(context_order(out_got, context_at), axis=1)
+    part_shape = (2, 2, rows, width)
+
+    def plane_first(theirs, mine):
+        return low(wide(mine) + wide(over_core(theirs)))
+
+    def plane_second(mine):
+        left, right = mine[..., :half_width], mine[..., half_width:]
+        return left[:, 0], over_x(left[:, 1]), right[0], over_y(right[1])
+
+    def plane_third(left, left_got, right, right_got):
+        left = low(wide(left) + wide(left_got))
+        right = low(wide(right) + wide(right_got))
+        return left[0], over_y(left[1]), right[0], over_x(right[1])
+
+    def plane_last(left, left_got, right, right_got):
+        return jnp.concatenate(
+            [wide(left) + wide(left_got), wide(right) + wide(right_got)], axis=-1
+        )
+
+    theirs = low(matmul(attended[length // 2 :], out_w)).reshape(part_shape)
+    mine = low(matmul(attended[: length // 2], out_w)).reshape(part_shape)
+    (mine,) = fence(plane_first(theirs, mine))
+    parts = fence(*plane_second(mine))
+    parts = fence(*plane_third(*parts), unit_got[1], cot_x[0], cot_own[1])
+    unit_got[1], cot_x[0], cot_own[1] = parts[4:]
+    own_residual = wide(own_tokens[:rows])
+    hidden = own_residual + plane_last(*parts[:4])
+    inverse_two, normal_two = norm_forward(hidden)
+    normed_two = low(normal_two * gain_two)
+    normed_two, cot_own[1], cot_own[0], cot_x[0], unit_got[0], unit_got[1], unit_got[2] = fence(
+        normed_two, cot_own[1], cot_own[0], cot_x[0], *unit_got
+    )
+
+    normed_own = [gather_z(normed_two[:part])]
+    unit_given = [over_y(jnp.concatenate([unit_got[0], unit_got[2]]))]
+    cot_x.append(over_x(cot_own[1]))
+    cot_core = [[over_core(cot_own[0]), over_core(cot_x[0])]]
+    own_units = jnp.zeros((width, units), jnp.bfloat16)
+    other_units = lax.dynamic_update_slice_in_dim(own_units, unit_own_given, places[0] * shard, 0)
+    for r, block in enumerate([unit_own] + list(unit_got)):
+        own_units = lax.dynamic_update_slice_in_dim(own_units, block, places[r] * shard, 0)
+    (
+        normed_own[0],
+        cot_x[1],
+        later,
+        cot_own[1],
+        own_units,
+        other_units,
+        unit_given[0],
+        unit_got[1],
+        *cot_core[0],
+    ) = fence(
+        normed_own[0],
+        cot_x[1],
+        normed_two[part:],
+        cot_own[1],
+        own_units,
+        other_units,
+        unit_given[0],
+        unit_got[1],
+        *cot_core[0],
+    )
+
+    normed_own.append(gather_z(later))
+    normed_x = [over_x(normed_own[0])]
+    unit_given.append(over_y(unit_got[1]))
+    cot_core.append([over_core(cot_own[1]), over_core(cot_x[1])])
+    for block, place in (
+        (unit_given[0][:shard], places[1]),
+        (unit_given[0][shard:], places[3]),
+        (unit_given[1], places[2]),
+    ):
+        other_units = lax.dynamic_update_slice_in_dim(other_units, block, place * shard, 0)
+    normed_core = over_core(normed_own[0])
+    (
+        normed_own[1],
+        normed_x[0],
+        normed_core,
+        own_units,
+        other_units,
+        cot_own[1],
+        cot_x[1],
+        *cot_core[1],
+    ) = fence(
+        normed_own[1],
+        normed_x[0],
+        normed_core,
+        own_units,
+        other_units,
+        cot_own[1],
+        cot_x[1],
+        *cot_core[1],
+    )
+    gate_w = place_pair(own_units[:, :unit_half], other_units[:, :unit_half], y_at, 1)
+    up_w = place_pair(own_units[:, unit_half:], other_units[:, unit_half:], y_at, 1)
+
+    def total(mine, theirs):
+        return low(wide(mine) + wide(theirs))
+
+    def piece_of(i, k, normed):
+        cot = ((cot_own, cot_x)[k][i], cot_core[i][k])
+        small = feed_forward_local(normed, cot, gate_w, up_w, down_w)
+        return list(normed) + list(cot) + list(small)
+
+    def send_y(term):
+        return over_y(cut(term, 1 - y_at, half_width, 0))
+
+    gate_w, up_w, normed_x[0], normed_own[1], normed_x_core = fence(
+        gate_w, up_w, normed_x[0], normed_own[1], over_core(normed_x[0])
+    )
+    kept = [None] * 4
+    normed_x.append(over_x(normed_own[1]))
+    kept[1] = piece_of(0, 1, (normed_x[0], normed_x_core))
+    kept[0] = piece_of(0, 0, (normed_own[0], normed_core))
+    normed_x[1], normed_own[1], *rest = fence(normed_x[1], normed_own[1], *kept[1], *kept[0])
+    kept[1], kept[0] = rest[:11], rest[11:]
+    give_core, keep_core, normed_x_core, normed_late, *rest = fence(
+        over_core(kept[1][8]),
+        over_core(kept[0][8]),
+        over_core(normed_x[1]),
+        over_core(normed_own[1]),
+        normed_x[1],
+        normed_own[1],
+        kept[1][7],
+        kept[0][7],
+    )
+    normed_x[1], normed_own[1], give, keep = rest
+    keeps = [total(keep, keep_core)]
+    give_x = [over_x(total(give, give_core))]
+    kept[3] = piece_of(1, 1, (normed_x[1], normed_x_core))
+    give_x[0], keeps[0], normed_late, normed_own[1], *kept[3] = fence(
+        give_x[0], keeps[0], normed_late, normed_own[1], *kept[3]
+    )
+    give_core, norm_term, give, normed_late, normed_own[1] = fence(
+        over_core(kept[3][8]), total(keeps[0], give_x[0]), kept[3][7], normed_late, normed_own[1]
+    )
+
+    norm_two = [scatter_z(norm_term)]
+    give_x.append(over_x(total(give, give_core)))
+    kept[2] = piece_of(1, 0, (normed_own[1], normed_late))
+
+    def weight_sum(wide_at, narrow_at, transposed=False):
+        return weight_local(
+            flat(piece[wide_at : wide_at + 2] for piece in kept),
+            [piece[narrow_at] for piece in kept],
+            transposed,
+        )
+
+    term_gate = weight_sum(0, 5)
+    give_x[1], norm_two[0], term_gate, *rest = fence(
+        give_x[1], norm_two[0], term_gate, *flat(kept)
+    )
+    kept = [rest[11 * i : 11 * i + 11] for i in range(4)]
+    keep_core, keep, give_x[1], term_gate, out_keep, out_keep_core, out_give, out_give_core, *rest = fence(
+        over_core(kept[2][8]),
+        kept[2][7],
+        give_x[1],
+        term_gate,
+        kept[0][9],
+        over_core(kept[0][10]),
+        kept[1][9],
+        over_core(kept[1][10]),
+        *flat(kept),
+    )
+    kept = [rest[11 * i : 11 * i + 11] for i in range(4)]
+
+    def unit_sum(term, given):
+        term = low(wide(cut(term, y_at, half_width, 0)) + wide(given))
+        return cut(term, core_at, half_width // 2, 0), over_core(
+            cut(term, 1 - core_at, half_width // 2, 0)
+        )
+
+    def to_owners(term):
+        return [cut(term, fsdp_at, width // 16, 0)] + [
+            shift_z(cut(term, (fsdp_at + step) % 4, width // 16, 0), step) for step in (1, 2, 3)
+        ]
+
+    norm_two.append(scatter_z(low(wide(keep) + wide(keep_core) + wide(give_x[1]))))
+    gate_given = send_y(term_gate)
+    out_x = [over_x(total(out_give, out_give_core))]
+    out_first = total(out_keep, out_keep_core)
+    term_up = weight_sum(0, 6)
+    term_down = weight_sum(2, 4, True)
+    norm_two[1], gate_given, out_x[0], term_up, term_down, *rest = fence(
+        norm_two[1],
+        gate_given,
+        out_x[0],
+        term_up,
+        term_down,
+        out_first,
+        *kept[2][9:],
+        *kept[3][9:],
+    )
+    out_first, parts_late = rest[0], [rest[1:3], rest[3:5]]
+
+    grad_norm_two = wide(jnp.concatenate(norm_two))
+    grad_hidden = wide(own_cotangent[:rows]) + norm_backward(
+        grad_norm_two, gain_two, inverse_two, normal_two
+    )
+    hidden_low = low(grad_hidden)
+    left, right = hidden_low[:, :half_width], hidden_low[:, half_width:]
+    gate_pair = unit_sum(term_gate, gate_given)
+    gain_two_sum = gain_start(jnp.sum(grad_norm_two * normal_two, axis=0).reshape(2, 2, 2, 2, -1))
+    left, left_got, right, right_got, *rest = fence(
+        left, over_x(left), right, over_y(right), *gate_pair, *gain_two_sum
+    )
+    gate_pair, gain_two_sum = rest[:2], rest[2:]
+    gain_two_sum = gain_next(*gain_two_sum, core_at, over_core, 1)
+    gate_term = place_pair(*gate_pair, core_at, 1)
+    ffn_out = [scatter_z(low(wide(out_first) + wide(out_x[0])))]
+    left = jnp.stack([left, left_got])
+    right = jnp.stack([right, right_got])
+    left, left_got, right, right_got, gate_term, *gain_two_sum = fence(
+        left, over_y(left), right, over_x(right), gate_term, *gain_two_sum
+    )
+    gain_two_sum = gain_next(*gain_two_sum, y_at, over_y)
+    mine = jnp.concatenate(
+        [jnp.stack([left, left_got]), jnp.stack([right, right_got], axis=1)], axis=-1
+    )
+    mine, theirs, gate_term, ffn_out[0], *gain_two_sum = fence(
+        mine, over_core(mine), gate_term, ffn_out[0], *gain_two_sum
+    )
+
+    hidden_low = jnp.stack([mine, theirs]).reshape(length, width)
+    gate_sent = to_owners(gate_term)
+    grad_attended = low(contract_cols(hidden_low, out_w))
+    grad_heads = attend_backward_local(turned, grad_attended, logsum, tables, heads, score_scale)
+    grad_heads, hidden_low, *rest = fence(grad_heads, hidden_low, *gate_sent, *gain_two_sum)
+    gate_sent, gain_two_sum = rest[:4], rest[4:]
+
+    high, lowest = fsdp_at // 2, fsdp_at % 2
+    gain_two_sum = gain_next(*gain_two_sum, high, functools.partial(exchange_z, distance=2))
+    theirs = low(contract_cols(grad_heads[length // 2 :], attn_w)).reshape(part_shape)
+    theirs = over_core(theirs)
+    mine = low(contract_cols(grad_heads[: length // 2], attn_w)).reshape(part_shape)
+    term_heads = contract_rows(normed_one, grad_heads)
+    gain_term = jnp.sum(term_heads * wide(attn_w), axis=1) / gain_one
+    term_heads = low(term_heads).reshape(4, 4, width // 16, all_cols).swapaxes(0, 1)
+    mine, theirs, term_heads, gain_term, *gain_two_sum = fence(
+        mine, theirs, term_heads.reshape(width, all_cols), gain_term, *gain_two_sum
+    )
+    owned_heads = scatter_z(term_heads)
+    gain_one_sum = gain_start(gain_term.reshape(2, 2, 2, 2, -1))
+    gain_two_sum = gain_next(*gain_two_sum, lowest, functools.partial(exchange_z, distance=1))
+    parts = fence(*plane_second(total(mine, theirs)), *gain_one_sum, *gain_two_sum, *flat(parts_late))
+    gain_one_sum = gain_next(*parts[4:6], core_at, over_core, 1)
+    grad_ffn_gain = parts[6] + parts[7]
+    parts_late = [parts[8:10], parts[10:12]]
+    out_last = [(first, over_core(second)) for first, second in parts_late]
+    parts = fence(*plane_third(*parts[:4]), *flat(out_last), *gain_one_sum, term_up, term_down)
+    grad_norm_one = plane_last(*parts[:4])
+    out_last = [total(*parts[4:6]), total(*parts[6:8])]
+    gain_one_sum = gain_next(*parts[8:10], y_at, over_y)
+    term_up, term_down = parts[10:]
+    normal_one = own_residual * inverse_one[:rows]
+    grad_input = low(
+        grad_hidden + norm_backward(grad_norm_one, gain_one, inverse_one[:rows], normal_one)
+    )
+
+    up_given = send_y(term_up)
+    out_x.append(over_x(out_last[1]))
+    out_x[1], up_given, grad_input, term_down, hidden_low, owned_heads, *gain_one_sum = fence(
+        out_x[1], up_given, grad_input, term_down, hidden_low, owned_heads, *gain_one_sum
+    )
+
+    ffn_out.append(scatter_z(low(wide(out_last[0]) + wide(out_x[1]))))
+    down_cols = [cut(term_down, i, half_width, 1) for i in (y_at, 1 - y_at)]
+    down_given = over_y(down_cols[1])
+    grad_tokens = place_pair(grad_input, over_x(grad_input), tensor_at, 0)
+    up_pair = unit_sum(term_up, up_given)
+    up_sent = to_owners(place_pair(*up_pair, core_at, 1))
+    heads_got = context_send(owned_heads, context_at)
+    gain_one_sum = gain_next(*gain_one_sum, high, functools.partial(exchange_z, distance=2))
+    gain_one_sum = gain_next(*gain_one_sum, lowest, functools.partial(exchange_z, distance=1))
+    grad_attn_gain = gain_one_sum[0] + gain_one_sum[1]
+    grad_w_out = wide(scatter_z(low(contract_rows(attended, hidden_low))))
+    down_sum = low(wide(down_cols[0]) + wide(down_given))
+    quarter = half_width // 2
+    down_blocks = place_pair(
+        cut(down_sum, core_at, quarter, 1),
+        over_core(cut(down_sum, 1 - core_at, quarter, 1)),
+        core_at,
+        0,
+    )
+    down_got = [cut(down_blocks, fsdp_at, unit_half, 0)] + [
+        shift_z(cut(down_blocks, (fsdp_at + step) % 4, unit_half, 0), step) for step in (1, 2, 3)
+    ]
+    block_out = low(hidden + wide(jnp.concatenate(ffn_out)))
+    output = place_pair(block_out, over_x(block_out), tensor_at, 0)
+    got = context_order(heads_got, context_at)
+    grad_w_query = wide(jnp.concatenate([block[:, :head_cols] for block in got], axis=1))
+    grad_w_key = wide(
+        jnp.concatenate([block[:, head_cols : head_cols + kv_cols] for block in got], axis=1)
+    )
+    grad_w_value = wide(jnp.concatenate([block[:, head_cols + kv_cols :] for block in got], axis=1))
+    unit_owned = []
+    for got in (gate_sent, up_sent):
+        owned = jnp.zeros((width // 16, 8 * units), jnp.float32)
+        for r in range(4):
+            owned = lax.dynamic_update_slice_in_dim(owned, wide(got[r]), places[r] * 2 * units, 1)
+        unit_owned.append(owned)
+    grad_w_gate, grad_w_up = unit_owned
+    down_stack = jnp.stack(down_got)
+    down_blocks = jnp.concatenate(
+        [
+            lax.dynamic_index_in_dim(down_stack, (fsdp_at - i) % 4, 0, keepdims=False)
+            for i in range(4)
+        ]
+    )
+    got = context_order(context_send(down_blocks, context_at), context_at)
+    grad_w_down = wide(jnp.concatenate(got, axis=1))
+    return (
+        output[None],
+        grad_tokens[None],
+        grad_attn_gain,
+        grad_w_query,
+        grad_w_key,
+        grad_w_value,
+        grad_w_out,
+        grad_ffn_gain,
+        grad_w_gate,
+        grad_w_up,
+        grad_w_down,
+    )
+
+
 def solution(mesh):
+    sizes = tuple(mesh.shape[a] for a in ("tensor", "context", "fsdp"))
     return jax.shard_map(
-        per_device,
+        per_device_moved if sizes == (2, 4, 4) else per_device_general,
         mesh=mesh,
         in_specs=(
             P("fsdp", "context", None),

time: 2930 us -> 647 us (0.22)
  waiting for transfers between devices: 2570 us -> 300 us
  matrix products: 192 us -> 20 us
  blocking collectives: 87 us -> 0 us
  Pallas kernels: 0 us -> 86.6 us
  starting transfers between devices: 1.82 us -> 76 us
  other arithmetic: 26.4 us -> 81.3 us
  local copies, waits for them, and re-layouts: 25.3 us -> 62.6 us
    reduce_scatter x9 -> x6, waiting for transfers between devices: 1350 us -> 4.53 us  [scatter_z(): return lax.psum_scatter(block, 'fsdp', scatter_dimension=0, tiled=True)]
    all_gather x9 -> x5, waiting for transfers between devices: 1080 us -> 16.9 us  [the longest x1 14.6 us: per_device_moved(): lax.all_gather(jnp.concatenate(pieces), 'fsdp', axis=0, tiled=False)]
    ppermute x0 -> x85, waiting for transfers between devices: none -> 278 us  [the longest x19 108 us: over_y(): return lax.ppermute(block, 'context', [(i, i ^ 2) for i in range(4)])]
    psum x4 -> x0, waiting for transfers between devices: 136 us -> none  [the longest x1 48.4 us: per_device(): grad_norm_two = lax.psum(grad_norm_two, 'tensor')]
    pallas_call x0 -> x9, Pallas kernels: none -> 86.6 us  [the longest x4 45.9 us: feed_forward_local(): pl.pallas_call(feed_forward_kernel, out_shape=[small] * 3 + [large] * 4,...]
    ppermute x0 -> x85, starting transfers between devices: none -> 74.8 us  [the longest x19 21 us: over_y(): return lax.ppermute(block, 'context', [(i, i ^ 2) for i in range(4)])]
    dot_general x13 -> x3, matrix products: 75.4 us -> 5.12 us  [matmul(): return jnp.dot(left, right, preferred_element_type=jnp.float32)]
    dot_general x7 -> x2, matrix products: 70.9 us -> 8.35 us  [contract_rows(): lax.dot_general(left, right, (((0,), (0,)), ((), ())), preferred_element_...]
  transfers between devices with their start and end apart: 22 -> 96, of which waited for: 20 -> 47; matrix products, arithmetic and copies ran while one was open for 6% -> 16% of each run, Pallas kernels for 0% -> 13%
where the time goes in v2:
time: 647 us; the launch traced here: 642 us
  waiting for transfers between devices  300 us (46%)
  Pallas kernels  86.6 us (13%)
  other arithmetic  81.3 us (13%)
  starting transfers between devices  76 us (12%)
  local copies, waits for them, and re-layouts  62.6 us (10%)
  matrix products  20 us (3%)
  between operations  16.3 us (3%)
    ppermute x19, waiting for transfers between devices, over_y(): return lax.ppermute(block, 'context', [(i, i ^ 2) for i in range(4)])  108 us
    ppermute x12, waiting for transfers between devices, shift_z(): return lax.ppermute(block, 'fsdp', [(i, (i + step) % 4) for i in range(4)])  85.7 us
    ppermute x18, waiting for transfers between devices, over_x(): return lax.ppermute(block, 'tensor', [(0, 1), (1, 0)])  59.8 us
    pallas_call x4, Pallas kernels, feed_forward_local(): pl.pallas_call(feed_forward_kernel, out_shape=[small] * 3 + [large] * 4,...  45.9 us
    convert_element_type x23, other arithmetic, low(): return values.astype(jnp.bfloat16)  31.5 us
    unnamed x268, local copies, waits for them, and re-layouts  25.6 us
    pallas_call x3, Pallas kernels, weight_local(): pl.pallas_call(functools.partial(weight_kernel, len(wides)), grid=(2,), i...  24.1 us
    ppermute x19, starting transfers between devices, over_y(): return lax.ppermute(block, 'context', [(i, i ^ 2) for i in range(4)])  21 us
  transfers between devices with their start and end apart: 96, of which 47 were waited for; matrix products, arithmetic and copies ran while one was open for 16% of the time, Pallas kernels for 13%

profile of v2, /device:TPU:0, one launch (start us, length us, event | category | flops | bytes accessed | tf_op | source)
XLA Modules:
  0.0 642.4 jit_solution(8643360740495212822)
XLA Ops:
  16.4 22.5 %collective-permute-done = bf16[256,2048]{1,0:T(8,128)(2,1)S(1)} collective-permute-done((bf16[256,2048]{1,0:T(8,128)(2,1)S(1)}, bf16[256,2048]{1,0:T(8,128)(2,1)S(1)}, u32[]{:S(2)}, u32[]{:S(2)}) %collective-permute-start) | collective-permute-done | bytes 1048608 | tf_op jit(solution)/shard_map/ppermute | solution.py:365
  54.1 10.1 %collective-permute-done.2 = bf16[512,512]{1,0:T(8,128)(2,1)S(1)} collective-permute-done((bf16[512,512]{1,0:T(8,128)(2,1)S(1)}, bf16[512,512]{1,0:T(8,128)(2,1)S(1)}, u32[]{:S(2)}, u32[]{:S(2)}) %collective-permute-start.2) | collective-permute-done | bytes 524320 | tf_op jit(solution)/shard_map/ppermute | solution.py:365
  64.3 14.6 %all-gather.15.cloned.1.call-done = bf16[3136,512]{1,0:T(8,128)(2,1)} async-done(((bf16[784,512]{1,0:T(8,128)(2,1)}), bf16[3136,512]{1,0:T(8,128)(2,1)}) %all-gather.15.cloned.1.call-update) | async-done | bytes 3211280 | tf_op jit(solution)/shard_map/all_gather | solution.py:676
  97.2 8.6 %shard_map.212 = (bf16[1024,512]{1,0:T(8,128)(2,1)S(1)}, bf16[1024,256]{1,0:T(8,128)(2,1)S(1)}, f32[1024,2]{1,0:T(8,128)S(1)}) custom-call(f32[1024,512]{1,0:T(8,128)S(1)} %copy-done.19, f32[1024,128]{1,0:T(8,128)S(1)} %get-tuple-element.315.cos_ref, f32[1024,128]{1,0:T(8,128)S(1)} %get-tuple-element.316.sine_ref, s32[1024,2]{1,0:T(8,128)S(1)} %copy.40.tag_ref, ...), custom_call_target="tpu_custom_call" | custom-call | flops 1 | bytes 1 | tf_op jit(solution)/shard_map/pallas_call | solution.py:591
  109.2 17.0 %collective-permute-done.6 = bf16[512,512]{1,0:T(8,128)(2,1)S(1)} collective-permute-done((bf16[512,512]{1,0:T(8,128)(2,1)}, bf16[512,512]{1,0:T(8,128)(2,1)S(1)}, u32[]{:S(2)}, u32[]{:S(2)}) %collective-permute-start.6) | collective-permute-done | bytes 524320 | tf_op jit(solution)/shard_map/ppermute | solution.py:377
  141.1 9.6 %collective-permute-done.11 = bf16[2,128,1024]{2,1,0:T(8,128)(2,1)} collective-permute-done((bf16[2,128,1024]{2,1,0:T(8,128)(2,1)}, bf16[2,128,1024]{2,1,0:T(8,128)(2,1)}, u32[]{:S(2)}, u32[]{:S(2)}) %collective-permute-start.11) | collective-permute-done | bytes 524320 | tf_op jit(solution)/shard_map/ppermute | solution.py:373
  157.6 23.8 %collective-permute-done.15 = bf16[512,512]{1,0:T(8,128)(2,1)} collective-permute-done((bf16[512,512]{1,0:T(8,128)(2,1)}, bf16[512,512]{1,0:T(8,128)(2,1)}, u32[]{:S(2)}, u32[]{:S(2)}) %collective-permute-start.15) | collective-permute-done | bytes 524320 | tf_op jit(solution)/shard_map/ppermute | solution.py:377
  193.1 16.8 %collective-permute-done.17.refs_2_.refs_6_ = bf16[256,2048]{1,0:T(8,128)(2,1)} collective-permute-done((bf16[256,2048]{1,0:T(8,128)(2,1)}, bf16[256,2048]{1,0:T(8,128)(2,1)}, u32[]{:S(2)}, u32[]{:S(2)}) %collective-permute-start.17) | collective-permute-done | bytes 1048608 | tf_op jit(solution)/shard_map/ppermute | solution.py:373
  219.7 10.2 %collective-permute-done.23 = bf16[512,512]{1,0:T(8,128)(2,1)S(1)} collective-permute-done((bf16[512,512]{1,0:T(8,128)(2,1)}, bf16[512,512]{1,0:T(8,128)(2,1)S(1)}, u32[]{:S(2)}, u32[]{:S(2)}) %collective-permute-start.23) | collective-permute-done | bytes 524320 | tf_op jit(solution)/shard_map/ppermute | solution.py:365
  250.2 11.3 %shard_map.214 = (bf16[512,512]{1,0:T(8,128)(2,1)S(1)}, bf16[512,512]{1,0:T(8,128)(2,1)S(1)}, bf16[512,512]{1,0:T(8,128)(2,1)S(1)}, bf16[256,2048]{1,0:T(8,128)(...) custom-call(bf16[256,2048]{1,0:T(8,128)(2,1)} %all-gather.11.cloned.1.call-don, ...), custom_call_target="tpu_custom_call" | custom-call | flops 1 | bytes 1 | tf_op jit(solution)/shard_map/pallas_call | solution.py:538
  266.0 11.5 %shard_map.213 = (bf16[512,512]{1,0:T(8,128)(2,1)S(1)}, bf16[512,512]{1,0:T(8,128)(2,1)S(1)}, bf16[512,512]{1,0:T(8,128)(2,1)S(1)}, bf16[256,2048]{1,0:T(8,128)(...) custom-call(bf16[256,2048]{1,0:T(8,128)(2,1)} %copy-done.3, ...), custom_call_target="tpu_custom_call" | custom-call | flops 1 | bytes 1 | tf_op jit(solution)/shard_map/pallas_call | solution.py:538
  286.3 11.3 %shard_map.215 = (bf16[512,512]{1,0:T(8,128)(2,1)S(1)}, bf16[512,512]{1,0:T(8,128)(2,1)S(1)}, bf16[512,512]{1,0:T(8,128)(2,1)S(1)}, bf16[256,2048]{1,0:T(8,128)(...) custom-call(bf16[256,2048]{1,0:T(8,128)(2,1)} %collective-permute-done.27.refs, ...), custom_call_target="tpu_custom_call" | custom-call | flops 1 | bytes 1 | tf_op jit(solution)/shard_map/pallas_call | solution.py:538
  299.4 11.6 %collective-permute-done.32 = bf16[256,2048]{1,0:T(8,128)(2,1)S(1)} collective-permute-done((bf16[256,2048]{1,0:T(8,128)(2,1)S(1)}, bf16[256,2048]{1,0:T(8,128)(2,1)S(1)}, u32[]{:S(2)}, u32[]{:S(2)}) %collective-permute-start.32) | collective-permute-done | bytes 1048608 | tf_op jit(solution)/shard_map/ppermute | solution.py:373
  315.4 11.8 %shard_map.216 = (bf16[512,512]{1,0:T(8,128)(2,1)S(1)}, bf16[512,512]{1,0:T(8,128)(2,1)S(1)}, bf16[512,512]{1,0:T(8,128)(2,1)S(1)}, bf16[256,2048]{1,0:T(8,128)(...) custom-call(bf16[256,2048]{1,0:T(8,128)(2,1)} %all-gather.13.cloned.1.call-don, ...), custom_call_target="tpu_custom_call" | custom-call | flops 1 | bytes 1 | tf_op jit(solution)/shard_map/pallas_call | solution.py:538
  328.4 8.8 %shard_map.217 = bf16[2048,512]{1,0:T(8,128)(2,1)} custom-call(bf16[256,2048]{1,0:T(8,128)(2,1)S(1)} %copy-done.2, bf16[256,2048]{1,0:T(8,128)(2,1)S(1)} %copy-done.6, bf16[256,2048]{1,0:T(8,128)(2,1)S(1)} %copy-done.4, bf16[256,2048]{1,0:T(8,128)(2,1)} %copy-done.70, bf16[256,2048]{1,0:T(8,128)(2,1)} %all-gather.13.cloned.1.call-done.refs_0_.refs_4_, ...), custom_call_target="tpu_custom_call" | custom-call | flops 1 | bytes 1 | tf_op jit(solution)/shard_map/pallas_call | solution.py:568
  361.2 7.7 %shard_map.218 = bf16[2048,512]{1,0:T(8,128)(2,1)} custom-call(bf16[256,2048]{1,0:T(8,128)(2,1)S(1)} %copy-done.2, bf16[256,2048]{1,0:T(8,128)(2,1)S(1)} %copy-done.6, bf16[256,2048]{1,0:T(8,128)(2,1)S(1)} %copy-done.4, bf16[256,2048]{1,0:T(8,128)(2,1)} %copy-done.70, bf16[256,2048]{1,0:T(8,128)(2,1)} %all-gather.13.cloned.1.call-done.refs_0_.refs_4_, ...), custom_call_target="tpu_custom_call" | custom-call | flops 1 | bytes 1 | tf_op jit(solution)/shard_map/pallas_call | solution.py:568
  369.0 7.6 %shard_map.219 = bf16[512,2048]{1,0:T(8,128)(2,1)} custom-call(bf16[256,2048]{1,0:T(8,128)(2,1)S(1)} %copy-done.14, bf16[256,2048]{1,0:T(8,128)(2,1)S(1)} %copy-done.18, bf16[256,2048]{1,0:T(8,128)(2,1)S(1)} %copy-done.16, bf16[256,2048]{1,0:T(8,128)(2,1)} %collective-permute-done.20.refs_3_, bf16[256,2048]{1,0:T(8,128)(2,1)} %all-gather.9.cloned.1.call-done.refs_2_.refs_4_, ...), custom_call_target="tpu_custom_call" | custom-call | flops 1 | bytes 1 | tf_op jit(solution)/shard_map/pallas_call | solution.py:568
  397.1 9.1 %collective-permute-done.44 = bf16[2,128,1024]{2,1,0:T(8,128)(2,1)S(1)} collective-permute-done((bf16[2,128,1024]{2,1,0:T(8,128)(2,1)S(1)}, bf16[2,128,1024]{2,1,0:T(8,128)(2,1)S(1)}, u32[]{:S(2)}, u32[]{:S(2)}) %collective-permute-start.44) | collective-permute-done | bytes 524320 | tf_op jit(solution)/shard_map/ppermute | solution.py:365
  426.3 8.0 %shard_map.220 = bf16[1024,512]{1,0:T(8,128)(2,1)S(1)} custom-call(bf16[1024,512]{1,0:T(8,128)(2,1)S(1)} %copy-done.27, bf16[1024,256]{1,0:T(8,128)(2,1)S(1)} %convolution_convert_fusion.5.grad_ref, f32[1024,2]{1,0:T(8,128)S(1)} %copy-done.32, f32[1024,128]{1,0:T(8,128)S(1)} %copy-done.10, f32[1024,128]{1,0:T(8,128)S(1)} %copy-done.8, ...), custom_call_target="tpu_custom_call" | custom-call | flops 1 | bytes 1 | tf_op jit(solution)/shard_map/pallas_call | solution.py:605
  434.4 7.1 %collective-permute-done.50 = bf16[128,1024]{1,0:T(8,128)(2,1)S(1)} collective-permute-done((bf16[128,1024]{1,0:T(8,128)(2,1)S(1)}, bf16[128,1024]{1,0:T(8,128)(2,1)S(1)}, u32[]{:S(2)}, u32[]{:S(2)}) %collective-permute-start.50) | collective-permute-done | bytes 262176 | tf_op jit(solution)/shard_map/ppermute | solution.py:377
  499.7 20.5 %collective-permute-done.65 = f32[2,2,128]{2,1,0:T(2,128)S(1)} collective-permute-done((f32[2,2,128]{2,1,0:T(2,128)S(1)}, f32[2,2,128]{2,1,0:T(2,128)S(1)}, u32[]{:S(2)}, u32[]{:S(2)}) %collective-permute-start.65) | collective-permute-done | bytes 2080 | tf_op jit(solution)/shard_map/ppermute | solution.py:365
  553.5 16.5 %collective-permute-done.77 = bf16[512,1024]{1,0:T(8,128)(2,1)S(1)} collective-permute-done((bf16[512,1024]{1,0:T(8,128)(2,1)}, bf16[512,1024]{1,0:T(8,128)(2,1)S(1)}, u32[]{:S(2)}, u32[]{:S(2)}) %collective-permute-start.77) | collective-permute-done | bytes 1048608 | tf_op jit(solution)/shard_map/ppermute | solution.py:365
  578.9 11.5 %collective-permute-done.81 = bf16[256,512]{1,0:T(8,128)(2,1)S(1)} collective-permute-done((bf16[256,512]{1,0:T(8,128)(2,1)S(1)}, bf16[256,512]{1,0:T(8,128)(2,1)S(1)}, u32[]{:S(2)}, u32[]{:S(2)}) %collective-permute-start.81) | collective-permute-done | bytes 262176 | tf_op jit(solution)/shard_map/ppermute | solution.py:377
  590.4 24.7 %collective-permute-done.80 = bf16[256,512]{1,0:T(8,128)(2,1)S(1)} collective-permute-done((bf16[256,512]{1,0:T(8,128)(2,1)S(1)}, bf16[256,512]{1,0:T(8,128)(2,1)S(1)}, u32[]{:S(2)}, u32[]{:S(2)}) %collective-permute-start.80) | collective-permute-done | bytes 262176 | tf_op jit(solution)/shard_map/ppermute | solution.py:377
  (641 shorter events, 313.8 us)
Async XLA Ops:
  7.2 71.6 %all-gather.15.cloned.1.call-start = ((), (), s32[]{:S(2)}) async-start(), calls=%async_computation.16 | async-start | bytes 4014080 | tf_op jit(solution)/shard_map/all_gather | solution.py:676
  11.4 114.8 %all-gather.7.cloned.1.call-start = ((), (), s32[]{:S(2)}) async-start(), calls=%async_computation.6 | async-start | bytes 1310720 | tf_op jit(solution)/shard_map/all_gather | solution.py:385
  12.7 26.2 %collective-permute-start = (bf16[256,2048]{1,0:T(8,128)(2,1)S(1)}, bf16[256,2048]{1,0:T(8,128)(2,1)S(1)}, u32[]{:S(2)}, u32[]{:S(2)}) collective-permute-start(bf16[256,2048]{1,0:T(8,128)(2,1)S(1)} %pad_maximum_fusion.5), channel_id=1, source_target_pairs={{0,8},{4,12},{8,0},{12,4},{1,9},{5,13},{9,1},{13,5},{2,10},{6,14},... | collective-permute-start | bytes 3145736 | tf_op jit(solution)/shard_map/ppermute | solution.py:365
  15.7 29.2 %collective-permute-start.3 = (s32[256]{0:T(256)S(1)}, s32[256]{0:T(256)S(1)}, u32[]{:S(2)}, u32[]{:S(2)}) collective-permute-start(s32[256]{0:T(256)S(1)} %pad_add_fusion.3), channel_id=1, source_target_pairs={{0,8},{4,12},{8,0},{12,4},{1,9},{5,13},{9,1},{13,5},{2,10},{6,14},... | collective-permute-start | bytes 3080 | tf_op jit(solution)/shard_map/ppermute | solution.py:365
  79.7 101.7 %all-gather.9.cloned.1.call-start = ((), (), s32[]{:S(2)}) async-start(), calls=%async_computation.7 | async-start | bytes 1310720 | tf_op jit(solution)/shard_map/all_gather | solution.py:385
  83.7 42.5 %collective-permute-start.6 = (bf16[512,512]{1,0:T(8,128)(2,1)}, bf16[512,512]{1,0:T(8,128)(2,1)S(1)}, u32[]{:S(2)}, u32[]{:S(2)}) collective-permute-start(bf16[512,512]{1,0:T(8,128)(2,1)} %pad_maximum_fusion.17), channel_id=1, source_target_pairs={{0,3},{1,0},{2,1},{3,2},{4,7},{5,4},{6,5},{7,6},{8,11},{9,8},{10,9... | collective-permute-start | bytes 1572872 | tf_op jit(solution)/shard_map/ppermute | solution.py:377
  138.6 73.9 %all-gather.11.cloned.1.call-start = ((), (), s32[]{:S(2)}) async-start(), calls=%async_computation.8 | async-start | bytes 1310720 | tf_op jit(solution)/shard_map/all_gather | solution.py:385
  138.7 42.8 %collective-permute-start.15 = (bf16[512,512]{1,0:T(8,128)(2,1)}, bf16[512,512]{1,0:T(8,128)(2,1)}, u32[]{:S(2)}, u32[]{:S(2)}) collective-permute-start(bf16[512,512]{1,0:T(8,128)(2,1)} %pad_maximum_fusion.16), channel_id=1, source_target_pairs={{0,2},{1,3},{2,0},{3,1},{4,6},{5,7},{6,4},{7,5},{8,10},{9,11},{10,... | collective-permute-start | bytes 1572872 | tf_op jit(solution)/shard_map/ppermute | solution.py:377
  140.5 40.9 %collective-permute-start.16 = (bf16[256,2048]{1,0:T(8,128)(2,1)S(1)}, bf16[256,2048]{1,0:T(8,128)(2,1)S(1)}, u32[]{:S(2)}, u32[]{:S(2)}) collective-permute-start(bf16[256,2048]{1,0:T(8,128)(2,1)S(1)} %copy-done.13), channel_id=1, source_target_pairs={{0,16},{16,0},{1,17},{17,1},{2,18},{18,2},{3,19},{19,3},{4,20},{20... | collective-permute-start | bytes 3145736 | tf_op jit(solution)/shard_map/ppermute | solution.py:373
  154.0 27.4 %collective-permute-start.13 = (bf16[128,1024]{1,0:T(8,128)(2,1)}, bf16[128,1024]{1,0:T(8,128)(2,1)}, u32[]{:S(2)}, u32[]{:S(2)}) collective-permute-start(bf16[128,1024]{1,0:T(8,128)(2,1)} %get-tuple-element.706), channel_id=1, source_target_pairs={{0,8},{4,12},{8,0},{12,4},{1,9},{5,13},{9,1},{13,5},{2,10},{6,14},... | collective-permute-start | bytes 786440 | tf_op jit(solution)/shard_map/ppermute | solution.py:365
  185.2 54.8 %all-gather.13.cloned.1.call-start = ((), (), s32[]{:S(2)}) async-start(), calls=%async_computation.9 | async-start | bytes 1310720 | tf_op jit(solution)/shard_map/all_gather | solution.py:385
  212.5 127.6 %reduce-scatter.7.cloned.1.call-start = ((), (), s32[]{:S(2)}) async-start(), calls=%async_computation.10 | async-start | bytes 1310720 | tf_op jit(solution)/shard_map/reduce_scatter | solution.py:389
  245.6 31.9 %collective-permute-start.27 = (bf16[256,2048]{1,0:T(8,128)(2,1)S(1)}, bf16[256,2048]{1,0:T(8,128)(2,1)}, u32[]{:S(2)}, u32[]{:S(2)}) collective-permute-start(bf16[256,2048]{1,0:T(8,128)(2,1)S(1)} %copy-done.69), channel_id=1, source_target_pairs={{0,16},{16,0},{1,17},{17,1},{2,18},{18,2},{3,19},{19,3},{4,20},{20... | collective-permute-start | bytes 3145736 | tf_op jit(solution)/shard_map/ppermute | solution.py:373
  313.8 67.3 %reduce-scatter.9.cloned.1.call-start = ((), (), s32[]{:S(2)}) async-start(), calls=%async_computation.11 | async-start | bytes 1310720 | tf_op jit(solution)/shard_map/reduce_scatter | solution.py:389
  349.2 67.8 %reduce-scatter.11.cloned.1.call-start = ((), (), s32[]{:S(2)}) async-start(), calls=%async_computation.12 | async-start | bytes 1310720 | tf_op jit(solution)/shard_map/reduce_scatter | solution.py:389
  351.8 27.6 %collective-permute-start.38 = (bf16[1024,512]{1,0:T(8,128)(2,1)}, bf16[1024,512]{1,0:T(8,128)(2,1)}, u32[]{:S(2)}, u32[]{:S(2)}) collective-permute-start(bf16[1024,512]{1,0:T(8,128)(2,1)} %constant_dynamic-slice_fusion.32), channel_id=1, source_target_pairs={{0,8},{4,12},{8,0},{12,4},{1,9},{5,13},{9,1},{13,5},{2,10},{6,14},... | collective-permute-start | bytes 3145736 | tf_op jit(solution)/shard_map/ppermute | solution.py:365
  391.0 130.1 %reduce-scatter.13.cloned.1.call-start = ((), (), s32[]{:S(2)}) async-start(), calls=%async_computation.13 | async-start | bytes 2621440 | tf_op jit(solution)/shard_map/reduce_scatter | solution.py:389
  463.3 154.9 %reduce-scatter.15.cloned.1.call-start = ((), (), s32[]{:S(2)}) async-start(), calls=%async_computation.14 | async-start | bytes 1310720 | tf_op jit(solution)/shard_map/reduce_scatter | solution.py:389
  524.3 95.9 %reduce-scatter.17.cloned.1.call-start = ((), (), s32[]{:S(2)}) async-start(), calls=%async_computation.15 | async-start | bytes 1310720 | tf_op jit(solution)/shard_map/reduce_scatter | solution.py:389
  527.4 43.1 %collective-permute-start.67 = (bf16[128,2048]{1,0:T(8,128)(2,1)}, bf16[128,2048]{1,0:T(8,128)(2,1)}, u32[]{:S(2)}, u32[]{:S(2)}) collective-permute-start(bf16[128,2048]{1,0:T(8,128)(2,1)} %fusion.15), channel_id=1, source_target_pairs={{0,16},{16,0},{1,17},{17,1},{2,18},{18,2},{3,19},{19,3},{4,20},{20... | collective-permute-start | bytes 1572872 | tf_op jit(solution)/shard_map/ppermute | solution.py:373
  550.6 28.2 %collective-permute-start.75 = (bf16[128,1024]{1,0:T(8,128)(2,1)S(1)}, bf16[128,1024]{1,0:T(8,128)(2,1)S(1)}, u32[]{:S(2)}, u32[]{:S(2)}) collective-permute-start(bf16[128,1024]{1,0:T(8,128)(2,1)S(1)} %get-tuple-element.661), channel_id=1, source_target_pairs={{0,2},{1,3},{2,0},{3,1},{4,6},{5,7},{6,4},{7,5},{8,10},{9,11},{10,... | collective-permute-start | bytes 786440 | tf_op jit(solution)/shard_map/ppermute | solution.py:377
  552.0 26.8 %collective-permute-start.76 = (bf16[128,1024]{1,0:T(8,128)(2,1)S(1)}, bf16[128,1024]{1,0:T(8,128)(2,1)S(1)}, u32[]{:S(2)}, u32[]{:S(2)}) collective-permute-start(bf16[128,1024]{1,0:T(8,128)(2,1)S(1)} %get-tuple-element.659), channel_id=1, source_target_pairs={{0,3},{1,0},{2,1},{3,2},{4,7},{5,4},{6,5},{7,6},{8,11},{9,8},{10,9... | collective-permute-start | bytes 786440 | tf_op jit(solution)/shard_map/ppermute | solution.py:377
  578.1 37.0 %collective-permute-start.80 = (bf16[256,512]{1,0:T(8,128)(2,1)S(1)}, bf16[256,512]{1,0:T(8,128)(2,1)S(1)}, u32[]{:S(2)}, u32[]{:S(2)}) collective-permute-start(bf16[256,512]{1,0:T(8,128)(2,1)S(1)} %get-tuple-element.657), channel_id=1, source_target_pairs={{0,2},{1,3},{2,0},{3,1},{4,6},{5,7},{6,4},{7,5},{8,10},{9,11},{10,... | collective-permute-start | bytes 786440 | tf_op jit(solution)/shard_map/ppermute | solution.py:377
  578.3 36.8 %collective-permute-start.79 = (bf16[256,512]{1,0:T(8,128)(2,1)S(1)}, bf16[256,512]{1,0:T(8,128)(2,1)S(1)}, u32[]{:S(2)}, u32[]{:S(2)}) collective-permute-start(bf16[256,512]{1,0:T(8,128)(2,1)S(1)} %get-tuple-element.656), channel_id=1, source_target_pairs={{0,1},{1,2},{2,3},{3,0},{4,5},{5,6},{6,7},{7,4},{8,9},{9,10},{10,1... | collective-permute-start | bytes 786440 | tf_op jit(solution)/shard_map/ppermute | solution.py:377
  (206 other events, 1970.4 us)
Sparse Core Ops, SparseCore 0:
  11.5 67.2 all-gather.14
  81.0 44.1 all-gather.6
  138.7 40.9 all-gather.8
  185.3 25.2 all-gather.10
  212.6 27.3 all-gather.12
  313.9 25.8 reduce-scatter.6
  349.3 25.8 reduce-scatter.8
  391.1 25.7 reduce-scatter.10
  463.4 44.8 reduce-scatter.12
  524.4 27.1 reduce-scatter.14
  554.7 51.6 reduce-scatter.16

commit v3 on v2

--- a/solution.py
+++ b/solution.py
@@ -377,10 +377,6 @@
     return lax.ppermute(block, "fsdp", [(i, (i + step) % 4) for i in range(4)])
 
 
-def exchange_z(block, distance):
-    return lax.ppermute(block, "fsdp", [(i, i ^ distance) for i in range(4)])
-
-
 def gather_z(block):
     return lax.all_gather(block, "fsdp", axis=0, tiled=True)
 
@@ -705,8 +701,8 @@
     residual = wide(all_tokens)
     inverse_one = lax.rsqrt(jnp.mean(residual * residual, axis=-1, keepdims=True) + norm_epsilon)
     all_tokens, unit_own = fence(all_tokens, unit_own)
-    packed, unit_own_given, all_tokens, inverse_one, own_cotangent, *rest = fence(
-        packed, over_y(unit_own), all_tokens, inverse_one, own_cotangent, *unit_out, *tables
+    packed, unit_own_given, all_tokens, inverse_one, own_cotangent, down_w, *rest = fence(
+        packed, over_y(unit_own), all_tokens, inverse_one, own_cotangent, down_w, *unit_out, *tables
     )
     unit_out, tables = rest[:3], rest[3:]
 
@@ -935,91 +931,113 @@
     hidden_low = low(grad_hidden)
     left, right = hidden_low[:, :half_width], hidden_low[:, half_width:]
     gate_pair = unit_sum(term_gate, gate_given)
-    gain_two_sum = gain_start(jnp.sum(grad_norm_two * normal_two, axis=0).reshape(2, 2, 2, 2, -1))
+    def gain_send(term):
+        term = term.reshape(2, 2, 4, -1)
+        parts = [
+            lax.dynamic_index_in_dim(term, (fsdp_at + step) % 4, 2, keepdims=False)
+            for step in range(4)
+        ]
+        return parts[:1] + [shift_z(parts[step], step) for step in (1, 2, 3)]
+
+    gain_two_all = gain_send(jnp.sum(grad_norm_two * normal_two, axis=0))
     left, left_got, right, right_got, *rest = fence(
-        left, over_x(left), right, over_y(right), *gate_pair, *gain_two_sum
-    )
-    gate_pair, gain_two_sum = rest[:2], rest[2:]
-    gain_two_sum = gain_next(*gain_two_sum, core_at, over_core, 1)
+        left, over_x(left), right, over_y(right), *gate_pair, *gain_two_all
+    )
+    gate_pair, gain_two_sum = rest[:2], gain_start(sum(rest[2:]))
     gate_term = place_pair(*gate_pair, core_at, 1)
     ffn_out = [scatter_z(low(wide(out_first) + wide(out_x[0])))]
     left = jnp.stack([left, left_got])
     right = jnp.stack([right, right_got])
-    left, left_got, right, right_got, gate_term, *gain_two_sum = fence(
-        left, over_y(left), right, over_x(right), gate_term, *gain_two_sum
-    )
-    gain_two_sum = gain_next(*gain_two_sum, y_at, over_y)
+    out_last = flat((first, over_core(second)) for first, second in parts_late)
+    left, left_got, right, right_got, gate_term, *rest = fence(
+        left, over_y(left), right, over_x(right), gate_term, *gain_two_sum, *out_last
+    )
+    gain_two_sum, out_last = rest[:2], [total(*rest[2:4]), total(*rest[4:])]
+    gain_two_sum = gain_next(*gain_two_sum, core_at, over_core, 1)
     mine = jnp.concatenate(
         [jnp.stack([left, left_got]), jnp.stack([right, right_got], axis=1)], axis=-1
     )
-    mine, theirs, gate_term, ffn_out[0], *gain_two_sum = fence(
-        mine, over_core(mine), gate_term, ffn_out[0], *gain_two_sum
-    )
+    mine, theirs, gate_term, ffn_out[0], term_up, *rest = fence(
+        mine, over_core(mine), gate_term, ffn_out[0], term_up, *gain_two_sum, *out_last
+    )
+    gain_two_sum, out_last = rest[:2], rest[2:]
 
     hidden_low = jnp.stack([mine, theirs]).reshape(length, width)
     gate_sent = to_owners(gate_term)
+    owned_out = scatter_z(low(contract_rows(attended, hidden_low)))
+    up_given = send_y(term_up)
+    out_x.append(over_x(out_last[1]))
     grad_attended = low(contract_cols(hidden_low, out_w))
     grad_heads = attend_backward_local(turned, grad_attended, logsum, tables, heads, score_scale)
-    grad_heads, hidden_low, *rest = fence(grad_heads, hidden_low, *gate_sent, *gain_two_sum)
-    gate_sent, gain_two_sum = rest[:4], rest[4:]
-
-    high, lowest = fsdp_at // 2, fsdp_at % 2
-    gain_two_sum = gain_next(*gain_two_sum, high, functools.partial(exchange_z, distance=2))
+    gain_two_sum = gain_next(*gain_two_sum, y_at, over_y)
+    grad_heads, hidden_low, *gain_two_sum = fence(grad_heads, hidden_low, *gain_two_sum)
+    grad_ffn_gain = gain_two_sum[0] + gain_two_sum[1]
+
     theirs = low(contract_cols(grad_heads[length // 2 :], attn_w)).reshape(part_shape)
     theirs = over_core(theirs)
     mine = low(contract_cols(grad_heads[: length // 2], attn_w)).reshape(part_shape)
     term_heads = contract_rows(normed_one, grad_heads)
     gain_term = jnp.sum(term_heads * wide(attn_w), axis=1) / gain_one
     term_heads = low(term_heads).reshape(4, 4, width // 16, all_cols).swapaxes(0, 1)
-    mine, theirs, term_heads, gain_term, *gain_two_sum = fence(
-        mine, theirs, term_heads.reshape(width, all_cols), gain_term, *gain_two_sum
-    )
+    mine, theirs, term_heads, gain_term, owned_out, term_up, up_given, out_x[1], *gate_sent = fence(
+        mine,
+        theirs,
+        term_heads.reshape(width, all_cols),
+        gain_term,
+        owned_out,
+        term_up,
+        up_given,
+        out_x[1],
+        *gate_sent,
+    )
+    up_pair = unit_sum(term_up, up_given)
     owned_heads = scatter_z(term_heads)
-    gain_one_sum = gain_start(gain_term.reshape(2, 2, 2, 2, -1))
-    gain_two_sum = gain_next(*gain_two_sum, lowest, functools.partial(exchange_z, distance=1))
-    parts = fence(*plane_second(total(mine, theirs)), *gain_one_sum, *gain_two_sum, *flat(parts_late))
+    gain_one_all = gain_send(gain_term)
+    parts = fence(*plane_second(total(mine, theirs)), *gain_one_all, *up_pair)
+    gain_one_sum = gain_start(sum(parts[4:8]))
+    grad_w_out = wide(owned_out)
+    up_term = place_pair(*parts[8:], core_at, 1)
+    parts = fence(*plane_third(*parts[:4]), *gain_one_sum, up_term, term_down, *out_last)
+    grad_norm_one = plane_last(*parts[:4])
     gain_one_sum = gain_next(*parts[4:6], core_at, over_core, 1)
-    grad_ffn_gain = parts[6] + parts[7]
-    parts_late = [parts[8:10], parts[10:12]]
-    out_last = [(first, over_core(second)) for first, second in parts_late]
-    parts = fence(*plane_third(*parts[:4]), *flat(out_last), *gain_one_sum, term_up, term_down)
-    grad_norm_one = plane_last(*parts[:4])
-    out_last = [total(*parts[4:6]), total(*parts[6:8])]
-    gain_one_sum = gain_next(*parts[8:10], y_at, over_y)
-    term_up, term_down = parts[10:]
+    up_term, term_down = parts[6:8]
+    out_last = parts[8:]
     normal_one = own_residual * inverse_one[:rows]
     grad_input = low(
         grad_hidden + norm_backward(grad_norm_one, gain_one, inverse_one[:rows], normal_one)
     )
 
-    up_given = send_y(term_up)
-    out_x.append(over_x(out_last[1]))
-    out_x[1], up_given, grad_input, term_down, hidden_low, owned_heads, *gain_one_sum = fence(
-        out_x[1], up_given, grad_input, term_down, hidden_low, owned_heads, *gain_one_sum
-    )
-
-    ffn_out.append(scatter_z(low(wide(out_last[0]) + wide(out_x[1]))))
+    out_term = low(wide(out_last[0]) + wide(out_x[1]))
     down_cols = [cut(term_down, i, half_width, 1) for i in (y_at, 1 - y_at)]
     down_given = over_y(down_cols[1])
-    grad_tokens = place_pair(grad_input, over_x(grad_input), tensor_at, 0)
-    up_pair = unit_sum(term_up, up_given)
-    up_sent = to_owners(place_pair(*up_pair, core_at, 1))
-    heads_got = context_send(owned_heads, context_at)
-    gain_one_sum = gain_next(*gain_one_sum, high, functools.partial(exchange_z, distance=2))
-    gain_one_sum = gain_next(*gain_one_sum, lowest, functools.partial(exchange_z, distance=1))
-    grad_attn_gain = gain_one_sum[0] + gain_one_sum[1]
-    grad_w_out = wide(scatter_z(low(contract_rows(attended, hidden_low))))
+    grad_input_x = over_x(grad_input)
+    down_given, grad_input, grad_input_x, up_term, *gain_one_sum = fence(
+        down_given, grad_input, grad_input_x, up_term, *gain_one_sum
+    )
+    grad_tokens = place_pair(grad_input, grad_input_x, tensor_at, 0)
     down_sum = low(wide(down_cols[0]) + wide(down_given))
     quarter = half_width // 2
-    down_blocks = place_pair(
+    down_own, down_core, up_term, out_term, owned_heads = fence(
         cut(down_sum, core_at, quarter, 1),
         over_core(cut(down_sum, 1 - core_at, quarter, 1)),
-        core_at,
-        0,
-    )
+        up_term,
+        out_term,
+        owned_heads,
+    )
+    ffn_out.append(scatter_z(out_term))
+
+    down_blocks = place_pair(down_own, down_core, core_at, 0)
     down_got = [cut(down_blocks, fsdp_at, unit_half, 0)] + [
         shift_z(cut(down_blocks, (fsdp_at + step) % 4, unit_half, 0), step) for step in (1, 2, 3)
     ]
+    heads_got = context_send(owned_heads, context_at)
+    gain_one_sum = gain_next(*gain_one_sum, y_at, over_y)
+    up_term, ffn_out[1], *rest = fence(
+        up_term, ffn_out[1], *down_got, *heads_got, *gain_one_sum
+    )
+    down_got, heads_got = rest[:4], rest[4:8]
+    grad_attn_gain = rest[8] + rest[9]
+    up_sent = to_owners(up_term)
     block_out = low(hidden + wide(jnp.concatenate(ffn_out)))
     output = place_pair(block_out, over_x(block_out), tensor_at, 0)
     got = context_order(heads_got, context_at)

time: 647 us -> 632 us (0.977)
  waiting for transfers between devices: 300 us -> 262 us
  starting transfers between devices: 76 us -> 89.3 us
  other arithmetic: 81.3 us -> 90.6 us
    ppermute x19, waiting for transfers between devices: 108 us -> 56.8 us  [over_y(): return lax.ppermute(block, 'context', [(i, i ^ 2) for i in range(4)])]
    ppermute x12 -> x18, starting transfers between devices: 18.6 us -> 35.9 us  [shift_z(): return lax.ppermute(block, 'fsdp', [(i, (i + step) % 4) for i in range(4)])]
    ppermute x12 -> x18, waiting for transfers between devices: 85.7 us -> 98.1 us  [shift_z(): return lax.ppermute(block, 'fsdp', [(i, (i + step) % 4) for i in range(4)])]
    ppermute x4 -> x0, starting transfers between devices: 10.5 us -> none  [exchange_z(): return lax.ppermute(block, 'fsdp', [(i, i ^ distance) for i in range(4)])]
    ppermute x18, waiting for transfers between devices: 59.8 us -> 69.6 us  [over_x(): return lax.ppermute(block, 'tensor', [(0, 1), (1, 0)])]
    convert_element_type x23 -> x24, other arithmetic: 31.5 us -> 37.5 us  [low(): return values.astype(jnp.bfloat16)]
    dynamic_slice x12 -> x14, local copies, waits for them, and re-layouts: 11.7 us -> 13.1 us  [cut(): return lax.dynamic_slice_in_dim(block, index * size, size, axis=axis)]
    unnamed x268 -> x300, local copies, waits for them, and re-layouts: 25.6 us -> 25.8 us
  transfers between devices with their start and end apart: 96 -> 98, of which waited for: 47 -> 45; matrix products, arithmetic and copies ran while one was open for 16% -> 18% of each run, Pallas kernels for 13% -> 14%
where the time goes in v3:
time: 632 us; the launch traced here: 627 us
  waiting for transfers between devices  262 us (41%)
  other arithmetic  90.6 us (14%)
  starting transfers between devices  89.3 us (14%)
  Pallas kernels  86.8 us (14%)
  local copies, waits for them, and re-layouts  62.3 us (10%)
  matrix products  19.7 us (3%)
  between operations  16.3 us (3%)
    ppermute x18, waiting for transfers between devices, shift_z(): return lax.ppermute(block, 'fsdp', [(i, (i + step) % 4) for i in range(4)])  98.1 us
    ppermute x18, waiting for transfers between devices, over_x(): return lax.ppermute(block, 'tensor', [(0, 1), (1, 0)])  69.6 us
    ppermute x19, waiting for transfers between devices, over_y(): return lax.ppermute(block, 'context', [(i, i ^ 2) for i in range(4)])  56.8 us
    pallas_call x4, Pallas kernels, feed_forward_local(): pl.pallas_call(feed_forward_kernel, out_shape=[small] * 3 + [large] * 4,...  46.1 us
    convert_element_type x24, other arithmetic, low(): return values.astype(jnp.bfloat16)  37.5 us
    ppermute x18, starting transfers between devices, shift_z(): return lax.ppermute(block, 'fsdp', [(i, (i + step) % 4) for i in range(4)])  35.9 us
    unnamed x300, local copies, waits for them, and re-layouts  25.8 us
    pallas_call x3, Pallas kernels, weight_local(): pl.pallas_call(functools.partial(weight_kernel, len(wides)), grid=(2,), i...  24.2 us
  transfers between devices with their start and end apart: 98, of which 45 were waited for; matrix products, arithmetic and copies ran while one was open for 18% of the time, Pallas kernels for 14%

profile of v3, /device:TPU:0, one launch (start us, length us, event | category | flops | bytes accessed | tf_op | source)
XLA Modules:
  0.0 626.7 jit_solution(11897006991669808123)
XLA Ops:
  16.4 22.5 %collective-permute-done = bf16[256,2048]{1,0:T(8,128)(2,1)S(1)} collective-permute-done((bf16[256,2048]{1,0:T(8,128)(2,1)S(1)}, bf16[256,2048]{1,0:T(8,128)(2,1)S(1)}, u32[]{:S(2)}, u32[]{:S(2)}) %collective-permute-start) | collective-permute-done | bytes 1048608 | tf_op jit(solution)/shard_map/ppermute | solution.py:365
  56.6 10.1 %collective-permute-done.2 = bf16[512,512]{1,0:T(8,128)(2,1)S(1)} collective-permute-done((bf16[512,512]{1,0:T(8,128)(2,1)S(1)}, bf16[512,512]{1,0:T(8,128)(2,1)S(1)}, u32[]{:S(2)}, u32[]{:S(2)}) %collective-permute-start.2) | collective-permute-done | bytes 524320 | tf_op jit(solution)/shard_map/ppermute | solution.py:365
  66.7 12.1 %all-gather.15.cloned.1.call-done = bf16[3136,512]{1,0:T(8,128)(2,1)} async-done(((bf16[784,512]{1,0:T(8,128)(2,1)}), bf16[3136,512]{1,0:T(8,128)(2,1)}) %all-gather.15.cloned.1.call-update) | async-done | bytes 3211280 | tf_op jit(solution)/shard_map/all_gather | solution.py:672
  96.9 8.6 %shard_map.212 = (bf16[1024,512]{1,0:T(8,128)(2,1)S(1)}, bf16[1024,256]{1,0:T(8,128)(2,1)S(1)}, f32[1024,2]{1,0:T(8,128)S(1)}) custom-call(f32[1024,512]{1,0:T(8,128)S(1)} %copy-done.19, f32[1024,128]{1,0:T(8,128)S(1)} %get-tuple-element.336.cos_ref, f32[1024,128]{1,0:T(8,128)S(1)} %get-tuple-element.337.sine_ref, s32[1024,2]{1,0:T(8,128)S(1)} %copy.40.tag_ref, ...), custom_call_target="tpu_custom_call" | custom-call | flops 1 | bytes 1 | tf_op jit(solution)/shard_map/pallas_call | solution.py:587
  109.2 16.7 %collective-permute-done.6 = bf16[512,512]{1,0:T(8,128)(2,1)S(1)} collective-permute-done((bf16[512,512]{1,0:T(8,128)(2,1)}, bf16[512,512]{1,0:T(8,128)(2,1)S(1)}, u32[]{:S(2)}, u32[]{:S(2)}) %collective-permute-start.6) | collective-permute-done | bytes 524320 | tf_op jit(solution)/shard_map/ppermute | solution.py:377
  141.1 9.3 %collective-permute-done.11 = bf16[2,128,1024]{2,1,0:T(8,128)(2,1)} collective-permute-done((bf16[2,128,1024]{2,1,0:T(8,128)(2,1)}, bf16[2,128,1024]{2,1,0:T(8,128)(2,1)}, u32[]{:S(2)}, u32[]{:S(2)}) %collective-permute-start.11) | collective-permute-done | bytes 524320 | tf_op jit(solution)/shard_map/ppermute | solution.py:373
  157.2 23.8 %collective-permute-done.15 = bf16[512,512]{1,0:T(8,128)(2,1)} collective-permute-done((bf16[512,512]{1,0:T(8,128)(2,1)}, bf16[512,512]{1,0:T(8,128)(2,1)}, u32[]{:S(2)}, u32[]{:S(2)}) %collective-permute-start.15) | collective-permute-done | bytes 524320 | tf_op jit(solution)/shard_map/ppermute | solution.py:377
  192.8 16.8 %collective-permute-done.17.refs_2_.refs_6_ = bf16[256,2048]{1,0:T(8,128)(2,1)} collective-permute-done((bf16[256,2048]{1,0:T(8,128)(2,1)}, bf16[256,2048]{1,0:T(8,128)(2,1)}, u32[]{:S(2)}, u32[]{:S(2)}) %collective-permute-start.17) | collective-permute-done | bytes 1048608 | tf_op jit(solution)/shard_map/ppermute | solution.py:373
  219.4 10.2 %collective-permute-done.23 = bf16[512,512]{1,0:T(8,128)(2,1)S(1)} collective-permute-done((bf16[512,512]{1,0:T(8,128)(2,1)}, bf16[512,512]{1,0:T(8,128)(2,1)S(1)}, u32[]{:S(2)}, u32[]{:S(2)}) %collective-permute-start.23) | collective-permute-done | bytes 524320 | tf_op jit(solution)/shard_map/ppermute | solution.py:365
  247.0 11.3 %shard_map.214 = (bf16[512,512]{1,0:T(8,128)(2,1)S(1)}, bf16[512,512]{1,0:T(8,128)(2,1)S(1)}, bf16[512,512]{1,0:T(8,128)(2,1)S(1)}, bf16[256,2048]{1,0:T(8,128)(...) custom-call(bf16[256,2048]{1,0:T(8,128)(2,1)} %all-gather.11.cloned.1.call-don, ...), custom_call_target="tpu_custom_call" | custom-call | flops 1 | bytes 1 | tf_op jit(solution)/shard_map/pallas_call | solution.py:534
  262.7 11.7 %shard_map.213 = (bf16[512,512]{1,0:T(8,128)(2,1)S(1)}, bf16[512,512]{1,0:T(8,128)(2,1)S(1)}, bf16[512,512]{1,0:T(8,128)(2,1)S(1)}, bf16[256,2048]{1,0:T(8,128)(...) custom-call(bf16[256,2048]{1,0:T(8,128)(2,1)} %copy-done.3, ...), custom_call_target="tpu_custom_call" | custom-call | flops 1 | bytes 1 | tf_op jit(solution)/shard_map/pallas_call | solution.py:534
  282.8 11.3 %shard_map.215 = (bf16[512,512]{1,0:T(8,128)(2,1)S(1)}, bf16[512,512]{1,0:T(8,128)(2,1)S(1)}, bf16[512,512]{1,0:T(8,128)(2,1)S(1)}, bf16[256,2048]{1,0:T(8,128)(...) custom-call(bf16[256,2048]{1,0:T(8,128)(2,1)} %copy-done.74, ...), custom_call_target="tpu_custom_call" | custom-call | flops 1 | bytes 1 | tf_op jit(solution)/shard_map/pallas_call | solution.py:534
  295.9 11.6 %collective-permute-done.32 = bf16[256,2048]{1,0:T(8,128)(2,1)S(1)} collective-permute-done((bf16[256,2048]{1,0:T(8,128)(2,1)S(1)}, bf16[256,2048]{1,0:T(8,128)(2,1)S(1)}, u32[]{:S(2)}, u32[]{:S(2)}) %collective-permute-start.32) | collective-permute-done | bytes 1048608 | tf_op jit(solution)/shard_map/ppermute | solution.py:373
  311.6 11.8 %shard_map.216 = (bf16[512,512]{1,0:T(8,128)(2,1)S(1)}, bf16[512,512]{1,0:T(8,128)(2,1)S(1)}, bf16[512,512]{1,0:T(8,128)(2,1)S(1)}, bf16[256,2048]{1,0:T(8,128)(...) custom-call(bf16[256,2048]{1,0:T(8,128)(2,1)} %all-gather.13.cloned.1.call-don, ...), custom_call_target="tpu_custom_call" | custom-call | flops 1 | bytes 1 | tf_op jit(solution)/shard_map/pallas_call | solution.py:534
  324.6 8.8 %shard_map.217 = bf16[2048,512]{1,0:T(8,128)(2,1)} custom-call(bf16[256,2048]{1,0:T(8,128)(2,1)S(1)} %copy-done.2, bf16[256,2048]{1,0:T(8,128)(2,1)S(1)} %copy-done.6, bf16[256,2048]{1,0:T(8,128)(2,1)S(1)} %copy-done.4, bf16[256,2048]{1,0:T(8,128)(2,1)} %copy-done.73, bf16[256,2048]{1,0:T(8,128)(2,1)} %all-gather.13.cloned.1.call-done.refs_0_.refs_4_, ...), custom_call_target="tpu_custom_call" | custom-call | flops 1 | bytes 1 | tf_op jit(solution)/shard_map/pallas_call | solution.py:564
  358.0 7.7 %shard_map.218 = bf16[2048,512]{1,0:T(8,128)(2,1)} custom-call(bf16[256,2048]{1,0:T(8,128)(2,1)S(1)} %copy-done.2, bf16[256,2048]{1,0:T(8,128)(2,1)S(1)} %copy-done.6, bf16[256,2048]{1,0:T(8,128)(2,1)S(1)} %copy-done.4, bf16[256,2048]{1,0:T(8,128)(2,1)} %copy-done.73, bf16[256,2048]{1,0:T(8,128)(2,1)} %all-gather.13.cloned.1.call-done.refs_0_.refs_4_, ...), custom_call_target="tpu_custom_call" | custom-call | flops 1 | bytes 1 | tf_op jit(solution)/shard_map/pallas_call | solution.py:564
  365.8 7.6 %shard_map.219 = bf16[512,2048]{1,0:T(8,128)(2,1)} custom-call(bf16[256,2048]{1,0:T(8,128)(2,1)S(1)} %copy-done.14, bf16[256,2048]{1,0:T(8,128)(2,1)S(1)} %copy-done.18, bf16[256,2048]{1,0:T(8,128)(2,1)S(1)} %copy-done.16, bf16[256,2048]{1,0:T(8,128)(2,1)} %collective-permute-done.20.refs_3_, bf16[256,2048]{1,0:T(8,128)(2,1)} %all-gather.9.cloned.1.call-done.refs_2_.refs_4_, ...), custom_call_target="tpu_custom_call" | custom-call | flops 1 | bytes 1 | tf_op jit(solution)/shard_map/pallas_call | solution.py:564
  401.3 9.8 %collective-permute-done.48 = f32[2,2,128]{2,1,0:T(2,128)S(1)} collective-permute-done((f32[2,2,128]{2,1,0:T(2,128)S(1)}, f32[2,2,128]{2,1,0:T(2,128)S(1)}, u32[]{:S(2)}, u32[]{:S(2)}) %collective-permute-start.48) | collective-permute-done | bytes 2080 | tf_op jit(solution)/shard_map/ppermute | solution.py:373
  431.3 8.0 %shard_map.220 = bf16[1024,512]{1,0:T(8,128)(2,1)S(1)} custom-call(bf16[1024,512]{1,0:T(8,128)(2,1)S(1)} %copy-done.29, bf16[1024,256]{1,0:T(8,128)(2,1)S(1)} %copy-done.57, f32[1024,2]{1,0:T(8,128)S(1)} %copy-done.34, f32[1024,128]{1,0:T(8,128)S(1)} %copy-done.10, f32[1024,128]{1,0:T(8,128)S(1)} %copy-done.8, s32[1024,2]{1,0:T(8,128)S(1)} %copy-done.12, ...), custom_call_target="tpu_custom_call" | custom-call | flops 1 | bytes 1 | tf_op jit(solution)/shard_map/pallas_call | solution.py:601
  463.4 7.2 %collective-permute-done.58 = bf16[128,1024]{1,0:T(8,128)(2,1)S(1)} collective-permute-done((bf16[128,1024]{1,0:T(8,128)(2,1)S(1)}, bf16[128,1024]{1,0:T(8,128)(2,1)S(1)}, u32[]{:S(2)}, u32[]{:S(2)}) %collective-permute-start.58) | collective-permute-done | bytes 262176 | tf_op jit(solution)/shard_map/ppermute | solution.py:377
  512.6 8.5 %collective-permute-done.70 = bf16[128,2048]{1,0:T(8,128)(2,1)} collective-permute-done((bf16[128,2048]{1,0:T(8,128)(2,1)}, bf16[128,2048]{1,0:T(8,128)(2,1)}, u32[]{:S(2)}, u32[]{:S(2)}) %collective-permute-start.70) | collective-permute-done | bytes 524320 | tf_op jit(solution)/shard_map/ppermute | solution.py:373
  521.1 7.7 %collective-permute-done.69 = bf16[512,1024]{1,0:T(8,128)(2,1)} collective-permute-done((bf16[512,1024]{1,0:T(8,128)(2,1)}, bf16[512,1024]{1,0:T(8,128)(2,1)}, u32[]{:S(2)}, u32[]{:S(2)}) %collective-permute-start.69) | collective-permute-done | bytes 1048608 | tf_op jit(solution)/shard_map/ppermute | solution.py:365
  559.9 19.0 %collective-permute-done.74 = bf16[256,512]{1,0:T(8,128)(2,1)S(1)} collective-permute-done((bf16[256,512]{1,0:T(8,128)(2,1)S(1)}, bf16[256,512]{1,0:T(8,128)(2,1)S(1)}, u32[]{:S(2)}, u32[]{:S(2)}) %collective-permute-start.74) | collective-permute-done | bytes 262176 | tf_op jit(solution)/shard_map/ppermute | solution.py:377
  598.7 9.9 %collective-permute-done.82 = bf16[128,1024]{1,0:T(8,128)(2,1)S(1)} collective-permute-done((bf16[128,1024]{1,0:T(8,128)(2,1)S(1)}, bf16[128,1024]{1,0:T(8,128)(2,1)S(1)}, u32[]{:S(2)}, u32[]{:S(2)}) %collective-permute-start.82) | collective-permute-done | bytes 262176 | tf_op jit(solution)/shard_map/ppermute | solution.py:377
  (675 shorter events, 328.3 us)
Async XLA Ops:
  7.2 71.6 %all-gather.15.cloned.1.call-start = ((), (), s32[]{:S(2)}) async-start(), calls=%async_computation.16 | async-start | bytes 4014080 | tf_op jit(solution)/shard_map/all_gather | solution.py:672
  11.4 114.5 %all-gather.7.cloned.1.call-start = ((), (), s32[]{:S(2)}) async-start(), calls=%async_computation.6 | async-start | bytes 1310720 | tf_op jit(solution)/shard_map/all_gather | solution.py:381
  15.7 31.7 %collective-permute-start.3 = (s32[256]{0:T(256)S(1)}, s32[256]{0:T(256)S(1)}, u32[]{:S(2)}, u32[]{:S(2)}) collective-permute-start(s32[256]{0:T(256)S(1)} %pad_add_fusion.3), channel_id=1, source_target_pairs={{0,8},{4,12},{8,0},{12,4},{1,9},{5,13},{9,1},{13,5},{2,10},{6,14},... | collective-permute-start | bytes 3080 | tf_op jit(solution)/shard_map/ppermute | solution.py:365
  79.7 101.4 %all-gather.9.cloned.1.call-start = ((), (), s32[]{:S(2)}) async-start(), calls=%async_computation.7 | async-start | bytes 1310720 | tf_op jit(solution)/shard_map/all_gather | solution.py:381
  83.7 42.1 %collective-permute-start.6 = (bf16[512,512]{1,0:T(8,128)(2,1)}, bf16[512,512]{1,0:T(8,128)(2,1)S(1)}, u32[]{:S(2)}, u32[]{:S(2)}) collective-permute-start(bf16[512,512]{1,0:T(8,128)(2,1)} %pad_maximum_fusion.18), channel_id=1, source_target_pairs={{0,3},{1,0},{2,1},{3,2},{4,7},{5,4},{6,5},{7,6},{8,11},{9,8},{10,9... | collective-permute-start | bytes 1572872 | tf_op jit(solution)/shard_map/ppermute | solution.py:377
  138.3 73.9 %all-gather.11.cloned.1.call-start = ((), (), s32[]{:S(2)}) async-start(), calls=%async_computation.8 | async-start | bytes 1310720 | tf_op jit(solution)/shard_map/all_gather | solution.py:381
  138.3 42.8 %collective-permute-start.15 = (bf16[512,512]{1,0:T(8,128)(2,1)}, bf16[512,512]{1,0:T(8,128)(2,1)}, u32[]{:S(2)}, u32[]{:S(2)}) collective-permute-start(bf16[512,512]{1,0:T(8,128)(2,1)} %pad_maximum_fusion.17), channel_id=1, source_target_pairs={{0,2},{1,3},{2,0},{3,1},{4,6},{5,7},{6,4},{7,5},{8,10},{9,11},{10,... | collective-permute-start | bytes 1572872 | tf_op jit(solution)/shard_map/ppermute | solution.py:377
  140.5 40.5 %collective-permute-start.16 = (bf16[256,2048]{1,0:T(8,128)(2,1)S(1)}, bf16[256,2048]{1,0:T(8,128)(2,1)S(1)}, u32[]{:S(2)}, u32[]{:S(2)}) collective-permute-start(bf16[256,2048]{1,0:T(8,128)(2,1)S(1)} %copy-done.13), channel_id=1, source_target_pairs={{0,16},{16,0},{1,17},{17,1},{2,18},{18,2},{3,19},{19,3},{4,20},{20... | collective-permute-start | bytes 3145736 | tf_op jit(solution)/shard_map/ppermute | solution.py:373
  153.6 27.4 %collective-permute-start.13 = (bf16[128,1024]{1,0:T(8,128)(2,1)}, bf16[128,1024]{1,0:T(8,128)(2,1)}, u32[]{:S(2)}, u32[]{:S(2)}) collective-permute-start(bf16[128,1024]{1,0:T(8,128)(2,1)} %get-tuple-element.752), channel_id=1, source_target_pairs={{0,8},{4,12},{8,0},{12,4},{1,9},{5,13},{9,1},{13,5},{2,10},{6,14},... | collective-permute-start | bytes 786440 | tf_op jit(solution)/shard_map/ppermute | solution.py:365
  184.8 55.2 %all-gather.13.cloned.1.call-start = ((), (), s32[]{:S(2)}) async-start(), calls=%async_computation.9 | async-start | bytes 1310720 | tf_op jit(solution)/shard_map/all_gather | solution.py:381
  212.2 124.1 %reduce-scatter.7.cloned.1.call-start = ((), (), s32[]{:S(2)}) async-start(), calls=%async_computation.10 | async-start | bytes 1310720 | tf_op jit(solution)/shard_map/reduce_scatter | solution.py:385
  245.6 28.9 %collective-permute-start.27 = (bf16[256,2048]{1,0:T(8,128)(2,1)S(1)}, bf16[256,2048]{1,0:T(8,128)(2,1)S(1)}, u32[]{:S(2)}, u32[]{:S(2)}) collective-permute-start(bf16[256,2048]{1,0:T(8,128)(2,1)S(1)} %copy-done.72), channel_id=1, source_target_pairs={{0,16},{16,0},{1,17},{17,1},{2,18},{18,2},{3,19},{19,3},{4,20},{20... | collective-permute-start | bytes 3145736 | tf_op jit(solution)/shard_map/ppermute | solution.py:373
  310.2 67.4 %reduce-scatter.9.cloned.1.call-start = ((), (), s32[]{:S(2)}) async-start(), calls=%async_computation.11 | async-start | bytes 1310720 | tf_op jit(solution)/shard_map/reduce_scatter | solution.py:385
  345.4 74.9 %reduce-scatter.11.cloned.1.call-start = ((), (), s32[]{:S(2)}) async-start(), calls=%async_computation.12 | async-start | bytes 1310720 | tf_op jit(solution)/shard_map/reduce_scatter | solution.py:385
  348.2 27.9 %collective-permute-start.38 = (bf16[1024,512]{1,0:T(8,128)(2,1)}, bf16[1024,512]{1,0:T(8,128)(2,1)}, u32[]{:S(2)}, u32[]{:S(2)}) collective-permute-start(bf16[1024,512]{1,0:T(8,128)(2,1)} %constant_dynamic-slice_fusion.38), channel_id=1, source_target_pairs={{0,8},{4,12},{8,0},{12,4},{1,9},{5,13},{9,1},{13,5},{2,10},{6,14},... | collective-permute-start | bytes 3145736 | tf_op jit(solution)/shard_map/ppermute | solution.py:365
  393.1 81.3 %reduce-scatter.13.cloned.1.call-start = ((), (), s32[]{:S(2)}) async-start(), calls=%async_computation.13 | async-start | bytes 1310720 | tf_op jit(solution)/shard_map/reduce_scatter | solution.py:385
  430.0 105.2 %reduce-scatter.15.cloned.1.call-start = ((), (), s32[]{:S(2)}) async-start(), calls=%async_computation.14 | async-start | bytes 2621440 | tf_op jit(solution)/shard_map/reduce_scatter | solution.py:385
  442.0 32.4 %collective-permute-start.54 = (bf16[2,2,128,2048]{3,2,1,0:T(8,128)(2,1)}, bf16[2,2,128,2048]{3,2,1,0:T(8,128)(2,1)}, u32[]{:S(2)}, u32[]{:S(2)}) collective-permute-start(bf16[2,2,128,2048]{3,2,1,0:T(8,128)(2,1)} %bitcast.60), channel_id=1, source_target_pairs={{0,4},{4,0},{8,12},{12,8},{1,5},{5,1},{9,13},{13,9},{2,6},{6,2},{1... | collective-permute-start | bytes 6291464 | tf_op jit(solution)/shard_map/ppermute | solution.py:361
  442.1 30.6 %collective-permute-start.55 = (bf16[1024,512]{1,0:T(8,128)(2,1)S(1)}, bf16[1024,512]{1,0:T(8,128)(2,1)S(1)}, u32[]{:S(2)}, u32[]{:S(2)}) collective-permute-start(bf16[1024,512]{1,0:T(8,128)(2,1)S(1)} %constant_dynamic-slice_fusion.27), channel_id=1, source_target_pairs={{0,8},{4,12},{8,0},{12,4},{1,9},{5,13},{9,1},{13,5},{2,10},{6,14},... | collective-permute-start | bytes 3145736 | tf_op jit(solution)/shard_map/ppermute | solution.py:365
  442.7 31.6 %collective-permute-start.56 = (bf16[256,2048]{1,0:T(8,128)(2,1)}, bf16[256,2048]{1,0:T(8,128)(2,1)}, u32[]{:S(2)}, u32[]{:S(2)}) collective-permute-start(bf16[256,2048]{1,0:T(8,128)(2,1)} %add_convert_fusion.4), channel_id=1, source_target_pairs={{0,16},{16,0},{1,17},{17,1},{2,18},{18,2},{3,19},{19,3},{4,20},{20... | collective-permute-start | bytes 3145736 | tf_op jit(solution)/shard_map/ppermute | solution.py:373
  492.4 87.8 %reduce-scatter.17.cloned.1.call-start = ((), (), s32[]{:S(2)}) async-start(), calls=%async_computation.15 | async-start | bytes 1310720 | tf_op jit(solution)/shard_map/reduce_scatter | solution.py:385
  545.2 33.7 %collective-permute-start.74 = (bf16[256,512]{1,0:T(8,128)(2,1)S(1)}, bf16[256,512]{1,0:T(8,128)(2,1)S(1)}, u32[]{:S(2)}, u32[]{:S(2)}) collective-permute-start(bf16[256,512]{1,0:T(8,128)(2,1)S(1)} %get-tuple-element.703), channel_id=1, source_target_pairs={{0,2},{1,3},{2,0},{3,1},{4,6},{5,7},{6,4},{7,5},{8,10},{9,11},{10,... | collective-permute-start | bytes 786440 | tf_op jit(solution)/shard_map/ppermute | solution.py:377
  547.9 31.7 %collective-permute-start.75 = (bf16[256,512]{1,0:T(8,128)(2,1)S(1)}, bf16[256,512]{1,0:T(8,128)(2,1)}, u32[]{:S(2)}, u32[]{:S(2)}) collective-permute-start(bf16[256,512]{1,0:T(8,128)(2,1)S(1)} %get-tuple-element.700), channel_id=1, source_target_pairs={{0,3},{1,0},{2,1},{3,2},{4,7},{5,4},{6,5},{7,6},{8,11},{9,8},{10,9... | collective-permute-start | bytes 786440 | tf_op jit(solution)/shard_map/ppermute | solution.py:377
  581.4 37.1 %collective-permute-start.80 = (bf16[128,2048]{1,0:T(8,128)(2,1)S(1)}, bf16[128,2048]{1,0:T(8,128)(2,1)S(1)}, u32[]{:S(2)}, u32[]{:S(2)}) collective-permute-start(bf16[128,2048]{1,0:T(8,128)(2,1)S(1)} %add_convert_fusion.15), channel_id=1, source_target_pairs={{0,16},{16,0},{1,17},{17,1},{2,18},{18,2},{3,19},{19,3},{4,20},{20... | collective-permute-start | bytes 1572872 | tf_op jit(solution)/shard_map/ppermute | solution.py:373
  (224 other events, 2046.6 us)
Sparse Core Ops, SparseCore 0:
  11.5 67.2 all-gather.14
  81.0 44.1 all-gather.6
  138.4 40.9 all-gather.8
  185.0 25.5 all-gather.10
  212.6 27.4 all-gather.12
  310.4 25.7 reduce-scatter.6
  345.5 25.7 reduce-scatter.8
  393.2 26.9 reduce-scatter.10
  430.1 28.0 reduce-scatter.12
  492.5 42.6 reduce-scatter.14
  538.2 41.9 reduce-scatter.16

commit v4 on v3

--- a/solution.py
+++ b/solution.py
@@ -970,7 +970,10 @@
     grad_attended = low(contract_cols(hidden_low, out_w))
     grad_heads = attend_backward_local(turned, grad_attended, logsum, tables, heads, score_scale)
     gain_two_sum = gain_next(*gain_two_sum, y_at, over_y)
-    grad_heads, hidden_low, *gain_two_sum = fence(grad_heads, hidden_low, *gain_two_sum)
+    grad_heads, hidden_low, up_given, out_x[1], *rest = fence(
+        grad_heads, hidden_low, up_given, out_x[1], *gate_sent, *gain_two_sum
+    )
+    gate_sent, gain_two_sum = rest[:4], rest[4:]
     grad_ffn_gain = gain_two_sum[0] + gain_two_sum[1]
 
     theirs = low(contract_cols(grad_heads[length // 2 :], attn_w)).reshape(part_shape)

time: 632 us -> 637 us (level)
  waiting for transfers between devices: 262 us -> 277 us
  starting transfers between devices: 89.3 us -> 79.2 us
    ppermute x19, waiting for transfers between devices: 56.8 us -> 70.5 us  [over_y(): return lax.ppermute(block, 'context', [(i, i ^ 2) for i in range(4)])]
    unnamed x300 -> x276, local copies, waits for them, and re-layouts: 25.8 us -> 23 us
  transfers between devices with their start and end apart: 98 -> 98, of which waited for: 45 -> 46; matrix products, arithmetic and copies ran while one was open for 18% -> 19% of each run, Pallas kernels for 14% -> 14%
where the time goes in v4:
time: 637 us; the launch traced here: 632 us
  waiting for transfers between devices  277 us (43%)
  other arithmetic  92.1 us (14%)
  Pallas kernels  86.7 us (14%)
  starting transfers between devices  79.2 us (12%)
  local copies, waits for them, and re-layouts  60.7 us (10%)
  matrix products  19.4 us (3%)
  between operations  16.1 us (3%)
    ppermute x18, waiting for transfers between devices, shift_z(): return lax.ppermute(block, 'fsdp', [(i, (i + step) % 4) for i in range(4)])  94.6 us
    ppermute x18, waiting for transfers between devices, over_x(): return lax.ppermute(block, 'tensor', [(0, 1), (1, 0)])  75.7 us
    ppermute x19, waiting for transfers between devices, over_y(): return lax.ppermute(block, 'context', [(i, i ^ 2) for i in range(4)])  70.5 us
    pallas_call x4, Pallas kernels, feed_forward_local(): pl.pallas_call(feed_forward_kernel, out_shape=[small] * 3 + [large] * 4,...  45.9 us
    convert_element_type x24, other arithmetic, low(): return values.astype(jnp.bfloat16)  37.6 us
    ppermute x18, starting transfers between devices, shift_z(): return lax.ppermute(block, 'fsdp', [(i, (i + step) % 4) for i in range(4)])  30 us
    pallas_call x3, Pallas kernels, weight_local(): pl.pallas_call(functools.partial(weight_kernel, len(wides)), grid=(2,), i...  24.2 us
    unnamed x276, local copies, waits for them, and re-layouts  23 us
  transfers between devices with their start and end apart: 98, of which 46 were waited for; matrix products, arithmetic and copies ran while one was open for 19% of the time, Pallas kernels for 14%

profile of v4, /device:TPU:0, one launch (start us, length us, event | category | flops | bytes accessed | tf_op | source)
XLA Modules:
  0.0 631.5 jit_solution(9237801999583118220)
XLA Ops:
  16.4 22.5 %collective-permute-done = bf16[256,2048]{1,0:T(8,128)(2,1)S(1)} collective-permute-done((bf16[256,2048]{1,0:T(8,128)(2,1)S(1)}, bf16[256,2048]{1,0:T(8,128)(2,1)S(1)}, u32[]{:S(2)}, u32[]{:S(2)}) %collective-permute-start) | collective-permute-done | bytes 1048608 | tf_op jit(solution)/shard_map/ppermute | solution.py:365
  56.5 10.1 %collective-permute-done.2 = bf16[512,512]{1,0:T(8,128)(2,1)S(1)} collective-permute-done((bf16[512,512]{1,0:T(8,128)(2,1)S(1)}, bf16[512,512]{1,0:T(8,128)(2,1)S(1)}, u32[]{:S(2)}, u32[]{:S(2)}) %collective-permute-start.2) | collective-permute-done | bytes 524320 | tf_op jit(solution)/shard_map/ppermute | solution.py:365
  66.7 12.2 %all-gather.15.cloned.1.call-done = bf16[3136,512]{1,0:T(8,128)(2,1)} async-done(((bf16[784,512]{1,0:T(8,128)(2,1)}), bf16[3136,512]{1,0:T(8,128)(2,1)}) %all-gather.15.cloned.1.call-update) | async-done | bytes 3211280 | tf_op jit(solution)/shard_map/all_gather | solution.py:672
  97.2 8.6 %shard_map.212 = (bf16[1024,512]{1,0:T(8,128)(2,1)S(1)}, bf16[1024,256]{1,0:T(8,128)(2,1)S(1)}, f32[1024,2]{1,0:T(8,128)S(1)}) custom-call(f32[1024,512]{1,0:T(8,128)S(1)} %copy-done.19, f32[1024,128]{1,0:T(8,128)S(1)} %get-tuple-element.342.cos_ref, f32[1024,128]{1,0:T(8,128)S(1)} %get-tuple-element.343.sine_ref, s32[1024,2]{1,0:T(8,128)S(1)} %copy.40.tag_ref, ...), custom_call_target="tpu_custom_call" | custom-call | flops 1 | bytes 1 | tf_op jit(solution)/shard_map/pallas_call | solution.py:587
  109.2 16.9 %collective-permute-done.6 = bf16[512,512]{1,0:T(8,128)(2,1)S(1)} collective-permute-done((bf16[512,512]{1,0:T(8,128)(2,1)}, bf16[512,512]{1,0:T(8,128)(2,1)S(1)}, u32[]{:S(2)}, u32[]{:S(2)}) %collective-permute-start.6) | collective-permute-done | bytes 524320 | tf_op jit(solution)/shard_map/ppermute | solution.py:377
  141.1 9.6 %collective-permute-done.11 = bf16[2,128,1024]{2,1,0:T(8,128)(2,1)} collective-permute-done((bf16[2,128,1024]{2,1,0:T(8,128)(2,1)}, bf16[2,128,1024]{2,1,0:T(8,128)(2,1)}, u32[]{:S(2)}, u32[]{:S(2)}) %collective-permute-start.11) | collective-permute-done | bytes 524320 | tf_op jit(solution)/shard_map/ppermute | solution.py:373
  157.5 23.8 %collective-permute-done.15 = bf16[512,512]{1,0:T(8,128)(2,1)} collective-permute-done((bf16[512,512]{1,0:T(8,128)(2,1)}, bf16[512,512]{1,0:T(8,128)(2,1)}, u32[]{:S(2)}, u32[]{:S(2)}) %collective-permute-start.15) | collective-permute-done | bytes 524320 | tf_op jit(solution)/shard_map/ppermute | solution.py:377
  193.1 16.8 %collective-permute-done.17.refs_2_.refs_6_ = bf16[256,2048]{1,0:T(8,128)(2,1)} collective-permute-done((bf16[256,2048]{1,0:T(8,128)(2,1)}, bf16[256,2048]{1,0:T(8,128)(2,1)}, u32[]{:S(2)}, u32[]{:S(2)}) %collective-permute-start.17) | collective-permute-done | bytes 1048608 | tf_op jit(solution)/shard_map/ppermute | solution.py:373
  219.7 10.2 %collective-permute-done.23 = bf16[512,512]{1,0:T(8,128)(2,1)S(1)} collective-permute-done((bf16[512,512]{1,0:T(8,128)(2,1)}, bf16[512,512]{1,0:T(8,128)(2,1)S(1)}, u32[]{:S(2)}, u32[]{:S(2)}) %collective-permute-start.23) | collective-permute-done | bytes 524320 | tf_op jit(solution)/shard_map/ppermute | solution.py:365
  247.1 11.3 %shard_map.214 = (bf16[512,512]{1,0:T(8,128)(2,1)S(1)}, bf16[512,512]{1,0:T(8,128)(2,1)S(1)}, bf16[512,512]{1,0:T(8,128)(2,1)S(1)}, bf16[256,2048]{1,0:T(8,128)(...) custom-call(bf16[256,2048]{1,0:T(8,128)(2,1)} %all-gather.11.cloned.1.call-don, ...), custom_call_target="tpu_custom_call" | custom-call | flops 1 | bytes 1 | tf_op jit(solution)/shard_map/pallas_call | solution.py:534
  262.7 11.5 %shard_map.213 = (bf16[512,512]{1,0:T(8,128)(2,1)S(1)}, bf16[512,512]{1,0:T(8,128)(2,1)S(1)}, bf16[512,512]{1,0:T(8,128)(2,1)S(1)}, bf16[256,2048]{1,0:T(8,128)(...) custom-call(bf16[256,2048]{1,0:T(8,128)(2,1)} %copy-done.3, ...), custom_call_target="tpu_custom_call" | custom-call | flops 1 | bytes 1 | tf_op jit(solution)/shard_map/pallas_call | solution.py:534
  282.6 11.3 %shard_map.215 = (bf16[512,512]{1,0:T(8,128)(2,1)S(1)}, bf16[512,512]{1,0:T(8,128)(2,1)S(1)}, bf16[512,512]{1,0:T(8,128)(2,1)S(1)}, bf16[256,2048]{1,0:T(8,128)(...) custom-call(bf16[256,2048]{1,0:T(8,128)(2,1)} %copy-done.70, ...), custom_call_target="tpu_custom_call" | custom-call | flops 1 | bytes 1 | tf_op jit(solution)/shard_map/pallas_call | solution.py:534
  295.7 11.6 %collective-permute-done.32 = bf16[256,2048]{1,0:T(8,128)(2,1)S(1)} collective-permute-done((bf16[256,2048]{1,0:T(8,128)(2,1)S(1)}, bf16[256,2048]{1,0:T(8,128)(2,1)S(1)}, u32[]{:S(2)}, u32[]{:S(2)}) %collective-permute-start.32) | collective-permute-done | bytes 1048608 | tf_op jit(solution)/shard_map/ppermute | solution.py:373
  311.7 11.8 %shard_map.216 = (bf16[512,512]{1,0:T(8,128)(2,1)S(1)}, bf16[512,512]{1,0:T(8,128)(2,1)S(1)}, bf16[512,512]{1,0:T(8,128)(2,1)S(1)}, bf16[256,2048]{1,0:T(8,128)(...) custom-call(bf16[256,2048]{1,0:T(8,128)(2,1)} %all-gather.13.cloned.1.call-don, ...), custom_call_target="tpu_custom_call" | custom-call | flops 1 | bytes 1 | tf_op jit(solution)/shard_map/pallas_call | solution.py:534
  324.6 8.8 %shard_map.217 = bf16[2048,512]{1,0:T(8,128)(2,1)} custom-call(bf16[256,2048]{1,0:T(8,128)(2,1)S(1)} %copy-done.2, bf16[256,2048]{1,0:T(8,128)(2,1)S(1)} %copy-done.6, bf16[256,2048]{1,0:T(8,128)(2,1)S(1)} %copy-done.4, bf16[256,2048]{1,0:T(8,128)(2,1)} %copy-done.69, bf16[256,2048]{1,0:T(8,128)(2,1)} %all-gather.13.cloned.1.call-done.refs_0_.refs_4_, ...), custom_call_target="tpu_custom_call" | custom-call | flops 1 | bytes 1 | tf_op jit(solution)/shard_map/pallas_call | solution.py:564
  357.5 7.7 %shard_map.218 = bf16[2048,512]{1,0:T(8,128)(2,1)} custom-call(bf16[256,2048]{1,0:T(8,128)(2,1)S(1)} %copy-done.2, bf16[256,2048]{1,0:T(8,128)(2,1)S(1)} %copy-done.6, bf16[256,2048]{1,0:T(8,128)(2,1)S(1)} %copy-done.4, bf16[256,2048]{1,0:T(8,128)(2,1)} %copy-done.69, bf16[256,2048]{1,0:T(8,128)(2,1)} %all-gather.13.cloned.1.call-done.refs_0_.refs_4_, ...), custom_call_target="tpu_custom_call" | custom-call | flops 1 | bytes 1 | tf_op jit(solution)/shard_map/pallas_call | solution.py:564
  401.1 9.8 %collective-permute-done.48 = f32[2,2,128]{2,1,0:T(2,128)S(1)} collective-permute-done((f32[2,2,128]{2,1,0:T(2,128)S(1)}, f32[2,2,128]{2,1,0:T(2,128)S(1)}, u32[]{:S(2)}, u32[]{:S(2)}) %collective-permute-start.48) | collective-permute-done | bytes 2080 | tf_op jit(solution)/shard_map/ppermute | solution.py:373
  434.3 13.1 %collective-permute-done.58 = f32[128]{0:T(128)S(1)} collective-permute-done((f32[128]{0:T(128)S(1)}, f32[128]{0:T(128)S(1)}, u32[]{:S(2)}, u32[]{:S(2)}) %collective-permute-start.58) | collective-permute-done | bytes 544 | tf_op jit(solution)/shard_map/ppermute | solution.py:365
  453.0 8.0 %shard_map.220 = bf16[1024,512]{1,0:T(8,128)(2,1)S(1)} custom-call(bf16[1024,512]{1,0:T(8,128)(2,1)S(1)} %copy-done.29, bf16[1024,256]{1,0:T(8,128)(2,1)S(1)} %convolution_convert_fusion.5.grad_ref, f32[1024,2]{1,0:T(8,128)S(1)} %copy-done.32, f32[1024,128]{1,0:T(8,128)S(1)} %copy-done.10, f32[1024,128]{1,0:T(8,128)S(1)} %copy-done.8, ...), custom_call_target="tpu_custom_call" | custom-call | flops 1 | bytes 1 | tf_op jit(solution)/shard_map/pallas_call | solution.py:601
  462.3 7.8 %collective-permute-done.57 = bf16[128,1024]{1,0:T(8,128)(2,1)S(1)} collective-permute-done((bf16[128,1024]{1,0:T(8,128)(2,1)}, bf16[128,1024]{1,0:T(8,128)(2,1)S(1)}, u32[]{:S(2)}, u32[]{:S(2)}) %collective-permute-start.57) | collective-permute-done | bytes 262176 | tf_op jit(solution)/shard_map/ppermute | solution.py:377
  519.8 9.2 %collective-permute-done.70 = bf16[128,2048]{1,0:T(8,128)(2,1)S(1)} collective-permute-done((bf16[128,2048]{1,0:T(8,128)(2,1)}, bf16[128,2048]{1,0:T(8,128)(2,1)S(1)}, u32[]{:S(2)}, u32[]{:S(2)}) %collective-permute-start.70) | collective-permute-done | bytes 524320 | tf_op jit(solution)/shard_map/ppermute | solution.py:373
  529.0 8.3 %collective-permute-done.69 = bf16[512,1024]{1,0:T(8,128)(2,1)} collective-permute-done((bf16[512,1024]{1,0:T(8,128)(2,1)}, bf16[512,1024]{1,0:T(8,128)(2,1)}, u32[]{:S(2)}, u32[]{:S(2)}) %collective-permute-start.69) | collective-permute-done | bytes 1048608 | tf_op jit(solution)/shard_map/ppermute | solution.py:365
  568.4 16.6 %collective-permute-done.74 = bf16[256,512]{1,0:T(8,128)(2,1)S(1)} collective-permute-done((bf16[256,512]{1,0:T(8,128)(2,1)S(1)}, bf16[256,512]{1,0:T(8,128)(2,1)S(1)}, u32[]{:S(2)}, u32[]{:S(2)}) %collective-permute-start.74) | collective-permute-done | bytes 262176 | tf_op jit(solution)/shard_map/ppermute | solution.py:377
  603.4 10.0 %collective-permute-done.82 = bf16[128,1024]{1,0:T(8,128)(2,1)S(1)} collective-permute-done((bf16[128,1024]{1,0:T(8,128)(2,1)S(1)}, bf16[128,1024]{1,0:T(8,128)(2,1)S(1)}, u32[]{:S(2)}, u32[]{:S(2)}) %collective-permute-start.82) | collective-permute-done | bytes 262176 | tf_op jit(solution)/shard_map/ppermute | solution.py:377
  (651 shorter events, 327.8 us)
Async XLA Ops:
  7.2 71.6 %all-gather.15.cloned.1.call-start = ((), (), s32[]{:S(2)}) async-start(), calls=%async_computation.16 | async-start | bytes 4014080 | tf_op jit(solution)/shard_map/all_gather | solution.py:672
  11.4 114.7 %all-gather.7.cloned.1.call-start = ((), (), s32[]{:S(2)}) async-start(), calls=%async_computation.6 | async-start | bytes 1310720 | tf_op jit(solution)/shard_map/all_gather | solution.py:381
  15.7 31.6 %collective-permute-start.3 = (s32[256]{0:T(256)S(1)}, s32[256]{0:T(256)S(1)}, u32[]{:S(2)}, u32[]{:S(2)}) collective-permute-start(s32[256]{0:T(256)S(1)} %pad_add_fusion.3), channel_id=1, source_target_pairs={{0,8},{4,12},{8,0},{12,4},{1,9},{5,13},{9,1},{13,5},{2,10},{6,14},... | collective-permute-start | bytes 3080 | tf_op jit(solution)/shard_map/ppermute | solution.py:365
  79.7 101.7 %all-gather.9.cloned.1.call-start = ((), (), s32[]{:S(2)}) async-start(), calls=%async_computation.7 | async-start | bytes 1310720 | tf_op jit(solution)/shard_map/all_gather | solution.py:381
  83.7 42.4 %collective-permute-start.6 = (bf16[512,512]{1,0:T(8,128)(2,1)}, bf16[512,512]{1,0:T(8,128)(2,1)S(1)}, u32[]{:S(2)}, u32[]{:S(2)}) collective-permute-start(bf16[512,512]{1,0:T(8,128)(2,1)} %pad_maximum_fusion.18), channel_id=1, source_target_pairs={{0,3},{1,0},{2,1},{3,2},{4,7},{5,4},{6,5},{7,6},{8,11},{9,8},{10,9... | collective-permute-start | bytes 1572872 | tf_op jit(solution)/shard_map/ppermute | solution.py:377
  138.6 73.9 %all-gather.11.cloned.1.call-start = ((), (), s32[]{:S(2)}) async-start(), calls=%async_computation.8 | async-start | bytes 1310720 | tf_op jit(solution)/shard_map/all_gather | solution.py:381
  138.6 42.8 %collective-permute-start.15 = (bf16[512,512]{1,0:T(8,128)(2,1)}, bf16[512,512]{1,0:T(8,128)(2,1)}, u32[]{:S(2)}, u32[]{:S(2)}) collective-permute-start(bf16[512,512]{1,0:T(8,128)(2,1)} %pad_maximum_fusion.17), channel_id=1, source_target_pairs={{0,2},{1,3},{2,0},{3,1},{4,6},{5,7},{6,4},{7,5},{8,10},{9,11},{10,... | collective-permute-start | bytes 1572872 | tf_op jit(solution)/shard_map/ppermute | solution.py:377
  140.5 40.8 %collective-permute-start.16 = (bf16[256,2048]{1,0:T(8,128)(2,1)S(1)}, bf16[256,2048]{1,0:T(8,128)(2,1)S(1)}, u32[]{:S(2)}, u32[]{:S(2)}) collective-permute-start(bf16[256,2048]{1,0:T(8,128)(2,1)S(1)} %copy-done.13), channel_id=1, source_target_pairs={{0,16},{16,0},{1,17},{17,1},{2,18},{18,2},{3,19},{19,3},{4,20},{20... | collective-permute-start | bytes 3145736 | tf_op jit(solution)/shard_map/ppermute | solution.py:373
  185.1 54.9 %all-gather.13.cloned.1.call-start = ((), (), s32[]{:S(2)}) async-start(), calls=%async_computation.9 | async-start | bytes 1310720 | tf_op jit(solution)/shard_map/all_gather | solution.py:381
  212.5 123.9 %reduce-scatter.7.cloned.1.call-start = ((), (), s32[]{:S(2)}) async-start(), calls=%async_computation.10 | async-start | bytes 1310720 | tf_op jit(solution)/shard_map/reduce_scatter | solution.py:385
  245.6 28.7 %collective-permute-start.27 = (bf16[256,2048]{1,0:T(8,128)(2,1)S(1)}, bf16[256,2048]{1,0:T(8,128)(2,1)S(1)}, u32[]{:S(2)}, u32[]{:S(2)}) collective-permute-start(bf16[256,2048]{1,0:T(8,128)(2,1)S(1)} %copy-done.68), channel_id=1, source_target_pairs={{0,16},{16,0},{1,17},{17,1},{2,18},{18,2},{3,19},{19,3},{4,20},{20... | collective-permute-start | bytes 3145736 | tf_op jit(solution)/shard_map/ppermute | solution.py:373
  310.1 67.4 %reduce-scatter.9.cloned.1.call-start = ((), (), s32[]{:S(2)}) async-start(), calls=%async_computation.11 | async-start | bytes 1310720 | tf_op jit(solution)/shard_map/reduce_scatter | solution.py:385
  345.5 74.7 %reduce-scatter.11.cloned.1.call-start = ((), (), s32[]{:S(2)}) async-start(), calls=%async_computation.12 | async-start | bytes 1310720 | tf_op jit(solution)/shard_map/reduce_scatter | solution.py:385
  348.1 27.6 %collective-permute-start.38 = (bf16[1024,512]{1,0:T(8,128)(2,1)}, bf16[1024,512]{1,0:T(8,128)(2,1)}, u32[]{:S(2)}, u32[]{:S(2)}) collective-permute-start(bf16[1024,512]{1,0:T(8,128)(2,1)} %constant_dynamic-slice_fusion.38), channel_id=1, source_target_pairs={{0,8},{4,12},{8,0},{12,4},{1,9},{5,13},{9,1},{13,5},{2,10},{6,14},... | collective-permute-start | bytes 3145736 | tf_op jit(solution)/shard_map/ppermute | solution.py:365
  393.0 87.7 %reduce-scatter.13.cloned.1.call-start = ((), (), s32[]{:S(2)}) async-start(), calls=%async_computation.13 | async-start | bytes 1310720 | tf_op jit(solution)/shard_map/reduce_scatter | solution.py:385
  422.4 47.8 %collective-permute-start.53 = (bf16[1024,512]{1,0:T(8,128)(2,1)}, bf16[1024,512]{1,0:T(8,128)(2,1)}, u32[]{:S(2)}, u32[]{:S(2)}) collective-permute-start(bf16[1024,512]{1,0:T(8,128)(2,1)} %constant_dynamic-slice_fusion.29), channel_id=1, source_target_pairs={{0,8},{4,12},{8,0},{12,4},{1,9},{5,13},{9,1},{13,5},{2,10},{6,14},... | collective-permute-start | bytes 3145736 | tf_op jit(solution)/shard_map/ppermute | solution.py:365
  423.9 46.3 %collective-permute-start.54 = (bf16[256,2048]{1,0:T(8,128)(2,1)}, bf16[256,2048]{1,0:T(8,128)(2,1)S(1)}, u32[]{:S(2)}, u32[]{:S(2)}) collective-permute-start(bf16[256,2048]{1,0:T(8,128)(2,1)} %add_convert_fusion.4), channel_id=1, source_target_pairs={{0,16},{16,0},{1,17},{17,1},{2,18},{18,2},{3,19},{19,3},{4,20},{20... | collective-permute-start | bytes 3145736 | tf_op jit(solution)/shard_map/ppermute | solution.py:373
  429.7 31.4 %collective-permute-start.55 = (bf16[128,1024]{1,0:T(8,128)(2,1)}, bf16[128,1024]{1,0:T(8,128)(2,1)}, u32[]{:S(2)}, u32[]{:S(2)}) collective-permute-start(bf16[128,1024]{1,0:T(8,128)(2,1)} %get-tuple-element.726), channel_id=1, source_target_pairs={{0,1},{1,2},{2,3},{3,0},{4,5},{5,6},{6,7},{7,4},{8,9},{9,10},{10,1... | collective-permute-start | bytes 786440 | tf_op jit(solution)/shard_map/ppermute | solution.py:377
  429.7 32.6 %collective-permute-start.56 = (bf16[128,1024]{1,0:T(8,128)(2,1)}, bf16[128,1024]{1,0:T(8,128)(2,1)}, u32[]{:S(2)}, u32[]{:S(2)}) collective-permute-start(bf16[128,1024]{1,0:T(8,128)(2,1)} %get-tuple-element.725), channel_id=1, source_target_pairs={{0,2},{1,3},{2,0},{3,1},{4,6},{5,7},{6,4},{7,5},{8,10},{9,11},{10,... | collective-permute-start | bytes 786440 | tf_op jit(solution)/shard_map/ppermute | solution.py:377
  434.3 108.5 %reduce-scatter.15.cloned.1.call-start = ((), (), s32[]{:S(2)}) async-start(), calls=%async_computation.14 | async-start | bytes 2621440 | tf_op jit(solution)/shard_map/reduce_scatter | solution.py:385
  494.3 91.5 %reduce-scatter.17.cloned.1.call-start = ((), (), s32[]{:S(2)}) async-start(), calls=%async_computation.15 | async-start | bytes 1310720 | tf_op jit(solution)/shard_map/reduce_scatter | solution.py:385
  553.9 31.1 %collective-permute-start.74 = (bf16[256,512]{1,0:T(8,128)(2,1)S(1)}, bf16[256,512]{1,0:T(8,128)(2,1)S(1)}, u32[]{:S(2)}, u32[]{:S(2)}) collective-permute-start(bf16[256,512]{1,0:T(8,128)(2,1)S(1)} %get-tuple-element.715), channel_id=1, source_target_pairs={{0,2},{1,3},{2,0},{3,1},{4,6},{5,7},{6,4},{7,5},{8,10},{9,11},{10,... | collective-permute-start | bytes 786440 | tf_op jit(solution)/shard_map/ppermute | solution.py:377
  553.9 31.8 %collective-permute-start.75 = (bf16[256,512]{1,0:T(8,128)(2,1)S(1)}, bf16[256,512]{1,0:T(8,128)(2,1)}, u32[]{:S(2)}, u32[]{:S(2)}) collective-permute-start(bf16[256,512]{1,0:T(8,128)(2,1)S(1)} %get-tuple-element.712), channel_id=1, source_target_pairs={{0,3},{1,0},{2,1},{3,2},{4,7},{5,4},{6,5},{7,6},{8,11},{9,8},{10,9... | collective-permute-start | bytes 786440 | tf_op jit(solution)/shard_map/ppermute | solution.py:377
  586.9 36.4 %collective-permute-start.80 = (bf16[128,2048]{1,0:T(8,128)(2,1)S(1)}, bf16[128,2048]{1,0:T(8,128)(2,1)S(1)}, u32[]{:S(2)}, u32[]{:S(2)}) collective-permute-start(bf16[128,2048]{1,0:T(8,128)(2,1)S(1)} %add_convert_fusion.15), channel_id=1, source_target_pairs={{0,16},{16,0},{1,17},{17,1},{2,18},{18,2},{3,19},{19,3},{4,20},{20... | collective-permute-start | bytes 1572872 | tf_op jit(solution)/shard_map/ppermute | solution.py:373
  (212 other events, 1999.5 us)
Sparse Core Ops, SparseCore 0:
  11.5 67.2 all-gather.14
  81.0 44.1 all-gather.6
  138.7 40.9 all-gather.8
  185.3 25.3 all-gather.10
  212.6 27.4 all-gather.12
  310.2 25.7 reduce-scatter.6
  345.6 25.7 reduce-scatter.8
  393.1 26.9 reduce-scatter.10
  434.4 36.6 reduce-scatter.12
  494.4 43.8 reduce-scatter.14
  542.9 40.6 reduce-scatter.16
